TPU v7x, 32 devices: a whole 2x2x4 slice. The times are simulated.
32 devices in a mesh: row: 8 (over y, x, core), col: 4 (over z).
Axes of the slice: x: 2, y: 2, z: 4, core: 2. Of those that a mesh axis runs over, the one named last changes fastest.
Arguments:
- diag_tiles: float32 [32, 256, 256], P('row'), as said below
- left_fac: bfloat16 [32, 32, 256, 128], P('row', 'col'), as said below
- right_fac: bfloat16 [32, 32, 256, 128], P('row', 'col'), as said below
- ranks: int32 [32, 32], replicated, may hold values from 16 to 128, as said below
Outputs:
- factored: float32 [32, 32, 256, 256], P('row', 'col')
Inputs may be any that keep to these rules, and one draw needn't show every extreme that they name: `ranks`: every entry is a multiple of 16; in every draw some tile below the diagonal has rank 128, and the mean rank is about a third of 128. `diag_tiles`: every tile is symmetric; the first diagonal tile and the updated second diagonal tile M are positive definite. `left_fac`: entries have mean zero and deviation one. `right_fac`: entries have mean zero and deviation one over the square root of 128.
All inputs are finite; a program needn't handle non-finite values.
Results may differ from a plain program's by a relative error of at most 0.0003.
Values sent between devices are 32-bit elements; how exact they have to be, the bound alone decides.
No kernel may reach another device: no remote copies, remote signals or barrier semaphores. Data moves between devices by JAX's collectives and lax.ppermute only.
A program may use at most 64 MiB of HBM per device.

v0:
```python
import functools

import jax
import jax.numpy as jnp
from jax import lax
from jax.experimental import pallas as pl
from jax.experimental.pallas import tpu as pltpu
from jax.sharding import PartitionSpec as P

PRECISE = lax.Precision.HIGHEST
AXES = ("row", "col")
BLOCK = 32
GROUP = 8
LANES = 128
NT = (((1,), (1,)), ((), ()))
TN = (((0,), (0,)), ((), ()))
NN = (((1,), (0,)), ((), ()))
ANYWHERE = pl.BlockSpec(memory_space=pl.ANY)
IN_VMEM = pl.BlockSpec(memory_space=pltpu.VMEM)
IN_SMEM = pl.BlockSpec(memory_space=pltpu.SMEM)
IN_HBM = pl.BlockSpec(memory_space=pltpu.HBM)
MEBI = 1024 * 1024


def dot32(lhs, rhs, dims):
    return lax.dot_general(lhs, rhs, dims, precision=PRECISE, preferred_element_type=jnp.float32)


def dot16(lhs, rhs, dims):
    return lax.dot_general(lhs, rhs, dims, preferred_element_type=jnp.float32)


def split2(value):
    high = value.astype(jnp.bfloat16)
    low = (value - high.astype(jnp.float32)).astype(jnp.bfloat16)
    return high, low


def params(mebibytes, **extra):
    return pltpu.CompilerParams(vmem_limit_bytes=mebibytes * MEBI, **extra)


def cost(flops, moved):
    return pl.CostEstimate(flops=int(flops), bytes_accessed=int(moved), transcendentals=0)


def eliminate(tiles):
    tiles, start = tiles
    rows = tiles[0].shape[0]
    done = []
    for first in range(0, rows, GROUP):
        height = rows - first
        row_ids = lax.broadcasted_iota(jnp.int32, (height, LANES), 0)
        heads = [
            jnp.broadcast_to(tiles[0][:, start + first + j : start + first + j + 1], (height, LANES))
            for j in range(GROUP)
        ]
        scale = jnp.zeros((GROUP, LANES), jnp.float32)
        for j in range(GROUP):
            pivot = heads[j][j : j + 1, :]
            factor = jnp.where(row_ids > j, heads[j] * (1.0 / pivot), 0.0)
            for other in range(j + 1, GROUP):
                heads[other] = heads[other] - factor * heads[other][j : j + 1, :]
            tiles = [tile - factor * tile[j : j + 1, :] for tile in tiles]
            root = lax.rsqrt(pivot)
            root = root * (1.5 - 0.5 * pivot * root * root)
            scale = jnp.where(row_ids[:GROUP] == j, root, scale)
        done.append([tile[:GROUP] * scale for tile in tiles])
        tiles = [tile[GROUP:] for tile in tiles]
    return [jnp.concatenate(parts, axis=0) for parts in zip(*done)]


def inverse_factor(source, work, result):
    order = source.shape[0]
    span = order // LANES
    for base in range(0, order, BLOCK):
        low = base // LANES
        row_ids = lax.broadcasted_iota(jnp.int32, (BLOCK, LANES), 0)
        lane_ids = lax.broadcasted_iota(jnp.int32, (BLOCK, LANES), 1)
        unit = jnp.where(lane_ids - base % LANES == row_ids, 1.0, 0.0)
        zero = jnp.zeros((BLOCK, LANES), jnp.float32)
        tiles = [source[base : base + BLOCK, s * LANES : (s + 1) * LANES] for s in range(low, span)]
        tiles += [zero] * low + [unit]
        if base:
            taken = dot32(
                work[0:base, base : base + BLOCK],
                work[0:base, low * LANES : order + (low + 1) * LANES],
                TN,
            )
            tiles = [tile - taken[:, s * LANES : (s + 1) * LANES] for s, tile in enumerate(tiles)]
        tiles = eliminate((tiles, base % LANES))
        for s, tile in enumerate(tiles):
            work[base : base + BLOCK, (low + s) * LANES : (low + s + 1) * LANES] = tile
        for s in range(low + 1, span):
            work[base : base + BLOCK, order + s * LANES : order + (s + 1) * LANES] = zero
    result[...] = work[:, order:]


def fetch(choice, candidates, target, sem):
    for n, candidate in enumerate(candidates):
        copy = pltpu.make_async_copy(candidate, target, sem)
        pl.when(choice == n)(copy.start)
    return pltpu.make_async_copy(candidates[0], target, sem).wait


def first_kernel(place, tiles, result, tile, work, sem):
    @pl.when(place[0] == 0)
    def _():
        copy = pltpu.make_async_copy(tiles.at[0], tile, sem)
        copy.start()
        copy.wait()
        inverse_factor(tile, work, result)


def first_inverse(place, tiles):
    order = tiles.shape[2]
    return pl.pallas_call(
        first_kernel,
        out_shape=jax.ShapeDtypeStruct((order, order), jnp.float32),
        in_specs=[IN_SMEM, ANYWHERE],
        out_specs=IN_VMEM,
        scratch_shapes=[
            pltpu.VMEM((order, order), jnp.float32),
            pltpu.VMEM((order, 2 * order), jnp.float32),
            pltpu.SemaphoreType.DMA,
        ],
        compiler_params=params(8),
        cost_estimate=cost(2**10, 2**10),
        name="first_inverse",
    )(place, tiles)


def second_kernel(place, ranks, tiles, bases, inverse, weights, shifted, work, sem):
    order = inverse.shape[0]
    cap = bases.shape[0] // 2

    @pl.when(place[0] == 1)
    def _():
        copy = pltpu.make_async_copy(tiles.at[0], shifted, sem)
        copy.start()
        weights[:order, :] = inverse[...]
        live = lax.broadcasted_iota(jnp.int32, (cap, order), 0) < ranks[1, 0]
        left = jnp.where(live, bases[:cap, :], 0.0)
        right = jnp.where(live, bases[cap:, :], 0.0)
        solved = dot32(right, inverse[...], NT)
        dense = dot32(left, solved, TN)
        copy.wait()
        shifted[...] = shifted[...] - dot32(dense, dense, NT)
        inverse_factor(shifted, work, weights.at[pl.ds(2 * order, order)])
        weights[order : 2 * order, :] = -dot32(dot32(weights[2 * order :, :], dense, NN), inverse[...], NN)


def second_inverse(place, ranks, tiles, bases, inverse):
    order = inverse.shape[0]
    return pl.pallas_call(
        second_kernel,
        out_shape=jax.ShapeDtypeStruct((3 * order, order), jnp.float32),
        in_specs=[IN_SMEM, IN_SMEM, ANYWHERE, IN_VMEM, IN_VMEM],
        out_specs=IN_VMEM,
        scratch_shapes=[
            pltpu.VMEM((order, order), jnp.float32),
            pltpu.VMEM((order, 2 * order), jnp.float32),
            pltpu.SemaphoreType.DMA,
        ],
        compiler_params=params(8),
        cost_estimate=cost(2**10, 2**10),
        name="second_inverse",
    )(place, ranks, tiles, bases, inverse)


def segment(ranks, panel, group, slot, slots, grid_rows):
    start, count = jnp.int32(0), jnp.int32(0)
    for s in range(slots):
        tile_row = s * grid_rows + group
        rank = jnp.where(tile_row > panel, ranks[tile_row, panel], 0)
        start = start + jnp.where(s < slot, rank, 0)
        count = count + jnp.where(s == slot, rank, 0)
    return start, count


def pack_kernel(capacity, grid_rows, place, ranks, left, right, packed, pivot, held, sem):
    slots, order, cap = held.shape[1:]
    copies = [
        pltpu.make_async_copy(source.at[:, 0], held.at[k], sem.at[k]) for k, source in enumerate((left, right))
    ]
    for copy in copies:
        copy.start()
    panel = jnp.minimum(place[1], 1)
    spot = lax.broadcasted_iota(jnp.int32, (capacity, cap), 0)
    column = lax.broadcasted_iota(jnp.int32, (capacity, cap), 1)
    chosen = []
    for slot in range(slots):
        start, count = segment(ranks, panel, place[0], slot, slots, grid_rows)
        hit = (spot - start == column) & (column < count)
        chosen.append(jnp.where(hit, 1.0, 0.0).astype(jnp.bfloat16))
    for k, copy in enumerate(copies):
        copy.wait()
        total = sum(dot16(chosen[slot], held[k, slot], NT) for slot in range(slots))
        packed[k * capacity : (k + 1) * capacity, :] = total
        pivot[k * cap : (k + 1) * cap, :] = total[:cap]


def pack(place, ranks, left_fac, right_fac, capacity, grid_rows):
    slots, _, order, cap = left_fac.shape
    return pl.pallas_call(
        functools.partial(pack_kernel, capacity, grid_rows),
        out_shape=(
            jax.ShapeDtypeStruct((2 * capacity, order), jnp.float32),
            jax.ShapeDtypeStruct((2 * cap, order), jnp.float32),
        ),
        in_specs=[IN_SMEM, IN_SMEM, IN_HBM, IN_HBM],
        out_specs=(IN_VMEM, IN_VMEM),
        scratch_shapes=[pltpu.VMEM((2, slots, order, cap), jnp.bfloat16), pltpu.SemaphoreType.DMA((2,))],
        compiler_params=params(16),
        cost_estimate=cost(2**10, 2**10),
        name="pack",
    )(place, ranks, left_fac, right_fac)


def pick_kernel(count, index, *refs):
    candidates, target, sem = refs[:count], refs[count], refs[count + 1]
    wait = fetch(index[0], candidates, target, sem)
    pl.when(index[0] >= 0)(wait)


def pick(index, candidates):
    return pl.pallas_call(
        functools.partial(pick_kernel, len(candidates)),
        out_shape=jax.ShapeDtypeStruct(candidates[0].shape, candidates[0].dtype),
        in_specs=[IN_SMEM] + [ANYWHERE] * len(candidates),
        out_specs=ANYWHERE,
        scratch_shapes=[pltpu.SemaphoreType.DMA],
        compiler_params=params(4),
        cost_estimate=cost(0, 2 * candidates[0].size * 4),
        name="pick",
    )(jnp.reshape(index, (1,)).astype(jnp.int32), *candidates)


def rows_kernel(capacity, grid_rows, count, place, ranks, *refs):
    sources, weights, stacked = refs[: 2 * count], refs[2 * count : 2 * count + 2], refs[2 * count + 2]
    landed, inverses, weight_high, weight_low, sems = refs[2 * count + 3 :]
    order = inverses.shape[1]
    inverses_in = fetch(1 - place[0] % 2, weights, inverses, sems.at[4])
    slots = stacked.shape[0]
    cap = LANES
    waits = []
    for t in range(2):
        for k in range(2):
            part = [source.at[pl.ds(k * capacity, capacity)] for source in sources[t * count : (t + 1) * count]]
            waits.append(fetch(place[1], part, landed.at[2 * t + k, pl.ds(0, capacity)], sems.at[2 * t + k]))
            landed[2 * t + k, capacity:, :] = jnp.zeros((cap, order), jnp.float32)
    inverses_in()
    base_parts, second_parts = split2(inverses[: 2 * order, :]), split2(inverses[2 * order :, :])
    for wait in waits:
        wait()
    solved0 = sum(dot16(landed[1].astype(jnp.bfloat16), part, NT) for part in base_parts)
    solved1 = sum(dot16(landed[3].astype(jnp.bfloat16), part, NT) for part in second_parts)
    for column, value in ((0, solved0), (2 * order, solved1)):
        high, low = split2(value)
        weight_high[:, column : column + value.shape[1]] = high
        weight_low[:, column : column + value.shape[1]] = low
    live = lax.broadcasted_iota(jnp.int32, (cap, order), 0)
    for slot in range(slots):
        pieces = []
        for t in range(2):
            start, rank = segment(ranks, t, place[0], slot, slots, grid_rows)
            spot = pl.ds(pl.multiple_of(start, 16), cap)
            left = jnp.where(live < rank, landed[2 * t, spot, :], 0.0).astype(jnp.bfloat16)
            columns = pl.ds(0, 2 * order) if t == 0 else pl.ds(2 * order, order)
            weights = jnp.concatenate([weight_high[spot, columns], weight_low[spot, columns]], axis=0)
            pieces.append(dot16(jnp.concatenate([left, left], axis=0), weights, TN))
        for column, value in ((0, pieces[0][:, :order]), (order, pieces[0][:, order:] + pieces[1])):
            high, low = split2(value)
            stacked[slot, :, column : column + order] = high
            stacked[slot, :, 2 * order + column : 2 * order + column + order] = low
            stacked[slot, :, 4 * order + column : 4 * order + column + order] = high


def row_panels(place, ranks, firsts, seconds, inverses, capacity, slots, grid_rows):
    order = inverses[0].shape[1]
    count = len(firsts)
    return pl.pallas_call(
        functools.partial(rows_kernel, capacity, grid_rows, count),
        out_shape=jax.ShapeDtypeStruct((slots, order, 6 * order), jnp.bfloat16),
        in_specs=[IN_SMEM] * 2 + [ANYWHERE] * (2 * count + 2),
        out_specs=IN_VMEM,
        scratch_shapes=[
            pltpu.VMEM((4, capacity + LANES, order), jnp.float32),
            pltpu.VMEM((3 * order, order), jnp.float32),
            pltpu.VMEM((capacity + LANES, 3 * order), jnp.bfloat16),
            pltpu.VMEM((capacity + LANES, 3 * order), jnp.bfloat16),
            pltpu.SemaphoreType.DMA((5,)),
        ],
        compiler_params=params(20),
        cost_estimate=cost(2**32, 2**22),
        name="row_panels",
    )(place, ranks, *firsts, *seconds, *inverses)


def schur_kernel(capacity, grid_rows, grid_cols, place, ranks, *refs):
    spread = grid_rows // grid_cols
    sources = refs[: 4 * spread]
    weights, (rows, left, right, out) = refs[4 * spread : 4 * spread + 2], refs[4 * spread + 2 : 4 * spread + 6]
    landed, inverses, weight0, weight1, bases, panel, sems = refs[4 * spread + 6 :]
    slots, order, cap = out.shape[0], out.shape[2], left.shape[3]
    padded = landed.shape[1]
    used = padded - LANES
    step = pl.program_id(0)
    row_here, col_here = place[0], place[1]
    mine = row_here // grid_cols

    @pl.when(step == 0)
    def _():
        inverses_in = fetch(1 - row_here % 2, weights, inverses, sems.at[4 * spread])
        passed = (row_here ^ col_here) & 1
        waits = []
        for n in range(2 * spread):
            for k in range(2):
                part = [source.at[pl.ds(k * capacity, capacity)] for source in sources[2 * n : 2 * n + 2]]
                waits.append(fetch(passed, part, landed.at[2 * n + k, pl.ds(0, capacity)], sems.at[2 * n + k]))
                if padded > capacity:
                    landed[2 * n + k, capacity:, :] = jnp.zeros((padded - capacity, order), jnp.float32)
        inverses_in()
        base_parts, second_parts = split2(inverses[: 2 * order, :]), split2(inverses[2 * order :, :])
        for wait in waits:
            wait()
        for g in range(spread):
            right0 = landed[4 * g + 1, :used, :].astype(jnp.bfloat16)
            right1 = landed[4 * g + 3, :used, :].astype(jnp.bfloat16)
            solved0 = sum(dot16(part, right0, NT) for part in base_parts)
            solved1 = sum(dot16(part, right1, NT) for part in second_parts)
            for target, at, value in (
                (weight0, 2 * g, solved0[:order]),
                (weight1, 4 * g, solved0[order:]),
                (weight1, 4 * g + 2, solved1),
            ):
                for n, piece in enumerate(split2(value)):
                    target[at + n, :, :used] = piece
                    target[at + n, :, used:] = jnp.zeros((order, padded - used), jnp.bfloat16)

    tile_col = step * grid_cols + col_here
    last_row = (slots - 1) * grid_rows + row_here

    @pl.when((tile_col > 1) & (last_row > tile_col))
    def _():
        part = step % spread
        g = part ^ mine
        group = part * grid_cols + col_here
        span = 2 * LANES
        ids = lax.broadcasted_iota(jnp.int32, (span, order), 0)
        windows = []
        for t in range(2):
            start, count = segment(ranks, t, group, step // spread, slots, grid_rows)
            first_lane = start // LANES * LANES
            window = pl.ds(pl.multiple_of(first_lane, LANES), span)
            value = landed[4 * g + 2 * t, window, :]
            live = (ids >= start - first_lane) & (ids < start - first_lane + count)
            value = jnp.where(live, value, 0.0).astype(jnp.bfloat16)
            bases[t * span : (t + 1) * span, :] = value
            windows.append(window)
        panel0 = sum(dot16(weight0[2 * g + n, :, windows[0]], bases[:span], NN) for n in range(2))
        panel1 = sum(
            dot16(weight1[4 * g + n, :, windows[n // 2]], bases[n // 2 * span : (n // 2 + 1) * span], NN)
            for n in range(4)
        )
        for at, value in ((0, panel0), (order, panel1)):
            high, low = split2(value)
            panel[at : at + order, :] = high
            panel[2 * order + at : 3 * order + at, :] = high
            panel[4 * order + at : 5 * order + at, :] = low

    for slot in range(slots):
        tile_row = slot * grid_rows + row_here
        below = tile_row > tile_col

        @pl.when(jnp.logical_not(below))
        def _():
            out[slot, 0] = jnp.zeros((order, order), jnp.float32)

        for t in range(2):

            @pl.when(below & (tile_col == t))
            def _():
                high = rows[slot, :, t * order : (t + 1) * order].astype(jnp.float32)
                low = rows[slot, :, (t + 2) * order : (t + 3) * order].astype(jnp.float32)
                out[slot, 0] = high + low

        @pl.when(below & (tile_col > 1))
        def _():
            basis = left[slot, 0].astype(jnp.float32)
            live = lax.broadcasted_iota(jnp.int32, basis.shape, 1) < ranks[tile_row, tile_col]
            front = dot16(jnp.where(live, basis, 0.0).astype(jnp.bfloat16), right[slot, 0], NT)
            out[slot, 0] = front - dot16(rows[slot], panel[...], NN)


def schur(place, ranks, col_arrays, inverses, rows, left_fac, right_fac, capacity, grid_rows, grid_cols):
    slots, steps, order, cap = left_fac.shape
    spread = grid_rows // grid_cols
    padded = (-(-capacity // LANES) + 1) * LANES
    flat = [array for pair in col_arrays for array in pair]
    factor = pl.BlockSpec((slots, 1, order, cap), lambda m: (0, m, 0, 0))
    return pl.pallas_call(
        functools.partial(schur_kernel, capacity, grid_rows, grid_cols),
        grid=(steps,),
        out_shape=pltpu.HBM((slots, steps, order, order), jnp.float32),
        in_specs=[IN_SMEM] * 2 + [ANYWHERE] * (len(flat) + 2) + [IN_VMEM, factor, factor],
        out_specs=pl.BlockSpec((slots, 1, order, order), lambda m: (0, m, 0, 0)),
        scratch_shapes=[
            pltpu.VMEM((4 * spread, padded, order), jnp.float32),
            pltpu.VMEM((3 * order, order), jnp.float32),
            pltpu.VMEM((2 * spread, order, padded), jnp.bfloat16),
            pltpu.VMEM((4 * spread, order, padded), jnp.bfloat16),
            pltpu.VMEM((4 * LANES, order), jnp.bfloat16),
            pltpu.VMEM((6 * order, order), jnp.bfloat16),
            pltpu.SemaphoreType.DMA((4 * spread + 1,)),
        ],
        compiler_params=params(40, dimension_semantics=("arbitrary",)),
        cost_estimate=cost(2**33, 2**24),
        name="schur",
    )(place, ranks, *flat, *inverses, rows, left_fac, right_fac)


def after(array, *others):
    return lax.optimization_barrier((array, *others))[0]


def device_program(capacity, early, diag_tiles, left_fac, right_fac, ranks):
    grid_rows = lax.axis_size("row")
    grid_cols = lax.axis_size("col")
    row_here = lax.axis_index("row")
    col_here = lax.axis_index("col")
    row_slots, _, order, cap = left_fac.shape
    assert cap == LANES and grid_rows % grid_cols == 0 and grid_cols >= 2
    spread = grid_rows // grid_cols
    row_bits = grid_rows.bit_length() - 1
    low_bits = grid_cols.bit_length() - 1
    assert 1 << row_bits == grid_rows and 1 << low_bits == grid_cols
    every_row = range(grid_rows)
    every_col = range(grid_cols)
    place = jnp.stack([row_here, col_here]).astype(jnp.int32)

    def move(array, pairs):
        flat = [(r * grid_cols + c, s * grid_cols + d) for (r, c), (s, d) in pairs]
        return lax.ppermute(array, AXES, flat)

    def down_column(array, root, fences):
        held = [root]
        for bit in range(1, row_bits):
            step = 1 << bit
            got = move(array, [((r, c), (r ^ step, c)) for r in held for c in every_col])
            got = after(got, fences[min(bit, len(fences)) - 1])
            mine = row_here % 2 == root
            array = pick(jnp.where(mine & (row_here >> bit == 0), 0, jnp.where(mine & (row_here >> bit == 1), 1, -1)), [array, got])
            held = held + [r ^ step for r in held]
        return array

    def to_other_parity(array, root):
        return move(array, [((r, c), (r ^ 1, c)) for r in every_row if r % 2 == root for c in every_col])

    def chain_step(array, s):
        return move(array, [((r, c - 1), (r, c)) for c in (s, s + 1) if c < grid_cols for r in every_row])

    inverse0 = first_inverse(place, diag_tiles)
    packed, pivot_bases = pack(after(place, inverse0), ranks, left_fac, right_fac, capacity, grid_rows)
    chain = [packed, chain_step(packed, 1)]
    back = move(packed, [((r, 1), (r, 0)) for r in every_row])

    received = [move(pivot_bases, [((1, 0), (1, c))]) for c in every_col if c]
    pivot_bases = jnp.where(col_here == 0, pivot_bases, sum(received))
    inverse0 = move(inverse0, [((0, c), (1, c)) for c in every_col])
    weights = second_inverse(place, ranks, diag_tiles, pivot_bases, inverse0)
    chain[1], weights, _ = lax.optimization_barrier((chain[1], weights, early))

    for s in range(2, grid_cols):
        chain.append(chain_step(chain[s - 1], s))
    firsts = list(chain)
    seconds = [back] + chain[:-1]
    offset = (row_here ^ col_here) & (grid_cols - 1)

    def source(candidates):
        return pick(jnp.where(offset == 0, col_here, -1), candidates)

    second_source = source(seconds)

    def hop(array, bit, held):
        step = 1 << bit
        return move(
            array,
            [
                ((r + h * grid_cols, c), ((r + h * grid_cols) ^ step, c))
                for c in every_col
                for r in held[c]
                for h in range(spread)
            ],
        )

    def low_hops(have, *fence):
        held = {c: [c] for c in every_col}
        for bit in range(1, low_bits):
            got = hop(have, bit, held)
            got = after(got, *fence) if fence else got
            arrived = (offset >> bit == 1) & (offset & 1 == 0)
            stays = (offset >> bit == 0) & (offset & 1 == 0)
            have = pick(jnp.where(arrived, 1, jnp.where(stays, 0, -1)), [have, got])
            held = {c: held[c] + [r ^ (1 << bit) for r in held[c]] for c in every_col}
        return have

    def high_hops(have):
        held = {c: [r for r in range(grid_cols) if (r ^ c) % 2 == 0] for c in every_col}
        sets = [have]
        for bit in range(low_bits, row_bits):
            sets = sets + [hop(array, bit, held) for array in sets]
        return [[array, hop(array, 0, held)] for array in sets]

    second_have = low_hops(second_source)
    first_source = source([after(array, second_have) for array in firsts])
    weights = down_column(weights, 1, [chain[min(2, grid_cols - 1)], first_source])
    inverses = [weights, to_other_parity(weights, 1)]
    rows = row_panels(place, ranks, firsts, seconds, inverses, capacity, row_slots, grid_rows)
    first_have = low_hops(first_source, rows)
    second_sets, first_sets = high_hops(second_have), high_hops(first_have)
    col_arrays = [sets[g] for g in range(spread) for sets in (first_sets, second_sets)]
    return schur(place, ranks, col_arrays, inverses, rows, left_fac, right_fac, capacity, grid_rows, grid_cols)


def shards(diag_tiles, left_fac, right_fac, ranks):
    row_slots, cap = left_fac.shape[0], left_fac.shape[3]
    grid_rows = lax.axis_size("row")
    full = row_slots * cap
    packed = max(cap, full * 5 // 8)
    args = (diag_tiles, left_fac, right_fac, ranks)
    tile_ids = jnp.arange(ranks.shape[0], dtype=jnp.int32)[:, None]
    live = jnp.where(tile_ids > jnp.arange(2, dtype=jnp.int32)[None, :], ranks[:, :2], 0)
    widest = jnp.max(sum(live[s * grid_rows : (s + 1) * grid_rows] for s in range(row_slots)))
    result = device_program(packed, widest, *args)
    if packed == full:
        return result

    def again(state):
        return jnp.zeros_like(state[0]), device_program(full, state[0], *args)

    return lax.while_loop(lambda state: state[0] > packed, again, (widest, result))[1]


def solution(mesh):
    in_specs = (P("row", None, None), P("row", "col", None, None), P("row", "col", None, None), P())
    out_specs = P("row", "col", None, None)
    return jax.shard_map(shards, mesh=mesh, in_specs=in_specs, out_specs=out_specs, check_vma=False)
```

profile of v0, /device:TPU:15, one launch (start us, length us, event | category | flops | bytes accessed | tf_op | source)
XLA Modules:
  0.0 126.3 jit_solution(7916512092424944387)
XLA Ops:
  0.0 0.1 pad_add_fusion.1.place
  0.1 0.6 first_inverse.3
  0.6 2.9 %pack.3 = (f32[640,256]{1,0:T(8,128)S(1)}, f32[256,256]{1,0:T(8,128)S(1)}) custom-call(s32[2]{0:T(128)S(1)} %pad_add_fusion.1.place, s32[32,32]{1,0:T(8,128)} %ranks.7, bf16[4,8,256,128]{3,2,1,0:T(8,128)(2,1)} %refs_11_.1, bf16[4,8,256,128]{3,2,1,0:T(8,128)(2,1)} %refs_12_.1), custom_call_target="tpu_custom_call" | custom-call | flops 1024 | bytes 1024 | tf_op jit(solution)/shard_map/pack/pallas_call | solution.py:205
  3.5 3.2 %collective-permute-start.20 = (f32[640,256]{1,0:T(8,128)S(1)}, f32[640,256]{1,0:T(8,128)S(1)}, u32[]{:S(2)}, u32[]{:S(2)}) collective-permute-start(f32[640,256]{1,0:T(8,128)S(1)} %get-tuple-element.63.refs_1_.refs_0_.refs_5_), channel_id=1, source_target_pairs={{0,1},{4,5},{8,9},{12,13},{16,17},{20,21},{24,25},{28,29},{1,2},{5... | collective-permute-start | bytes 1966088 | tf_op jit(solution)/shard_map/ppermute | solution.py:444
  6.7 0.7 collective-permute-start.23
  7.4 0.7 collective-permute-start.22
  8.1 0.7 collective-permute-start.21
  8.8 0.7 slice_select_fusion
  9.5 0.7 collective-permute-start.24
  10.2 0.6 fusion
  10.8 0.0 collective-permute-done.23
  10.8 0.0 collective-permute-done.22
  10.8 0.0 collective-permute-done.21
  10.8 0.1 add_select_fusion.1.bases
  10.9 1.2 second_inverse.3.refs_0_
  12.2 8.9 %collective-permute-done.20.refs_2_.refs_1_.refs_6_ = f32[640,256]{1,0:T(8,128)S(1)} collective-permute-done((f32[640,256]{1,0:T(8,128)S(1)}, f32[640,256]{1,0:T(8,128)S(1)}, u32[]{:S(2)}, u32[]{:S(2)}) %collective-permute-start.20) | collective-permute-done | bytes 655392 | tf_op jit(solution)/shard_map/ppermute | solution.py:444
  21.0 0.7 collective-permute-start.29
  21.7 3.2 %collective-permute-start.25 = (f32[640,256]{1,0:T(8,128)S(1)}, f32[640,256]{1,0:T(8,128)S(1)}, u32[]{:S(2)}, u32[]{:S(2)}) collective-permute-start(f32[640,256]{1,0:T(8,128)S(1)} %collective-permute-done.20.refs_2_.refs_1_.refs_6_), channel_id=1, source_target_pairs={{1,2},{5,6},{9,10},{13,14},{17,18},{21,22},{25,26},{29,30},{2,3},{... | collective-permute-start | bytes 1966088 | tf_op jit(solution)/shard_map/ppermute | solution.py:444
  25.0 2.1 %collective-permute-start.19 = (f32[640,256]{1,0:T(8,128)S(1)}, f32[640,256]{1,0:T(8,128)}, u32[]{:S(2)}, u32[]{:S(2)}) collective-permute-start(f32[640,256]{1,0:T(8,128)S(1)} %get-tuple-element.63.refs_1_.refs_0_.refs_5_), channel_id=1, source_target_pairs={{1,0},{5,4},{9,8},{13,12},{17,16},{21,20},{25,24},{29,28}} | collective-permute-start | bytes 1966088 | tf_op jit(solution)/shard_map/ppermute | solution.py:444
  27.1 10.3 %collective-permute-done.25.refs_3_.refs_2_.refs_7_ = f32[640,256]{1,0:T(8,128)S(1)} collective-permute-done((f32[640,256]{1,0:T(8,128)S(1)}, f32[640,256]{1,0:T(8,128)S(1)}, u32[]{:S(2)}, u32[]{:S(2)}) %collective-permute-start.25) | collective-permute-done | bytes 655392 | tf_op jit(solution)/shard_map/ppermute | solution.py:444
  37.4 0.0 collective-permute-done.29.refs_1_
  37.4 0.9 copy-done.3
  38.3 1.1 copy-done.4
  39.4 0.0 copy-start.11
  39.4 1.3 %collective-permute-start.30 = (f32[768,256]{1,0:T(8,128)S(1)}, f32[768,256]{1,0:T(8,128)}, u32[]{:S(2)}, u32[]{:S(2)}) collective-permute-start(f32[768,256]{1,0:T(8,128)S(1)} %pick.21.refs_0_), channel_id=1, source_target_pairs={{4,20},{5,21},{6,22},{7,23},{12,28},{13,29},{14,30},{15,31}} | collective-permute-start | bytes 2359304 | tf_op jit(solution)/shard_map/ppermute | solution.py:444
  40.8 1.3 %collective-permute-start.26 = (f32[640,256]{1,0:T(8,128)S(1)}, f32[640,256]{1,0:T(8,128)}, u32[]{:S(2)}, u32[]{:S(2)}) collective-permute-start(f32[640,256]{1,0:T(8,128)S(1)} %pick.18.refs_0_), channel_id=1, source_target_pairs={{0,8},{16,24},{5,13},{21,29},{10,2},{26,18},{15,7},{31,23}} | collective-permute-start | bytes 1966088 | tf_op jit(solution)/shard_map/ppermute | solution.py:444
  42.1 1.5 %collective-permute-start.27 = (f32[640,256]{1,0:T(8,128)S(1)}, f32[640,256]{1,0:T(8,128)}, u32[]{:S(2)}, u32[]{:S(2)}) collective-permute-start(f32[640,256]{1,0:T(8,128)S(1)} %collective-permute-done.25.refs_3_.refs_2_.refs_7_), channel_id=1, source_target_pairs={{2,3},{6,7},{10,11},{14,15},{18,19},{22,23},{26,27},{30,31}} | collective-permute-start | bytes 1966088 | tf_op jit(solution)/shard_map/ppermute | solution.py:444
  43.6 8.6 %collective-permute-done.26.refs_1_ = f32[640,256]{1,0:T(8,128)} collective-permute-done((f32[640,256]{1,0:T(8,128)S(1)}, f32[640,256]{1,0:T(8,128)}, u32[]{:S(2)}, u32[]{:S(2)}) %collective-permute-start.26) | collective-permute-done | bytes 655392 | tf_op jit(solution)/shard_map/ppermute | solution.py:444
  52.2 1.1 pick.19.refs_2_
  53.4 11.7 %collective-permute-done.30.refs_1_ = f32[768,256]{1,0:T(8,128)} collective-permute-done((f32[768,256]{1,0:T(8,128)S(1)}, f32[768,256]{1,0:T(8,128)}, u32[]{:S(2)}, u32[]{:S(2)}) %collective-permute-start.30) | collective-permute-done | bytes 786464 | tf_op jit(solution)/shard_map/ppermute | solution.py:444
  65.1 1.1 pick.22.refs_8_
  66.3 0.0 copy-start.7
  66.3 0.0 copy-start.9
  66.3 1.6 %collective-permute-start.31 = (f32[768,256]{1,0:T(8,128)S(1)}, f32[768,256]{1,0:T(8,128)S(1)}, u32[]{:S(2)}, u32[]{:S(2)}) collective-permute-start(f32[768,256]{1,0:T(8,128)S(1)} %pick.22.refs_8_), channel_id=1, source_target_pairs={{4,0},{5,1},{6,2},{7,3},{12,8},{13,9},{14,10},{15,11},{20,16},{21,... | collective-permute-start | bytes 2359304 | tf_op jit(solution)/shard_map/ppermute | solution.py:444
  67.9 1.3 %collective-permute-start.28 = (f32[640,256]{1,0:T(8,128)S(1)}, f32[640,256]{1,0:T(8,128)S(1)}, u32[]{:S(2)}, u32[]{:S(2)}) collective-permute-start(f32[640,256]{1,0:T(8,128)S(1)} %pick.20.refs_0_), channel_id=1, source_target_pairs={{0,8},{16,24},{5,13},{21,29},{10,2},{26,18},{15,7},{31,23}} | collective-permute-start | bytes 1966088 | tf_op jit(solution)/shard_map/ppermute | solution.py:444
  69.2 4.9 %collective-permute-start.36 = (f32[640,256]{1,0:T(8,128)S(1)}, f32[640,256]{1,0:T(8,128)S(1)}, u32[]{:S(2)}, u32[]{:S(2)}) collective-permute-start(f32[640,256]{1,0:T(8,128)S(1)} %pick.19.refs_2_), channel_id=1, source_target_pairs={{0,16},{16,0},{8,24},{24,8},{5,21},{21,5},{13,29},{29,13},{2,18},{... | collective-permute-start | bytes 1966088 | tf_op jit(solution)/shard_map/ppermute | solution.py:444
  74.2 2.7 %row_panels.3.refs_10_ = bf16[4,256,1536]{2,1,0:T(8,128)(2,1)S(1)} custom-call(s32[2]{0:T(128)S(1)} %pad_add_fusion.1.place, s32[32,32]{1,0:T(8,128)S(1)} %copy-done.11, f32[640,256]{1,0:T(8,128)S(1)} %get-tuple-element.63.refs_1_.refs_0_.refs_5_, f32[640,256]{1,0:T(8,128)S(1)} %collective-permute-done.20.refs_2_.refs_1_.refs_6_, ...), custom_call_target="tpu_custom_call" | custom-call | flops 4294967296 | bytes 4194304 | tf_op jit(solution)/shard_map/row_panels/pallas_call | solution.py:282
  76.9 2.4 %collective-permute-done.28.refs_1_ = f32[640,256]{1,0:T(8,128)S(1)} collective-permute-done((f32[640,256]{1,0:T(8,128)S(1)}, f32[640,256]{1,0:T(8,128)S(1)}, u32[]{:S(2)}, u32[]{:S(2)}) %collective-permute-start.28) | collective-permute-done | bytes 655392 | tf_op jit(solution)/shard_map/ppermute | solution.py:444
  79.3 0.2 pick.23.refs_0_
  79.5 0.0 copy-start.5
  79.5 5.0 %collective-permute-start.34 = (f32[640,256]{1,0:T(8,128)S(1)}, f32[640,256]{1,0:T(8,128)S(1)}, u32[]{:S(2)}, u32[]{:S(2)}) collective-permute-start(f32[640,256]{1,0:T(8,128)S(1)} %pick.23.refs_0_), channel_id=1, source_target_pairs={{0,16},{16,0},{8,24},{24,8},{5,21},{21,5},{13,29},{29,13},{2,18},{... | collective-permute-start | bytes 1966088 | tf_op jit(solution)/shard_map/ppermute | solution.py:444
  84.5 1.3 %collective-permute-start.33 = (f32[640,256]{1,0:T(8,128)S(1)}, f32[640,256]{1,0:T(8,128)S(1)}, u32[]{:S(2)}, u32[]{:S(2)}) collective-permute-start(f32[640,256]{1,0:T(8,128)S(1)} %pick.19.refs_2_), channel_id=1, source_target_pairs={{0,4},{16,20},{8,12},{24,28},{5,1},{21,17},{13,9},{29,25},{2,6},{1... | collective-permute-start | bytes 1966088 | tf_op jit(solution)/shard_map/ppermute | solution.py:444
  85.9 1.3 %collective-permute-start.37 = (f32[640,256]{1,0:T(8,128)S(1)}, f32[640,256]{1,0:T(8,128)S(1)}, u32[]{:S(2)}, u32[]{:S(2)}) collective-permute-start(f32[640,256]{1,0:T(8,128)S(1)} %collective-permute-done.36.refs_6_), channel_id=1, source_target_pairs={{0,4},{16,20},{8,12},{24,28},{5,1},{21,17},{13,9},{29,25},{2,6},{1... | collective-permute-start | bytes 1966088 | tf_op jit(solution)/shard_map/ppermute | solution.py:444
  87.2 1.3 %collective-permute-start.32 = (f32[640,256]{1,0:T(8,128)S(1)}, f32[640,256]{1,0:T(8,128)S(1)}, u32[]{:S(2)}, u32[]{:S(2)}) collective-permute-start(f32[640,256]{1,0:T(8,128)S(1)} %pick.23.refs_0_), channel_id=1, source_target_pairs={{0,4},{16,20},{8,12},{24,28},{5,1},{21,17},{13,9},{29,25},{2,6},{1... | collective-permute-start | bytes 1966088 | tf_op jit(solution)/shard_map/ppermute | solution.py:444
  88.6 3.9 %collective-permute-done.34.refs_4_ = f32[640,256]{1,0:T(8,128)S(1)} collective-permute-done((f32[640,256]{1,0:T(8,128)S(1)}, f32[640,256]{1,0:T(8,128)S(1)}, u32[]{:S(2)}, u32[]{:S(2)}) %collective-permute-start.34) | collective-permute-done | bytes 655392 | tf_op jit(solution)/shard_map/ppermute | solution.py:444
  92.5 17.5 %collective-permute-start.35 = (f32[640,256]{1,0:T(8,128)S(1)}, f32[640,256]{1,0:T(8,128)S(1)}, u32[]{:S(2)}, u32[]{:S(2)}) collective-permute-start(f32[640,256]{1,0:T(8,128)S(1)} %collective-permute-done.34.refs_4_), channel_id=1, source_target_pairs={{0,4},{16,20},{8,12},{24,28},{5,1},{21,17},{13,9},{29,25},{2,6},{1... | collective-permute-start | bytes 1966088 | tf_op jit(solution)/shard_map/ppermute | solution.py:444
  110.1 15.4 %schur.3 = f32[4,8,256,256]{3,2,1,0:T(8,128)} custom-call(s32[2]{0:T(128)S(1)} %pad_add_fusion.1.place, s32[32,32]{1,0:T(8,128)S(1)} %copy-done.11, f32[640,256]{1,0:T(8,128)S(1)} %pick.23.refs_0_, f32[640,256]{1,0:T(8,128)S(1)} %collective-permute-done.32.refs_1_, f32[640,256]{1,0:T(8,128)S(1)} %pick.19.refs_2_, ...), custom_call_target="tpu_custom_call" | custom-call | flops 8589934592 | bytes 16777216 | tf_op jit(solution)/shard_map/schur/pallas_call | solution.py:402
  125.5 0.6 while.9
  (18 shorter events, 0.1 us)
Async XLA Ops:
  3.5 17.5 %collective-permute-start.20 = (f32[640,256]{1,0:T(8,128)S(1)}, f32[640,256]{1,0:T(8,128)S(1)}, u32[]{:S(2)}, u32[]{:S(2)}) collective-permute-start(f32[640,256]{1,0:T(8,128)S(1)} %get-tuple-element.63.refs_1_.refs_0_.refs_5_), channel_id=1, source_target_pairs={{0,1},{4,5},{8,9},{12,13},{16,17},{20,21},{24,25},{28,29},{1,2},{5... | collective-permute-start | bytes 1966088 | tf_op jit(solution)/shard_map/ppermute | solution.py:444
  6.7 4.1 %collective-permute-start.23 = (f32[256,256]{1,0:T(8,128)S(1)}, f32[256,256]{1,0:T(8,128)S(1)}, u32[]{:S(2)}, u32[]{:S(2)}) collective-permute-start(f32[256,256]{1,0:T(8,128)S(1)} %get-tuple-element.61), channel_id=1, source_target_pairs={{4,7}} | collective-permute-start | bytes 786440 | tf_op jit(solution)/shard_map/ppermute | solution.py:444
  7.4 3.4 %collective-permute-start.22 = (f32[256,256]{1,0:T(8,128)S(1)}, f32[256,256]{1,0:T(8,128)S(1)}, u32[]{:S(2)}, u32[]{:S(2)}) collective-permute-start(f32[256,256]{1,0:T(8,128)S(1)} %get-tuple-element.61), channel_id=1, source_target_pairs={{4,6}} | collective-permute-start | bytes 786440 | tf_op jit(solution)/shard_map/ppermute | solution.py:444
  8.1 2.7 %collective-permute-start.21 = (f32[256,256]{1,0:T(8,128)S(1)}, f32[256,256]{1,0:T(8,128)S(1)}, u32[]{:S(2)}, u32[]{:S(2)}) collective-permute-start(f32[256,256]{1,0:T(8,128)S(1)} %get-tuple-element.61), channel_id=1, source_target_pairs={{4,5}} | collective-permute-start | bytes 786440 | tf_op jit(solution)/shard_map/ppermute | solution.py:444
  9.5 1.4 %collective-permute-start.24 = (f32[256,256]{1,0:T(8,128)S(1)}, f32[256,256]{1,0:T(8,128)S(1)}, u32[]{:S(2)}, u32[]{:S(2)}) collective-permute-start(f32[256,256]{1,0:T(8,128)S(1)} %first_inverse.3), channel_id=1, source_target_pairs={{0,4},{1,5},{2,6},{3,7}} | collective-permute-start | bytes 786440 | tf_op jit(solution)/shard_map/ppermute | solution.py:444
  21.0 16.4 %collective-permute-start.29 = (f32[768,256]{1,0:T(8,128)S(1)}, f32[768,256]{1,0:T(8,128)S(1)}, u32[]{:S(2)}, u32[]{:S(2)}) collective-permute-start(f32[768,256]{1,0:T(8,128)S(1)} %second_inverse.3.refs_0_), channel_id=1, source_target_pairs={{4,12},{5,13},{6,14},{7,15}} | collective-permute-start | bytes 2359304 | tf_op jit(solution)/shard_map/ppermute | solution.py:444
  21.7 15.7 %collective-permute-start.25 = (f32[640,256]{1,0:T(8,128)S(1)}, f32[640,256]{1,0:T(8,128)S(1)}, u32[]{:S(2)}, u32[]{:S(2)}) collective-permute-start(f32[640,256]{1,0:T(8,128)S(1)} %collective-permute-done.20.refs_2_.refs_1_.refs_6_), channel_id=1, source_target_pairs={{1,2},{5,6},{9,10},{13,14},{17,18},{21,22},{25,26},{29,30},{2,3},{... | collective-permute-start | bytes 1966088 | tf_op jit(solution)/shard_map/ppermute | solution.py:444
  25.0 15.8 %collective-permute-start.19 = (f32[640,256]{1,0:T(8,128)S(1)}, f32[640,256]{1,0:T(8,128)}, u32[]{:S(2)}, u32[]{:S(2)}) collective-permute-start(f32[640,256]{1,0:T(8,128)S(1)} %get-tuple-element.63.refs_1_.refs_0_.refs_5_), channel_id=1, source_target_pairs={{1,0},{5,4},{9,8},{13,12},{17,16},{21,20},{25,24},{29,28}} | collective-permute-start | bytes 1966088 | tf_op jit(solution)/shard_map/ppermute | solution.py:444
  37.4 0.9 copy-start.3
  38.3 1.1 copy-start.4
  39.4 34.7 %copy-start.11 = (s32[32,32]{1,0:T(8,128)S(1)}, s32[32,32]{1,0:T(8,128)}, u32[]{:S(2)}) copy-start(s32[32,32]{1,0:T(8,128)} %ranks.7) | copy-start | bytes 12292
  39.4 25.7 %collective-permute-start.30 = (f32[768,256]{1,0:T(8,128)S(1)}, f32[768,256]{1,0:T(8,128)}, u32[]{:S(2)}, u32[]{:S(2)}) collective-permute-start(f32[768,256]{1,0:T(8,128)S(1)} %pick.21.refs_0_), channel_id=1, source_target_pairs={{4,20},{5,21},{6,22},{7,23},{12,28},{13,29},{14,30},{15,31}} | collective-permute-start | bytes 2359304 | tf_op jit(solution)/shard_map/ppermute | solution.py:444
  40.8 11.4 %collective-permute-start.26 = (f32[640,256]{1,0:T(8,128)S(1)}, f32[640,256]{1,0:T(8,128)}, u32[]{:S(2)}, u32[]{:S(2)}) collective-permute-start(f32[640,256]{1,0:T(8,128)S(1)} %pick.18.refs_0_), channel_id=1, source_target_pairs={{0,8},{16,24},{5,13},{21,29},{10,2},{26,18},{15,7},{31,23}} | collective-permute-start | bytes 1966088 | tf_op jit(solution)/shard_map/ppermute | solution.py:444
  42.1 11.2 %collective-permute-start.27 = (f32[640,256]{1,0:T(8,128)S(1)}, f32[640,256]{1,0:T(8,128)}, u32[]{:S(2)}, u32[]{:S(2)}) collective-permute-start(f32[640,256]{1,0:T(8,128)S(1)} %collective-permute-done.25.refs_3_.refs_2_.refs_7_), channel_id=1, source_target_pairs={{2,3},{6,7},{10,11},{14,15},{18,19},{22,23},{26,27},{30,31}} | collective-permute-start | bytes 1966088 | tf_op jit(solution)/shard_map/ppermute | solution.py:444
  66.3 43.8 %copy-start.7 = (bf16[4,8,256,128]{3,2,1,0:T(8,128)(2,1)S(1)}, bf16[4,8,256,128]{3,2,1,0:T(8,128)(2,1)}, u32[]{:S(2)}) copy-start(bf16[4,8,256,128]{3,2,1,0:T(8,128)(2,1)} %refs_11_.1) | copy-start | bytes 6291460
  66.3 43.8 %copy-start.9 = (bf16[4,8,256,128]{3,2,1,0:T(8,128)(2,1)S(1)}, bf16[4,8,256,128]{3,2,1,0:T(8,128)(2,1)}, u32[]{:S(2)}) copy-start(bf16[4,8,256,128]{3,2,1,0:T(8,128)(2,1)} %refs_12_.1) | copy-start | bytes 6291460
  66.3 7.8 %collective-permute-start.31 = (f32[768,256]{1,0:T(8,128)S(1)}, f32[768,256]{1,0:T(8,128)S(1)}, u32[]{:S(2)}, u32[]{:S(2)}) collective-permute-start(f32[768,256]{1,0:T(8,128)S(1)} %pick.22.refs_8_), channel_id=1, source_target_pairs={{4,0},{5,1},{6,2},{7,3},{12,8},{13,9},{14,10},{15,11},{20,16},{21,... | collective-permute-start | bytes 2359304 | tf_op jit(solution)/shard_map/ppermute | solution.py:444
  67.9 11.3 %collective-permute-start.28 = (f32[640,256]{1,0:T(8,128)S(1)}, f32[640,256]{1,0:T(8,128)S(1)}, u32[]{:S(2)}, u32[]{:S(2)}) collective-permute-start(f32[640,256]{1,0:T(8,128)S(1)} %pick.20.refs_0_), channel_id=1, source_target_pairs={{0,8},{16,24},{5,13},{21,29},{10,2},{26,18},{15,7},{31,23}} | collective-permute-start | bytes 1966088 | tf_op jit(solution)/shard_map/ppermute | solution.py:444
  69.2 16.7 %collective-permute-start.36 = (f32[640,256]{1,0:T(8,128)S(1)}, f32[640,256]{1,0:T(8,128)S(1)}, u32[]{:S(2)}, u32[]{:S(2)}) collective-permute-start(f32[640,256]{1,0:T(8,128)S(1)} %pick.19.refs_2_), channel_id=1, source_target_pairs={{0,16},{16,0},{8,24},{24,8},{5,21},{21,5},{13,29},{29,13},{2,18},{... | collective-permute-start | bytes 1966088 | tf_op jit(solution)/shard_map/ppermute | solution.py:444
  79.5 46.0 %copy-start.5 = (f32[4,256,256]{2,1,0:T(8,128)S(1)}, f32[4,256,256]{2,1,0:T(8,128)}, u32[]{:S(2)}) copy-start(f32[4,256,256]{2,1,0:T(8,128)} %tiles.3) | copy-start | bytes 3145732
  79.5 13.0 %collective-permute-start.34 = (f32[640,256]{1,0:T(8,128)S(1)}, f32[640,256]{1,0:T(8,128)S(1)}, u32[]{:S(2)}, u32[]{:S(2)}) collective-permute-start(f32[640,256]{1,0:T(8,128)S(1)} %pick.23.refs_0_), channel_id=1, source_target_pairs={{0,16},{16,0},{8,24},{24,8},{5,21},{21,5},{13,29},{29,13},{2,18},{... | collective-permute-start | bytes 1966088 | tf_op jit(solution)/shard_map/ppermute | solution.py:444
  84.5 25.5 %collective-permute-start.33 = (f32[640,256]{1,0:T(8,128)S(1)}, f32[640,256]{1,0:T(8,128)S(1)}, u32[]{:S(2)}, u32[]{:S(2)}) collective-permute-start(f32[640,256]{1,0:T(8,128)S(1)} %pick.19.refs_2_), channel_id=1, source_target_pairs={{0,4},{16,20},{8,12},{24,28},{5,1},{21,17},{13,9},{29,25},{2,6},{1... | collective-permute-start | bytes 1966088 | tf_op jit(solution)/shard_map/ppermute | solution.py:444
  85.9 24.2 %collective-permute-start.37 = (f32[640,256]{1,0:T(8,128)S(1)}, f32[640,256]{1,0:T(8,128)S(1)}, u32[]{:S(2)}, u32[]{:S(2)}) collective-permute-start(f32[640,256]{1,0:T(8,128)S(1)} %collective-permute-done.36.refs_6_), channel_id=1, source_target_pairs={{0,4},{16,20},{8,12},{24,28},{5,1},{21,17},{13,9},{29,25},{2,6},{1... | collective-permute-start | bytes 1966088 | tf_op jit(solution)/shard_map/ppermute | solution.py:444
  87.2 22.8 %collective-permute-start.32 = (f32[640,256]{1,0:T(8,128)S(1)}, f32[640,256]{1,0:T(8,128)S(1)}, u32[]{:S(2)}, u32[]{:S(2)}) collective-permute-start(f32[640,256]{1,0:T(8,128)S(1)} %pick.23.refs_0_), channel_id=1, source_target_pairs={{0,4},{16,20},{8,12},{24,28},{5,1},{21,17},{13,9},{29,25},{2,6},{1... | collective-permute-start | bytes 1966088 | tf_op jit(solution)/shard_map/ppermute | solution.py:444
  92.5 17.6 %collective-permute-start.35 = (f32[640,256]{1,0:T(8,128)S(1)}, f32[640,256]{1,0:T(8,128)S(1)}, u32[]{:S(2)}, u32[]{:S(2)}) collective-permute-start(f32[640,256]{1,0:T(8,128)S(1)} %collective-permute-done.34.refs_4_), channel_id=1, source_target_pairs={{0,4},{16,20},{8,12},{24,28},{5,1},{21,17},{13,9},{29,25},{2,6},{1... | collective-permute-start | bytes 1966088 | tf_op jit(solution)/shard_map/ppermute | solution.py:444
where the time goes:
time: 124 us; the launch traced here: 126 us
  starting transfers between devices  50.5 us (41%)
  waiting for transfers between devices  45.8 us (37%)
  Pallas kernels  25.3 us (20%)
  local copies, waits for them, and re-layouts  2.04 us (2%)
  other arithmetic  1.5 us (1%)
    ppermute x19, starting transfers between devices, move(): return lax.ppermute(array, AXES, flat)  50.5 us
    ppermute x19, waiting for transfers between devices, move(): return lax.ppermute(array, AXES, flat)  45.8 us
    pallas_call x1, Pallas kernels, schur(): pl.pallas_call(functools.partial(schur_kernel, capacity, grid_rows, grid_...  15.4 us
    pallas_call x1, Pallas kernels, pack(): pl.pallas_call(functools.partial(pack_kernel, capacity, grid_rows), out_s...  2.88 us
    pallas_call x1, Pallas kernels, row_panels(): pl.pallas_call(functools.partial(rows_kernel, capacity, grid_rows, count)...  2.71 us
    pallas_call x6, Pallas kernels, pick(): pl.pallas_call(functools.partial(pick_kernel, len(candidates)), out_shape...  2.53 us
  transfers between devices with their start and end apart: 19, of which 6 were waited for; matrix products, arithmetic and copies ran while one was open for 1% of the time, Pallas kernels for 4%

commit v1 on v0

--- a/solution.py
+++ b/solution.py
@@ -231,7 +231,7 @@
         out_specs=ANYWHERE,
         scratch_shapes=[pltpu.SemaphoreType.DMA],
         compiler_params=params(4),
-        cost_estimate=cost(0, 2 * candidates[0].size * 4),
+        cost_estimate=cost(2**32, 2**20),
         name="pick",
     )(jnp.reshape(index, (1,)).astype(jnp.int32), *candidates)
 
@@ -292,7 +292,7 @@
             pltpu.SemaphoreType.DMA((5,)),
         ],
         compiler_params=params(20),
-        cost_estimate=cost(2**32, 2**22),
+        cost_estimate=cost(2**10, 2**10),
         name="row_panels",
     )(place, ranks, *firsts, *seconds, *inverses)
 
@@ -424,7 +424,7 @@
     return lax.optimization_barrier((array, *others))[0]
 
 
-def device_program(capacity, early, diag_tiles, left_fac, right_fac, ranks):
+def device_program(capacity, early, inverses, diag_tiles, left_fac, right_fac, ranks):
     grid_rows = lax.axis_size("row")
     grid_cols = lax.axis_size("col")
     row_here = lax.axis_index("row")
@@ -460,16 +460,19 @@
     def chain_step(array, s):
         return move(array, [((r, c - 1), (r, c)) for c in (s, s + 1) if c < grid_cols for r in every_row])
 
-    inverse0 = first_inverse(place, diag_tiles)
-    packed, pivot_bases = pack(after(place, inverse0), ranks, left_fac, right_fac, capacity, grid_rows)
+    factoring = inverses is None
+    if factoring:
+        inverse0 = first_inverse(place, diag_tiles)
+    packed, pivot_bases = pack(after(place, inverse0) if factoring else place, ranks, left_fac, right_fac, capacity, grid_rows)
     chain = [packed, chain_step(packed, 1)]
     back = move(packed, [((r, 1), (r, 0)) for r in every_row])
 
-    received = [move(pivot_bases, [((1, 0), (1, c))]) for c in every_col if c]
-    pivot_bases = jnp.where(col_here == 0, pivot_bases, sum(received))
-    inverse0 = move(inverse0, [((0, c), (1, c)) for c in every_col])
-    weights = second_inverse(place, ranks, diag_tiles, pivot_bases, inverse0)
-    chain[1], weights, _ = lax.optimization_barrier((chain[1], weights, early))
+    if factoring:
+        received = [move(pivot_bases, [((1, 0), (1, c))]) for c in every_col if c]
+        pivot_bases = jnp.where(col_here == 0, pivot_bases, sum(received))
+        inverse0 = move(inverse0, [((0, c), (1, c)) for c in every_col])
+        weights = second_inverse(place, ranks, diag_tiles, pivot_bases, inverse0)
+        chain[1], weights, _ = lax.optimization_barrier((chain[1], weights, early))
 
     for s in range(2, grid_cols):
         chain.append(chain_step(chain[s - 1], s))
@@ -512,15 +515,16 @@
             sets = sets + [hop(array, bit, held) for array in sets]
         return [[array, hop(array, 0, held)] for array in sets]
 
-    second_have = low_hops(second_source)
-    first_source = source([after(array, second_have) for array in firsts])
-    weights = down_column(weights, 1, [chain[min(2, grid_cols - 1)], first_source])
-    inverses = [weights, to_other_parity(weights, 1)]
+    first_source = source(firsts)
+    second_have = low_hops(second_source, first_source)
+    if factoring:
+        weights = down_column(weights, 1, [chain[min(2, grid_cols - 1)], second_have])
+        inverses = [weights, to_other_parity(weights, 1)]
     rows = row_panels(place, ranks, firsts, seconds, inverses, capacity, row_slots, grid_rows)
     first_have = low_hops(first_source, rows)
     second_sets, first_sets = high_hops(second_have), high_hops(first_have)
     col_arrays = [sets[g] for g in range(spread) for sets in (first_sets, second_sets)]
-    return schur(place, ranks, col_arrays, inverses, rows, left_fac, right_fac, capacity, grid_rows, grid_cols)
+    return schur(place, ranks, col_arrays, inverses, rows, left_fac, right_fac, capacity, grid_rows, grid_cols), inverses
 
 
 def shards(diag_tiles, left_fac, right_fac, ranks):
@@ -532,12 +536,12 @@
     tile_ids = jnp.arange(ranks.shape[0], dtype=jnp.int32)[:, None]
     live = jnp.where(tile_ids > jnp.arange(2, dtype=jnp.int32)[None, :], ranks[:, :2], 0)
     widest = jnp.max(sum(live[s * grid_rows : (s + 1) * grid_rows] for s in range(row_slots)))
-    result = device_program(packed, widest, *args)
+    result, inverses = device_program(packed, widest, None, *args)
     if packed == full:
         return result
 
     def again(state):
-        return jnp.zeros_like(state[0]), device_program(full, state[0], *args)
+        return jnp.zeros_like(state[0]), device_program(full, state[0], inverses, *args)[0]
 
     return lax.while_loop(lambda state: state[0] > packed, again, (widest, result))[1]
 

time: 124 us -> 121 us (0.976)
  the two profiles are of different devices: /device:TPU:15 before, /device:TPU:7 now
where the time goes in v1:
time: 121 us; the launch traced here: 120 us
  waiting for transfers between devices  70.7 us (58%)
  Pallas kernels  22.8 us (19%)
  starting transfers between devices  21.3 us (18%)
  local copies, waits for them, and re-layouts  2.47 us (2%)
  other arithmetic  1.54 us (1%)
    ppermute x19, waiting for transfers between devices, move(): return lax.ppermute(array, AXES, flat)  70.7 us
    ppermute x19, starting transfers between devices, move(): return lax.ppermute(array, AXES, flat)  21.3 us
    pallas_call x1, Pallas kernels, schur(): pl.pallas_call(functools.partial(schur_kernel, capacity, grid_rows, grid_...  15.3 us
    pallas_call x1, Pallas kernels, pack(): pl.pallas_call(functools.partial(pack_kernel, capacity, grid_rows), out_s...  2.88 us
    pallas_call x1, Pallas kernels, row_panels(): pl.pallas_call(functools.partial(rows_kernel, capacity, grid_rows, count)...  2.71 us
    unnamed x14, local copies, waits for them, and re-layouts  2.47 us
  transfers between devices with their start and end apart: 19, of which 7 were waited for; matrix products, arithmetic and copies ran while one was open for 1% of the time, Pallas kernels for 3%

profile of v1, /device:TPU:7, one launch (start us, length us, event | category | flops | bytes accessed | tf_op | source)
XLA Modules:
  0.0 119.9 jit_solution(5239857142686371418)
XLA Ops:
  0.0 0.1 pad_add_fusion.1.place
  0.1 1.2 %copy-done = f32[4,256,256]{2,1,0:T(8,128)S(1)} copy-done((f32[4,256,256]{2,1,0:T(8,128)S(1)}, f32[4,256,256]{2,1,0:T(8,128)}, u32[]{:S(2)}) %copy-start) | copy-done | bytes 1048600
  1.3 0.6 first_inverse.1
  1.9 2.9 %pack.3 = (f32[640,256]{1,0:T(8,128)S(1)}, f32[256,256]{1,0:T(8,128)S(1)}) custom-call(s32[2]{0:T(128)S(1)} %pad_add_fusion.1.place, s32[32,32]{1,0:T(8,128)} %ranks.7, bf16[4,8,256,128]{3,2,1,0:T(8,128)(2,1)} %refs_11_.1, bf16[4,8,256,128]{3,2,1,0:T(8,128)(2,1)} %refs_12_.1), custom_call_target="tpu_custom_call" | custom-call | flops 1024 | bytes 1024 | tf_op jit(solution)/shard_map/pack/pallas_call | solution.py:205
  4.8 3.2 %collective-permute-start.12 = (f32[640,256]{1,0:T(8,128)S(1)}, f32[640,256]{1,0:T(8,128)S(1)}, u32[]{:S(2)}, u32[]{:S(2)}) collective-permute-start(f32[640,256]{1,0:T(8,128)S(1)} %get-tuple-element.53.refs_0_.refs_1_.refs_5_), channel_id=1, source_target_pairs={{0,1},{4,5},{8,9},{12,13},{16,17},{20,21},{24,25},{28,29},{1,2},{5... | collective-permute-start | bytes 1966088 | tf_op jit(solution)/shard_map/ppermute | solution.py:444
  8.0 0.7 collective-permute-start.15
  8.7 0.7 collective-permute-start.14
  9.4 0.7 collective-permute-start.13
  10.1 0.7 slice_select_fusion
  10.8 0.7 collective-permute-start.16
  11.5 0.7 fusion
  12.1 0.0 collective-permute-done.15
  12.1 0.0 collective-permute-done.14
  12.1 0.0 collective-permute-done.13
  12.1 0.1 add_select_fusion.bases
  12.2 0.0 copy-start.1
  12.2 1.2 %copy-done.1 = f32[4,256,256]{2,1,0:T(8,128)S(1)} copy-done((f32[4,256,256]{2,1,0:T(8,128)S(1)}, f32[4,256,256]{2,1,0:T(8,128)}, u32[]{:S(2)}) %copy-start.1) | copy-done | bytes 1048600
  13.5 1.1 second_inverse.1.refs_0_
  14.6 6.7 %collective-permute-done.12.refs_1_.refs_2_.refs_6_ = f32[640,256]{1,0:T(8,128)S(1)} collective-permute-done((f32[640,256]{1,0:T(8,128)S(1)}, f32[640,256]{1,0:T(8,128)S(1)}, u32[]{:S(2)}, u32[]{:S(2)}) %collective-permute-start.12) | collective-permute-done | bytes 655392 | tf_op jit(solution)/shard_map/ppermute | solution.py:444
  21.3 0.7 collective-permute-start.17
  22.0 1.3 %collective-permute-start.20 = (f32[640,256]{1,0:T(8,128)S(1)}, f32[640,256]{1,0:T(8,128)S(1)}, u32[]{:S(2)}, u32[]{:S(2)}) collective-permute-start(f32[640,256]{1,0:T(8,128)S(1)} %get-tuple-element.53.refs_0_.refs_1_.refs_5_), channel_id=1, source_target_pairs={{1,0},{5,4},{9,8},{13,12},{17,16},{21,20},{25,24},{29,28}} | collective-permute-start | bytes 1966088 | tf_op jit(solution)/shard_map/ppermute | solution.py:444
  23.3 1.6 %collective-permute-start.21 = (f32[768,256]{1,0:T(8,128)S(1)}, f32[768,256]{1,0:T(8,128)}, u32[]{:S(2)}, u32[]{:S(2)}) collective-permute-start(f32[768,256]{1,0:T(8,128)S(1)} %second_inverse.1.refs_0_), channel_id=1, source_target_pairs={{4,12},{5,13},{6,14},{7,15}} | collective-permute-start | bytes 2359304 | tf_op jit(solution)/shard_map/ppermute | solution.py:444
  24.9 0.0 collective-permute-done.17.refs_2_.refs_3_.refs_7_
  24.9 0.7 collective-permute-start.18
  25.6 15.7 %collective-permute-done.20.refs_0_.refs_4_ = f32[640,256]{1,0:T(8,128)S(1)} collective-permute-done((f32[640,256]{1,0:T(8,128)S(1)}, f32[640,256]{1,0:T(8,128)S(1)}, u32[]{:S(2)}, u32[]{:S(2)}) %collective-permute-start.20) | collective-permute-done | bytes 655392 | tf_op jit(solution)/shard_map/ppermute | solution.py:444
  41.3 0.7 collective-permute-start.23
  42.0 1.3 %collective-permute-start.22 = (f32[768,256]{1,0:T(8,128)S(1)}, f32[768,256]{1,0:T(8,128)S(1)}, u32[]{:S(2)}, u32[]{:S(2)}) collective-permute-start(f32[768,256]{1,0:T(8,128)S(1)} %pick.15.refs_0_), channel_id=1, source_target_pairs={{4,20},{5,21},{6,22},{7,23},{12,28},{13,29},{14,30},{15,31}} | collective-permute-start | bytes 2359304 | tf_op jit(solution)/shard_map/ppermute | solution.py:444
  43.3 0.0 collective-permute-done.18.refs_3_
  43.5 0.0 copy-start.10
  43.5 38.1 %collective-permute-done.22.refs_1_ = f32[768,256]{1,0:T(8,128)S(1)} collective-permute-done((f32[768,256]{1,0:T(8,128)S(1)}, f32[768,256]{1,0:T(8,128)S(1)}, u32[]{:S(2)}, u32[]{:S(2)}) %collective-permute-start.22) | collective-permute-done | bytes 786464 | tf_op jit(solution)/shard_map/ppermute | solution.py:444
  81.5 0.1 pick.18.refs_8_
  81.6 1.3 %collective-permute-start.24 = (f32[768,256]{1,0:T(8,128)S(1)}, f32[768,256]{1,0:T(8,128)S(1)}, u32[]{:S(2)}, u32[]{:S(2)}) collective-permute-start(f32[768,256]{1,0:T(8,128)S(1)} %pick.18.refs_8_), channel_id=1, source_target_pairs={{4,0},{5,1},{6,2},{7,3},{12,8},{13,9},{14,10},{15,11},{20,16},{21,... | collective-permute-start | bytes 2359304 | tf_op jit(solution)/shard_map/ppermute | solution.py:444
  83.0 0.7 collective-permute-start.19
  83.7 0.7 collective-permute-start.29
  84.4 0.4 collective-permute-done.24.refs_9_
  84.8 2.7 %row_panels.3.refs_10_ = bf16[4,256,1536]{2,1,0:T(8,128)(2,1)S(1)} custom-call(s32[2]{0:T(128)S(1)} %pad_add_fusion.1.place, s32[32,32]{1,0:T(8,128)S(1)} %copy-done.10, f32[640,256]{1,0:T(8,128)S(1)} %get-tuple-element.53.refs_0_.refs_1_.refs_5_, f32[640,256]{1,0:T(8,128)S(1)} %collective-permute-done.12.refs_1_.refs_2_.refs_6_, ...), custom_call_target="tpu_custom_call" | custom-call | flops 1024 | bytes 1024 | tf_op jit(solution)/shard_map/row_panels/pallas_call | solution.py:282
  87.5 0.0 copy-start.2
  87.5 0.0 copy-start.4
  87.6 0.8 collective-permute-start.27
  88.5 1.4 %collective-permute-start.26 = (f32[640,256]{1,0:T(8,128)S(1)}, f32[640,256]{1,0:T(8,128)S(1)}, u32[]{:S(2)}, u32[]{:S(2)}) collective-permute-start(f32[640,256]{1,0:T(8,128)S(1)} %pick.17.refs_2_), channel_id=1, source_target_pairs={{0,4},{16,20},{8,12},{24,28},{5,1},{21,17},{13,9},{29,25},{2,6},{1... | collective-permute-start | bytes 1966088 | tf_op jit(solution)/shard_map/ppermute | solution.py:444
  89.9 1.3 %collective-permute-start.30 = (f32[640,256]{1,0:T(8,128)S(1)}, f32[640,256]{1,0:T(8,128)S(1)}, u32[]{:S(2)}, u32[]{:S(2)}) collective-permute-start(f32[640,256]{1,0:T(8,128)S(1)} %collective-permute-done.29.refs_6_), channel_id=1, source_target_pairs={{0,4},{16,20},{8,12},{24,28},{5,1},{21,17},{13,9},{29,25},{2,6},{1... | collective-permute-start | bytes 1966088 | tf_op jit(solution)/shard_map/ppermute | solution.py:444
  91.2 1.3 %collective-permute-start.25 = (f32[640,256]{1,0:T(8,128)S(1)}, f32[640,256]{1,0:T(8,128)S(1)}, u32[]{:S(2)}, u32[]{:S(2)}) collective-permute-start(f32[640,256]{1,0:T(8,128)S(1)} %pick.19.refs_0_), channel_id=1, source_target_pairs={{0,4},{16,20},{8,12},{24,28},{5,1},{21,17},{13,9},{29,25},{2,6},{1... | collective-permute-start | bytes 1966088 | tf_op jit(solution)/shard_map/ppermute | solution.py:444
  92.5 1.5 %collective-permute-start.28 = (f32[640,256]{1,0:T(8,128)S(1)}, f32[640,256]{1,0:T(8,128)S(1)}, u32[]{:S(2)}, u32[]{:S(2)}) collective-permute-start(f32[640,256]{1,0:T(8,128)S(1)} %collective-permute-done.27.refs_4_), channel_id=1, source_target_pairs={{0,4},{16,20},{8,12},{24,28},{5,1},{21,17},{13,9},{29,25},{2,6},{1... | collective-permute-start | bytes 1966088 | tf_op jit(solution)/shard_map/ppermute | solution.py:444
  94.0 0.6 collective-permute-done.30.refs_7_
  94.6 1.3 %collective-permute-done.25.refs_1_ = f32[640,256]{1,0:T(8,128)S(1)} collective-permute-done((f32[640,256]{1,0:T(8,128)S(1)}, f32[640,256]{1,0:T(8,128)S(1)}, u32[]{:S(2)}, u32[]{:S(2)}) %collective-permute-start.25) | collective-permute-done | bytes 655392 | tf_op jit(solution)/shard_map/ppermute | solution.py:444
  95.9 7.9 %collective-permute-done.28.refs_5_ = f32[640,256]{1,0:T(8,128)S(1)} collective-permute-done((f32[640,256]{1,0:T(8,128)S(1)}, f32[640,256]{1,0:T(8,128)S(1)}, u32[]{:S(2)}, u32[]{:S(2)}) %collective-permute-start.28) | collective-permute-done | bytes 655392 | tf_op jit(solution)/shard_map/ppermute | solution.py:444
  103.8 15.3 %schur.3 = f32[4,8,256,256]{3,2,1,0:T(8,128)} custom-call(s32[2]{0:T(128)S(1)} %pad_add_fusion.1.place, s32[32,32]{1,0:T(8,128)S(1)} %copy-done.10, f32[640,256]{1,0:T(8,128)S(1)} %pick.19.refs_0_, f32[640,256]{1,0:T(8,128)S(1)} %collective-permute-done.25.refs_1_, f32[640,256]{1,0:T(8,128)S(1)} %pick.17.refs_2_, ...), custom_call_target="tpu_custom_call" | custom-call | flops 8589934592 | bytes 16777216 | tf_op jit(solution)/shard_map/schur/pallas_call | solution.py:402
  119.1 0.6 while.9
  (20 shorter events, 0.2 us)
Async XLA Ops:
  0.1 1.2 %copy-start = (f32[4,256,256]{2,1,0:T(8,128)S(1)}, f32[4,256,256]{2,1,0:T(8,128)}, u32[]{:S(2)}) copy-start(f32[4,256,256]{2,1,0:T(8,128)} %tiles.3) | copy-start | bytes 3145732
  4.8 16.6 %collective-permute-start.12 = (f32[640,256]{1,0:T(8,128)S(1)}, f32[640,256]{1,0:T(8,128)S(1)}, u32[]{:S(2)}, u32[]{:S(2)}) collective-permute-start(f32[640,256]{1,0:T(8,128)S(1)} %get-tuple-element.53.refs_0_.refs_1_.refs_5_), channel_id=1, source_target_pairs={{0,1},{4,5},{8,9},{12,13},{16,17},{20,21},{24,25},{28,29},{1,2},{5... | collective-permute-start | bytes 1966088 | tf_op jit(solution)/shard_map/ppermute | solution.py:444
  8.0 4.1 %collective-permute-start.15 = (f32[256,256]{1,0:T(8,128)S(1)}, f32[256,256]{1,0:T(8,128)S(1)}, u32[]{:S(2)}, u32[]{:S(2)}) collective-permute-start(f32[256,256]{1,0:T(8,128)S(1)} %get-tuple-element.54), channel_id=1, source_target_pairs={{4,7}} | collective-permute-start | bytes 786440 | tf_op jit(solution)/shard_map/ppermute | solution.py:444
  8.7 3.4 %collective-permute-start.14 = (f32[256,256]{1,0:T(8,128)S(1)}, f32[256,256]{1,0:T(8,128)S(1)}, u32[]{:S(2)}, u32[]{:S(2)}) collective-permute-start(f32[256,256]{1,0:T(8,128)S(1)} %get-tuple-element.54), channel_id=1, source_target_pairs={{4,6}} | collective-permute-start | bytes 786440 | tf_op jit(solution)/shard_map/ppermute | solution.py:444
  9.4 2.8 %collective-permute-start.13 = (f32[256,256]{1,0:T(8,128)S(1)}, f32[256,256]{1,0:T(8,128)S(1)}, u32[]{:S(2)}, u32[]{:S(2)}) collective-permute-start(f32[256,256]{1,0:T(8,128)S(1)} %get-tuple-element.54), channel_id=1, source_target_pairs={{4,5}} | collective-permute-start | bytes 786440 | tf_op jit(solution)/shard_map/ppermute | solution.py:444
  10.8 1.4 %collective-permute-start.16 = (f32[256,256]{1,0:T(8,128)S(1)}, f32[256,256]{1,0:T(8,128)S(1)}, u32[]{:S(2)}, u32[]{:S(2)}) collective-permute-start(f32[256,256]{1,0:T(8,128)S(1)} %first_inverse.1), channel_id=1, source_target_pairs={{0,4},{1,5},{2,6},{3,7}} | collective-permute-start | bytes 786440 | tf_op jit(solution)/shard_map/ppermute | solution.py:444
  12.2 1.2 %copy-start.1 = (f32[4,256,256]{2,1,0:T(8,128)S(1)}, f32[4,256,256]{2,1,0:T(8,128)}, u32[]{:S(2)}) copy-start(f32[4,256,256]{2,1,0:T(8,128)} %tiles.3) | copy-start | bytes 3145732
  21.3 3.6 %collective-permute-start.17 = (f32[640,256]{1,0:T(8,128)S(1)}, f32[640,256]{1,0:T(8,128)S(1)}, u32[]{:S(2)}, u32[]{:S(2)}) collective-permute-start(f32[640,256]{1,0:T(8,128)S(1)} %collective-permute-done.12.refs_1_.refs_2_.refs_6_), channel_id=1, source_target_pairs={{1,2},{5,6},{9,10},{13,14},{17,18},{21,22},{25,26},{29,30},{2,3},{... | collective-permute-start | bytes 1966088 | tf_op jit(solution)/shard_map/ppermute | solution.py:444
  22.0 19.2 %collective-permute-start.20 = (f32[640,256]{1,0:T(8,128)S(1)}, f32[640,256]{1,0:T(8,128)S(1)}, u32[]{:S(2)}, u32[]{:S(2)}) collective-permute-start(f32[640,256]{1,0:T(8,128)S(1)} %get-tuple-element.53.refs_0_.refs_1_.refs_5_), channel_id=1, source_target_pairs={{1,0},{5,4},{9,8},{13,12},{17,16},{21,20},{25,24},{29,28}} | collective-permute-start | bytes 1966088 | tf_op jit(solution)/shard_map/ppermute | solution.py:444
  23.3 18.7 %collective-permute-start.21 = (f32[768,256]{1,0:T(8,128)S(1)}, f32[768,256]{1,0:T(8,128)}, u32[]{:S(2)}, u32[]{:S(2)}) collective-permute-start(f32[768,256]{1,0:T(8,128)S(1)} %second_inverse.1.refs_0_), channel_id=1, source_target_pairs={{4,12},{5,13},{6,14},{7,15}} | collective-permute-start | bytes 2359304 | tf_op jit(solution)/shard_map/ppermute | solution.py:444
  24.9 18.4 %collective-permute-start.18 = (f32[640,256]{1,0:T(8,128)S(1)}, f32[640,256]{1,0:T(8,128)S(1)}, u32[]{:S(2)}, u32[]{:S(2)}) collective-permute-start(f32[640,256]{1,0:T(8,128)S(1)} %collective-permute-done.17.refs_2_.refs_3_.refs_7_), channel_id=1, source_target_pairs={{2,3},{6,7},{10,11},{14,15},{18,19},{22,23},{26,27},{30,31}} | collective-permute-start | bytes 1966088 | tf_op jit(solution)/shard_map/ppermute | solution.py:444
  41.3 2.1 %collective-permute-start.23 = (f32[640,256]{1,0:T(8,128)S(1)}, f32[640,256]{1,0:T(8,128)S(1)}, u32[]{:S(2)}, u32[]{:S(2)}) collective-permute-start(f32[640,256]{1,0:T(8,128)S(1)} %pick.16.refs_0_), channel_id=1, source_target_pairs={{0,8},{16,24},{5,13},{21,29},{10,2},{26,18},{15,7},{31,23}} | collective-permute-start | bytes 1966088 | tf_op jit(solution)/shard_map/ppermute | solution.py:444
  42.0 39.5 %collective-permute-start.22 = (f32[768,256]{1,0:T(8,128)S(1)}, f32[768,256]{1,0:T(8,128)S(1)}, u32[]{:S(2)}, u32[]{:S(2)}) collective-permute-start(f32[768,256]{1,0:T(8,128)S(1)} %pick.15.refs_0_), channel_id=1, source_target_pairs={{4,20},{5,21},{6,22},{7,23},{12,28},{13,29},{14,30},{15,31}} | collective-permute-start | bytes 2359304 | tf_op jit(solution)/shard_map/ppermute | solution.py:444
  43.5 41.4 %copy-start.10 = (s32[32,32]{1,0:T(8,128)S(1)}, s32[32,32]{1,0:T(8,128)}, u32[]{:S(2)}) copy-start(s32[32,32]{1,0:T(8,128)} %ranks.7) | copy-start | bytes 12292
  81.6 22.2 %copy-start.6 = (f32[768,256]{1,0:T(8,128)}, f32[768,256]{1,0:T(8,128)S(1)}, u32[]{:S(2)}) copy-start(f32[768,256]{1,0:T(8,128)S(1)} %pick.18.refs_8_) | copy-start | bytes 2359300
  81.6 3.2 %collective-permute-start.24 = (f32[768,256]{1,0:T(8,128)S(1)}, f32[768,256]{1,0:T(8,128)S(1)}, u32[]{:S(2)}, u32[]{:S(2)}) collective-permute-start(f32[768,256]{1,0:T(8,128)S(1)} %pick.18.refs_8_), channel_id=1, source_target_pairs={{4,0},{5,1},{6,2},{7,3},{12,8},{13,9},{14,10},{15,11},{20,16},{21,... | collective-permute-start | bytes 2359304 | tf_op jit(solution)/shard_map/ppermute | solution.py:444
  83.0 4.6 %collective-permute-start.19 = (f32[640,256]{1,0:T(8,128)S(1)}, f32[640,256]{1,0:T(8,128)S(1)}, u32[]{:S(2)}, u32[]{:S(2)}) collective-permute-start(f32[640,256]{1,0:T(8,128)S(1)} %pick.14.refs_0_), channel_id=1, source_target_pairs={{0,8},{16,24},{5,13},{21,29},{10,2},{26,18},{15,7},{31,23}} | collective-permute-start | bytes 1966088 | tf_op jit(solution)/shard_map/ppermute | solution.py:444
  83.7 6.2 %collective-permute-start.29 = (f32[640,256]{1,0:T(8,128)S(1)}, f32[640,256]{1,0:T(8,128)S(1)}, u32[]{:S(2)}, u32[]{:S(2)}) collective-permute-start(f32[640,256]{1,0:T(8,128)S(1)} %pick.17.refs_2_), channel_id=1, source_target_pairs={{0,16},{16,0},{8,24},{24,8},{5,21},{21,5},{13,29},{29,13},{2,18},{... | collective-permute-start | bytes 1966088 | tf_op jit(solution)/shard_map/ppermute | solution.py:444
  84.8 19.0 %copy-start.8 = (f32[768,256]{1,0:T(8,128)}, f32[768,256]{1,0:T(8,128)S(1)}, u32[]{:S(2)}) copy-start(f32[768,256]{1,0:T(8,128)S(1)} %collective-permute-done.24.refs_9_) | copy-start | bytes 2359300
  87.5 16.2 %copy-start.2 = (bf16[4,8,256,128]{3,2,1,0:T(8,128)(2,1)S(1)}, bf16[4,8,256,128]{3,2,1,0:T(8,128)(2,1)}, u32[]{:S(2)}) copy-start(bf16[4,8,256,128]{3,2,1,0:T(8,128)(2,1)} %refs_11_.1) | copy-start | bytes 6291460
  87.5 16.2 %copy-start.4 = (bf16[4,8,256,128]{3,2,1,0:T(8,128)(2,1)S(1)}, bf16[4,8,256,128]{3,2,1,0:T(8,128)(2,1)}, u32[]{:S(2)}) copy-start(bf16[4,8,256,128]{3,2,1,0:T(8,128)(2,1)} %refs_12_.1) | copy-start | bytes 6291460
  87.6 4.9 %collective-permute-start.27 = (f32[640,256]{1,0:T(8,128)S(1)}, f32[640,256]{1,0:T(8,128)S(1)}, u32[]{:S(2)}, u32[]{:S(2)}) collective-permute-start(f32[640,256]{1,0:T(8,128)S(1)} %pick.19.refs_0_), channel_id=1, source_target_pairs={{0,16},{16,0},{8,24},{24,8},{5,21},{21,5},{13,29},{29,13},{2,18},{... | collective-permute-start | bytes 1966088 | tf_op jit(solution)/shard_map/ppermute | solution.py:444
  88.5 5.6 %collective-permute-start.26 = (f32[640,256]{1,0:T(8,128)S(1)}, f32[640,256]{1,0:T(8,128)S(1)}, u32[]{:S(2)}, u32[]{:S(2)}) collective-permute-start(f32[640,256]{1,0:T(8,128)S(1)} %pick.17.refs_2_), channel_id=1, source_target_pairs={{0,4},{16,20},{8,12},{24,28},{5,1},{21,17},{13,9},{29,25},{2,6},{1... | collective-permute-start | bytes 1966088 | tf_op jit(solution)/shard_map/ppermute | solution.py:444
  89.9 4.7 %collective-permute-start.30 = (f32[640,256]{1,0:T(8,128)S(1)}, f32[640,256]{1,0:T(8,128)S(1)}, u32[]{:S(2)}, u32[]{:S(2)}) collective-permute-start(f32[640,256]{1,0:T(8,128)S(1)} %collective-permute-done.29.refs_6_), channel_id=1, source_target_pairs={{0,4},{16,20},{8,12},{24,28},{5,1},{21,17},{13,9},{29,25},{2,6},{1... | collective-permute-start | bytes 1966088 | tf_op jit(solution)/shard_map/ppermute | solution.py:444
  91.2 4.7 %collective-permute-start.25 = (f32[640,256]{1,0:T(8,128)S(1)}, f32[640,256]{1,0:T(8,128)S(1)}, u32[]{:S(2)}, u32[]{:S(2)}) collective-permute-start(f32[640,256]{1,0:T(8,128)S(1)} %pick.19.refs_0_), channel_id=1, source_target_pairs={{0,4},{16,20},{8,12},{24,28},{5,1},{21,17},{13,9},{29,25},{2,6},{1... | collective-permute-start | bytes 1966088 | tf_op jit(solution)/shard_map/ppermute | solution.py:444
  92.5 11.3 %collective-permute-start.28 = (f32[640,256]{1,0:T(8,128)S(1)}, f32[640,256]{1,0:T(8,128)S(1)}, u32[]{:S(2)}, u32[]{:S(2)}) collective-permute-start(f32[640,256]{1,0:T(8,128)S(1)} %collective-permute-done.27.refs_4_), channel_id=1, source_target_pairs={{0,4},{16,20},{8,12},{24,28},{5,1},{21,17},{13,9},{29,25},{2,6},{1... | collective-permute-start | bytes 1966088 | tf_op jit(solution)/shard_map/ppermute | solution.py:444

commit v2 on v1

--- a/solution.py
+++ b/solution.py
@@ -117,7 +117,7 @@
     return pl.pallas_call(
         first_kernel,
         out_shape=jax.ShapeDtypeStruct((order, order), jnp.float32),
-        in_specs=[IN_SMEM, ANYWHERE],
+        in_specs=[IN_SMEM, IN_HBM],
         out_specs=IN_VMEM,
         scratch_shapes=[
             pltpu.VMEM((order, order), jnp.float32),
@@ -155,7 +155,7 @@
     return pl.pallas_call(
         second_kernel,
         out_shape=jax.ShapeDtypeStruct((3 * order, order), jnp.float32),
-        in_specs=[IN_SMEM, IN_SMEM, ANYWHERE, IN_VMEM, IN_VMEM],
+        in_specs=[IN_SMEM, IN_SMEM, IN_HBM, IN_VMEM, IN_VMEM],
         out_specs=IN_VMEM,
         scratch_shapes=[
             pltpu.VMEM((order, order), jnp.float32),
@@ -463,16 +463,18 @@
     factoring = inverses is None
     if factoring:
         inverse0 = first_inverse(place, diag_tiles)
+        passed = move(inverse0, [((0, c), (1, c)) for c in every_col])
     packed, pivot_bases = pack(after(place, inverse0) if factoring else place, ranks, left_fac, right_fac, capacity, grid_rows)
-    chain = [packed, chain_step(packed, 1)]
     back = move(packed, [((r, 1), (r, 0)) for r in every_row])
-
+    chain = [packed]
     if factoring:
         received = [move(pivot_bases, [((1, 0), (1, c))]) for c in every_col if c]
         pivot_bases = jnp.where(col_here == 0, pivot_bases, sum(received))
-        inverse0 = move(inverse0, [((0, c), (1, c)) for c in every_col])
-        weights = second_inverse(place, ranks, diag_tiles, pivot_bases, inverse0)
-        chain[1], weights, _ = lax.optimization_barrier((chain[1], weights, early))
+        chain.append(chain_step(after(packed, passed, pivot_bases), 1))
+        weights = second_inverse(place, ranks, diag_tiles, pivot_bases, passed)
+        chain[1], weights = lax.optimization_barrier((chain[1], weights))
+    else:
+        chain.append(chain_step(packed, 1))
 
     for s in range(2, grid_cols):
         chain.append(chain_step(chain[s - 1], s))
@@ -508,11 +510,12 @@
             held = {c: held[c] + [r ^ (1 << bit) for r in held[c]] for c in every_col}
         return have
 
-    def high_hops(have):
+    def high_hops(have, *fence):
         held = {c: [r for r in range(grid_cols) if (r ^ c) % 2 == 0] for c in every_col}
         sets = [have]
         for bit in range(low_bits, row_bits):
             sets = sets + [hop(array, bit, held) for array in sets]
+        sets = [after(array, *fence) if fence else array for array in sets]
         return [[array, hop(array, 0, held)] for array in sets]
 
     first_source = source(firsts)
@@ -522,7 +525,7 @@
         inverses = [weights, to_other_parity(weights, 1)]
     rows = row_panels(place, ranks, firsts, seconds, inverses, capacity, row_slots, grid_rows)
     first_have = low_hops(first_source, rows)
-    second_sets, first_sets = high_hops(second_have), high_hops(first_have)
+    second_sets, first_sets = high_hops(second_have, early), high_hops(first_have)
     col_arrays = [sets[g] for g in range(spread) for sets in (first_sets, second_sets)]
     return schur(place, ranks, col_arrays, inverses, rows, left_fac, right_fac, capacity, grid_rows, grid_cols), inverses
 

time: 121 us -> 116 us (0.959)
  the two profiles are of different devices: /device:TPU:7 before, /device:TPU:21 now
where the time goes in v2:
time: 116 us; the launch traced here: 115 us
  waiting for transfers between devices  66.3 us (57%)
  Pallas kernels  23.1 us (20%)
  starting transfers between devices  21.5 us (19%)
  local copies, waits for them, and re-layouts  2.47 us (2%)
    ppermute x19, waiting for transfers between devices, move(): return lax.ppermute(array, AXES, flat)  66.3 us
    ppermute x19, starting transfers between devices, move(): return lax.ppermute(array, AXES, flat)  21.5 us
    pallas_call x1, Pallas kernels, schur(): pl.pallas_call(functools.partial(schur_kernel, capacity, grid_rows, grid_...  15.6 us
    pallas_call x1, Pallas kernels, pack(): pl.pallas_call(functools.partial(pack_kernel, capacity, grid_rows), out_s...  2.88 us
    pallas_call x1, Pallas kernels, row_panels(): pl.pallas_call(functools.partial(rows_kernel, capacity, grid_rows, count)...  2.71 us
    unnamed x16, local copies, waits for them, and re-layouts  2.47 us
  transfers between devices with their start and end apart: 19, of which 9 were waited for; matrix products, arithmetic and copies ran while one was open for 1% of the time, Pallas kernels for 3%

profile of v2, /device:TPU:21, one launch (start us, length us, event | category | flops | bytes accessed | tf_op | source)
XLA Modules:
  0.0 115.4 jit_solution(11648694505013363362)
XLA Ops:
  0.0 0.1 pad_add_fusion.1.place
  0.1 1.2 %copy-done = f32[4,256,256]{2,1,0:T(8,128)S(1)} copy-done((f32[4,256,256]{2,1,0:T(8,128)S(1)}, f32[4,256,256]{2,1,0:T(8,128)}, u32[]{:S(2)}) %copy-start) | copy-done | bytes 1048600
  1.3 0.6 first_inverse.1
  1.9 2.9 %pack.3 = (f32[640,256]{1,0:T(8,128)S(1)}, f32[256,256]{1,0:T(8,128)S(1)}) custom-call(s32[2]{0:T(128)S(1)} %pad_add_fusion.1.place, s32[32,32]{1,0:T(8,128)} %ranks.7, bf16[4,8,256,128]{3,2,1,0:T(8,128)(2,1)} %refs_11_.1, bf16[4,8,256,128]{3,2,1,0:T(8,128)(2,1)} %refs_12_.1), custom_call_target="tpu_custom_call" | custom-call | flops 1024 | bytes 1024 | tf_op jit(solution)/shard_map/pack/pallas_call | solution.py:205
  4.8 0.7 collective-permute-start.15
  5.4 0.7 collective-permute-start.14
  6.1 0.7 collective-permute-start.13
  6.8 0.7 collective-permute-start.12
  7.5 0.0 collective-permute-done.15
  7.5 0.0 collective-permute-done.13
  7.5 0.1 add_select_fusion.bases
  7.6 0.0 collective-permute-done.12.inverse
  7.6 1.3 %collective-permute-start.16 = (f32[640,256]{1,0:T(8,128)S(1)}, f32[640,256]{1,0:T(8,128)S(1)}, u32[]{:S(2)}, u32[]{:S(2)}) collective-permute-start(f32[640,256]{1,0:T(8,128)S(1)} %get-tuple-element.61.refs_0_.refs_1_.refs_5_), channel_id=1, source_target_pairs={{0,1},{4,5},{8,9},{12,13},{16,17},{20,21},{24,25},{28,29},{1,2},{5... | collective-permute-start | bytes 1966088 | tf_op jit(solution)/shard_map/ppermute | solution.py:444
  8.9 0.0 copy-start.1
  8.9 1.2 %copy-done.1 = f32[4,256,256]{2,1,0:T(8,128)S(1)} copy-done((f32[4,256,256]{2,1,0:T(8,128)S(1)}, f32[4,256,256]{2,1,0:T(8,128)}, u32[]{:S(2)}) %copy-start.1) | copy-done | bytes 1048600
  10.1 1.1 second_inverse.1.refs_0_
  11.3 13.8 %collective-permute-done.16.refs_1_.refs_2_.refs_6_ = f32[640,256]{1,0:T(8,128)S(1)} collective-permute-done((f32[640,256]{1,0:T(8,128)S(1)}, f32[640,256]{1,0:T(8,128)S(1)}, u32[]{:S(2)}, u32[]{:S(2)}) %collective-permute-start.16) | collective-permute-done | bytes 655392 | tf_op jit(solution)/shard_map/ppermute | solution.py:444
  25.1 1.9 %collective-permute-start.17 = (f32[640,256]{1,0:T(8,128)S(1)}, f32[640,256]{1,0:T(8,128)S(1)}, u32[]{:S(2)}, u32[]{:S(2)}) collective-permute-start(f32[640,256]{1,0:T(8,128)S(1)} %collective-permute-done.16.refs_1_.refs_2_.refs_6_), channel_id=1, source_target_pairs={{1,2},{5,6},{9,10},{13,14},{17,18},{21,22},{25,26},{29,30},{2,3},{... | collective-permute-start | bytes 1966088 | tf_op jit(solution)/shard_map/ppermute | solution.py:444
  27.0 0.7 collective-permute-start.20
  27.7 1.6 %collective-permute-start.21 = (f32[768,256]{1,0:T(8,128)S(1)}, f32[768,256]{1,0:T(8,128)}, u32[]{:S(2)}, u32[]{:S(2)}) collective-permute-start(f32[768,256]{1,0:T(8,128)S(1)} %second_inverse.1.refs_0_), channel_id=1, source_target_pairs={{4,12},{5,13},{6,14},{7,15}} | collective-permute-start | bytes 2359304 | tf_op jit(solution)/shard_map/ppermute | solution.py:444
  29.3 12.4 %collective-permute-done.17.refs_2_.refs_3_.refs_7_ = f32[640,256]{1,0:T(8,128)S(1)} collective-permute-done((f32[640,256]{1,0:T(8,128)S(1)}, f32[640,256]{1,0:T(8,128)S(1)}, u32[]{:S(2)}, u32[]{:S(2)}) %collective-permute-start.17) | collective-permute-done | bytes 655392 | tf_op jit(solution)/shard_map/ppermute | solution.py:444
  41.7 2.2 %collective-permute-start.18 = (f32[640,256]{1,0:T(8,128)S(1)}, f32[640,256]{1,0:T(8,128)S(1)}, u32[]{:S(2)}, u32[]{:S(2)}) collective-permute-start(f32[640,256]{1,0:T(8,128)S(1)} %collective-permute-done.17.refs_2_.refs_3_.refs_7_), channel_id=1, source_target_pairs={{2,3},{6,7},{10,11},{14,15},{18,19},{22,23},{26,27},{30,31}} | collective-permute-start | bytes 1966088 | tf_op jit(solution)/shard_map/ppermute | solution.py:444
  43.9 0.0 collective-permute-done.20.refs_0_.refs_4_
  44.0 0.7 collective-permute-start.23
  44.7 1.3 %collective-permute-start.22 = (f32[768,256]{1,0:T(8,128)S(1)}, f32[768,256]{1,0:T(8,128)S(1)}, u32[]{:S(2)}, u32[]{:S(2)}) collective-permute-start(f32[768,256]{1,0:T(8,128)S(1)} %pick.15.refs_0_), channel_id=1, source_target_pairs={{4,20},{5,21},{6,22},{7,23},{12,28},{13,29},{14,30},{15,31}} | collective-permute-start | bytes 2359304 | tf_op jit(solution)/shard_map/ppermute | solution.py:444
  46.0 9.7 %collective-permute-done.18.refs_3_ = f32[640,256]{1,0:T(8,128)S(1)} collective-permute-done((f32[640,256]{1,0:T(8,128)S(1)}, f32[640,256]{1,0:T(8,128)S(1)}, u32[]{:S(2)}, u32[]{:S(2)}) %collective-permute-start.18) | collective-permute-done | bytes 655392 | tf_op jit(solution)/shard_map/ppermute | solution.py:444
  55.8 0.0 copy-start.11
  55.8 12.2 %collective-permute-done.22.refs_1_ = f32[768,256]{1,0:T(8,128)S(1)} collective-permute-done((f32[768,256]{1,0:T(8,128)S(1)}, f32[768,256]{1,0:T(8,128)S(1)}, u32[]{:S(2)}, u32[]{:S(2)}) %collective-permute-start.22) | collective-permute-done | bytes 786464 | tf_op jit(solution)/shard_map/ppermute | solution.py:444
  67.9 0.1 pick.18.refs_8_
  68.0 1.3 %collective-permute-start.24 = (f32[768,256]{1,0:T(8,128)S(1)}, f32[768,256]{1,0:T(8,128)S(1)}, u32[]{:S(2)}, u32[]{:S(2)}) collective-permute-start(f32[768,256]{1,0:T(8,128)S(1)} %pick.18.refs_8_), channel_id=1, source_target_pairs={{4,0},{5,1},{6,2},{7,3},{12,8},{13,9},{14,10},{15,11},{20,16},{21,... | collective-permute-start | bytes 2359304 | tf_op jit(solution)/shard_map/ppermute | solution.py:444
  69.4 0.7 collective-permute-start.19
  70.1 0.7 collective-permute-start.29
  70.8 0.4 collective-permute-done.24.refs_9_
  71.2 2.7 %row_panels.3.refs_10_ = bf16[4,256,1536]{2,1,0:T(8,128)(2,1)S(1)} custom-call(s32[2]{0:T(128)S(1)} %pad_add_fusion.1.place, s32[32,32]{1,0:T(8,128)S(1)} %copy-done.11, f32[640,256]{1,0:T(8,128)S(1)} %get-tuple-element.61.refs_0_.refs_1_.refs_5_, f32[640,256]{1,0:T(8,128)S(1)} %collective-permute-done.16.refs_1_.refs_2_.refs_6_, ...), custom_call_target="tpu_custom_call" | custom-call | flops 1024 | bytes 1024 | tf_op jit(solution)/shard_map/row_panels/pallas_call | solution.py:282
  73.9 0.0 copy-start.2
  74.0 0.0 copy-start.5
  74.0 0.8 collective-permute-start.27
  74.9 0.7 fusion
  75.6 1.4 %collective-permute-start.26 = (f32[640,256]{1,0:T(8,128)S(1)}, f32[640,256]{1,0:T(8,128)S(1)}, u32[]{:S(2)}, u32[]{:S(2)}) collective-permute-start(f32[640,256]{1,0:T(8,128)S(1)} %pick.17.refs_2_), channel_id=1, source_target_pairs={{0,4},{16,20},{8,12},{24,28},{5,1},{21,17},{13,9},{29,25},{2,6},{1... | collective-permute-start | bytes 1966088 | tf_op jit(solution)/shard_map/ppermute | solution.py:444
  77.0 1.3 %collective-permute-start.30 = (f32[640,256]{1,0:T(8,128)S(1)}, f32[640,256]{1,0:T(8,128)S(1)}, u32[]{:S(2)}, u32[]{:S(2)}) collective-permute-start(f32[640,256]{1,0:T(8,128)S(1)} %collective-permute-done.29.refs_6_), channel_id=1, source_target_pairs={{0,4},{16,20},{8,12},{24,28},{5,1},{21,17},{13,9},{29,25},{2,6},{1... | collective-permute-start | bytes 1966088 | tf_op jit(solution)/shard_map/ppermute | solution.py:444
  78.3 1.3 %collective-permute-start.25 = (f32[640,256]{1,0:T(8,128)S(1)}, f32[640,256]{1,0:T(8,128)S(1)}, u32[]{:S(2)}, u32[]{:S(2)}) collective-permute-start(f32[640,256]{1,0:T(8,128)S(1)} %pick.19.refs_0_), channel_id=1, source_target_pairs={{0,4},{16,20},{8,12},{24,28},{5,1},{21,17},{13,9},{29,25},{2,6},{1... | collective-permute-start | bytes 1966088 | tf_op jit(solution)/shard_map/ppermute | solution.py:444
  79.6 1.5 %collective-permute-start.28 = (f32[640,256]{1,0:T(8,128)S(1)}, f32[640,256]{1,0:T(8,128)S(1)}, u32[]{:S(2)}, u32[]{:S(2)}) collective-permute-start(f32[640,256]{1,0:T(8,128)S(1)} %collective-permute-done.27.refs_4_), channel_id=1, source_target_pairs={{0,4},{16,20},{8,12},{24,28},{5,1},{21,17},{13,9},{29,25},{2,6},{1... | collective-permute-start | bytes 1966088 | tf_op jit(solution)/shard_map/ppermute | solution.py:444
  81.1 10.1 %collective-permute-done.26.refs_3_ = f32[640,256]{1,0:T(8,128)S(1)} collective-permute-done((f32[640,256]{1,0:T(8,128)S(1)}, f32[640,256]{1,0:T(8,128)S(1)}, u32[]{:S(2)}, u32[]{:S(2)}) %collective-permute-start.26) | collective-permute-done | bytes 655392 | tf_op jit(solution)/shard_map/ppermute | solution.py:444
  91.3 1.3 %collective-permute-done.30.refs_7_ = f32[640,256]{1,0:T(8,128)S(1)} collective-permute-done((f32[640,256]{1,0:T(8,128)S(1)}, f32[640,256]{1,0:T(8,128)S(1)}, u32[]{:S(2)}, u32[]{:S(2)}) %collective-permute-start.30) | collective-permute-done | bytes 655392 | tf_op jit(solution)/shard_map/ppermute | solution.py:444
  92.6 1.3 %collective-permute-done.25.refs_1_ = f32[640,256]{1,0:T(8,128)S(1)} collective-permute-done((f32[640,256]{1,0:T(8,128)S(1)}, f32[640,256]{1,0:T(8,128)S(1)}, u32[]{:S(2)}, u32[]{:S(2)}) %collective-permute-start.25) | collective-permute-done | bytes 655392 | tf_op jit(solution)/shard_map/ppermute | solution.py:444
  93.9 5.0 %collective-permute-done.28.refs_5_ = f32[640,256]{1,0:T(8,128)S(1)} collective-permute-done((f32[640,256]{1,0:T(8,128)S(1)}, f32[640,256]{1,0:T(8,128)S(1)}, u32[]{:S(2)}, u32[]{:S(2)}) %collective-permute-start.28) | collective-permute-done | bytes 655392 | tf_op jit(solution)/shard_map/ppermute | solution.py:444
  99.0 15.6 %schur.3 = f32[4,8,256,256]{3,2,1,0:T(8,128)} custom-call(s32[2]{0:T(128)S(1)} %pad_add_fusion.1.place, s32[32,32]{1,0:T(8,128)S(1)} %copy-done.11, f32[640,256]{1,0:T(8,128)S(1)} %pick.19.refs_0_, f32[640,256]{1,0:T(8,128)S(1)} %collective-permute-done.25.refs_1_, f32[640,256]{1,0:T(8,128)S(1)} %pick.17.refs_2_, ...), custom_call_target="tpu_custom_call" | custom-call | flops 8589934592 | bytes 16777216 | tf_op jit(solution)/shard_map/schur/pallas_call | solution.py:402
  114.6 0.7 while.9
  (22 shorter events, 0.2 us)
Async XLA Ops:
  0.1 1.2 %copy-start = (f32[4,256,256]{2,1,0:T(8,128)S(1)}, f32[4,256,256]{2,1,0:T(8,128)}, u32[]{:S(2)}) copy-start(f32[4,256,256]{2,1,0:T(8,128)} %tiles.3) | copy-start | bytes 3145732
  4.8 2.7 %collective-permute-start.15 = (f32[256,256]{1,0:T(8,128)S(1)}, f32[256,256]{1,0:T(8,128)S(1)}, u32[]{:S(2)}, u32[]{:S(2)}) collective-permute-start(f32[256,256]{1,0:T(8,128)S(1)} %get-tuple-element.60), channel_id=1, source_target_pairs={{4,7}} | collective-permute-start | bytes 786440 | tf_op jit(solution)/shard_map/ppermute | solution.py:444
  5.4 2.1 %collective-permute-start.14 = (f32[256,256]{1,0:T(8,128)S(1)}, f32[256,256]{1,0:T(8,128)S(1)}, u32[]{:S(2)}, u32[]{:S(2)}) collective-permute-start(f32[256,256]{1,0:T(8,128)S(1)} %get-tuple-element.60), channel_id=1, source_target_pairs={{4,6}} | collective-permute-start | bytes 786440 | tf_op jit(solution)/shard_map/ppermute | solution.py:444
  6.1 1.4 %collective-permute-start.13 = (f32[256,256]{1,0:T(8,128)S(1)}, f32[256,256]{1,0:T(8,128)S(1)}, u32[]{:S(2)}, u32[]{:S(2)}) collective-permute-start(f32[256,256]{1,0:T(8,128)S(1)} %get-tuple-element.60), channel_id=1, source_target_pairs={{4,5}} | collective-permute-start | bytes 786440 | tf_op jit(solution)/shard_map/ppermute | solution.py:444
  6.8 0.8 collective-permute-start.12
  7.6 17.5 %collective-permute-start.16 = (f32[640,256]{1,0:T(8,128)S(1)}, f32[640,256]{1,0:T(8,128)S(1)}, u32[]{:S(2)}, u32[]{:S(2)}) collective-permute-start(f32[640,256]{1,0:T(8,128)S(1)} %get-tuple-element.61.refs_0_.refs_1_.refs_5_), channel_id=1, source_target_pairs={{0,1},{4,5},{8,9},{12,13},{16,17},{20,21},{24,25},{28,29},{1,2},{5... | collective-permute-start | bytes 1966088 | tf_op jit(solution)/shard_map/ppermute | solution.py:444
  8.9 1.2 %copy-start.1 = (f32[4,256,256]{2,1,0:T(8,128)S(1)}, f32[4,256,256]{2,1,0:T(8,128)}, u32[]{:S(2)}) copy-start(f32[4,256,256]{2,1,0:T(8,128)} %tiles.3) | copy-start | bytes 3145732
  25.1 16.6 %collective-permute-start.17 = (f32[640,256]{1,0:T(8,128)S(1)}, f32[640,256]{1,0:T(8,128)S(1)}, u32[]{:S(2)}, u32[]{:S(2)}) collective-permute-start(f32[640,256]{1,0:T(8,128)S(1)} %collective-permute-done.16.refs_1_.refs_2_.refs_6_), channel_id=1, source_target_pairs={{1,2},{5,6},{9,10},{13,14},{17,18},{21,22},{25,26},{29,30},{2,3},{... | collective-permute-start | bytes 1966088 | tf_op jit(solution)/shard_map/ppermute | solution.py:444
  27.0 16.9 %collective-permute-start.20 = (f32[640,256]{1,0:T(8,128)S(1)}, f32[640,256]{1,0:T(8,128)S(1)}, u32[]{:S(2)}, u32[]{:S(2)}) collective-permute-start(f32[640,256]{1,0:T(8,128)S(1)} %get-tuple-element.61.refs_0_.refs_1_.refs_5_), channel_id=1, source_target_pairs={{1,0},{5,4},{9,8},{13,12},{17,16},{21,20},{25,24},{29,28}} | collective-permute-start | bytes 1966088 | tf_op jit(solution)/shard_map/ppermute | solution.py:444
  27.7 16.9 %collective-permute-start.21 = (f32[768,256]{1,0:T(8,128)S(1)}, f32[768,256]{1,0:T(8,128)}, u32[]{:S(2)}, u32[]{:S(2)}) collective-permute-start(f32[768,256]{1,0:T(8,128)S(1)} %second_inverse.1.refs_0_), channel_id=1, source_target_pairs={{4,12},{5,13},{6,14},{7,15}} | collective-permute-start | bytes 2359304 | tf_op jit(solution)/shard_map/ppermute | solution.py:444
  41.7 14.0 %collective-permute-start.18 = (f32[640,256]{1,0:T(8,128)S(1)}, f32[640,256]{1,0:T(8,128)S(1)}, u32[]{:S(2)}, u32[]{:S(2)}) collective-permute-start(f32[640,256]{1,0:T(8,128)S(1)} %collective-permute-done.17.refs_2_.refs_3_.refs_7_), channel_id=1, source_target_pairs={{2,3},{6,7},{10,11},{14,15},{18,19},{22,23},{26,27},{30,31}} | collective-permute-start | bytes 1966088 | tf_op jit(solution)/shard_map/ppermute | solution.py:444
  44.0 11.7 %collective-permute-start.23 = (f32[640,256]{1,0:T(8,128)S(1)}, f32[640,256]{1,0:T(8,128)S(1)}, u32[]{:S(2)}, u32[]{:S(2)}) collective-permute-start(f32[640,256]{1,0:T(8,128)S(1)} %pick.16.refs_0_), channel_id=1, source_target_pairs={{0,8},{16,24},{5,13},{21,29},{10,2},{26,18},{15,7},{31,23}} | collective-permute-start | bytes 1966088 | tf_op jit(solution)/shard_map/ppermute | solution.py:444
  44.7 23.2 %collective-permute-start.22 = (f32[768,256]{1,0:T(8,128)S(1)}, f32[768,256]{1,0:T(8,128)S(1)}, u32[]{:S(2)}, u32[]{:S(2)}) collective-permute-start(f32[768,256]{1,0:T(8,128)S(1)} %pick.15.refs_0_), channel_id=1, source_target_pairs={{4,20},{5,21},{6,22},{7,23},{12,28},{13,29},{14,30},{15,31}} | collective-permute-start | bytes 2359304 | tf_op jit(solution)/shard_map/ppermute | solution.py:444
  55.8 15.5 %copy-start.11 = (s32[32,32]{1,0:T(8,128)S(1)}, s32[32,32]{1,0:T(8,128)}, u32[]{:S(2)}) copy-start(s32[32,32]{1,0:T(8,128)} %ranks.7) | copy-start | bytes 12292
  68.0 30.9 %copy-start.7 = (f32[768,256]{1,0:T(8,128)}, f32[768,256]{1,0:T(8,128)S(1)}, u32[]{:S(2)}) copy-start(f32[768,256]{1,0:T(8,128)S(1)} %pick.18.refs_8_) | copy-start | bytes 2359300
  68.0 3.2 %collective-permute-start.24 = (f32[768,256]{1,0:T(8,128)S(1)}, f32[768,256]{1,0:T(8,128)S(1)}, u32[]{:S(2)}, u32[]{:S(2)}) collective-permute-start(f32[768,256]{1,0:T(8,128)S(1)} %pick.18.refs_8_), channel_id=1, source_target_pairs={{4,0},{5,1},{6,2},{7,3},{12,8},{13,9},{14,10},{15,11},{20,16},{21,... | collective-permute-start | bytes 2359304 | tf_op jit(solution)/shard_map/ppermute | solution.py:444
  69.4 4.6 %collective-permute-start.19 = (f32[640,256]{1,0:T(8,128)S(1)}, f32[640,256]{1,0:T(8,128)S(1)}, u32[]{:S(2)}, u32[]{:S(2)}) collective-permute-start(f32[640,256]{1,0:T(8,128)S(1)} %pick.14.refs_0_), channel_id=1, source_target_pairs={{0,8},{16,24},{5,13},{21,29},{10,2},{26,18},{15,7},{31,23}} | collective-permute-start | bytes 1966088 | tf_op jit(solution)/shard_map/ppermute | solution.py:444
  70.1 6.9 %collective-permute-start.29 = (f32[640,256]{1,0:T(8,128)S(1)}, f32[640,256]{1,0:T(8,128)S(1)}, u32[]{:S(2)}, u32[]{:S(2)}) collective-permute-start(f32[640,256]{1,0:T(8,128)S(1)} %pick.17.refs_2_), channel_id=1, source_target_pairs={{0,16},{16,0},{8,24},{24,8},{5,21},{21,5},{13,29},{29,13},{2,18},{... | collective-permute-start | bytes 1966088 | tf_op jit(solution)/shard_map/ppermute | solution.py:444
  71.2 27.7 %copy-start.9 = (f32[768,256]{1,0:T(8,128)}, f32[768,256]{1,0:T(8,128)S(1)}, u32[]{:S(2)}) copy-start(f32[768,256]{1,0:T(8,128)S(1)} %collective-permute-done.24.refs_9_) | copy-start | bytes 2359300
  73.9 25.0 %copy-start.2 = (bf16[4,8,256,128]{3,2,1,0:T(8,128)(2,1)S(1)}, bf16[4,8,256,128]{3,2,1,0:T(8,128)(2,1)}, u32[]{:S(2)}) copy-start(bf16[4,8,256,128]{3,2,1,0:T(8,128)(2,1)} %refs_11_.1) | copy-start | bytes 6291460
  74.0 25.0 %copy-start.5 = (bf16[4,8,256,128]{3,2,1,0:T(8,128)(2,1)S(1)}, bf16[4,8,256,128]{3,2,1,0:T(8,128)(2,1)}, u32[]{:S(2)}) copy-start(bf16[4,8,256,128]{3,2,1,0:T(8,128)(2,1)} %refs_12_.1) | copy-start | bytes 6291460
  74.0 5.6 %collective-permute-start.27 = (f32[640,256]{1,0:T(8,128)S(1)}, f32[640,256]{1,0:T(8,128)S(1)}, u32[]{:S(2)}, u32[]{:S(2)}) collective-permute-start(f32[640,256]{1,0:T(8,128)S(1)} %pick.19.refs_0_), channel_id=1, source_target_pairs={{0,16},{16,0},{8,24},{24,8},{5,21},{21,5},{13,29},{29,13},{2,18},{... | collective-permute-start | bytes 1966088 | tf_op jit(solution)/shard_map/ppermute | solution.py:444
  75.6 39.0 %copy-start.3 = (bf16[4,8,256,128]{3,2,1,0:T(8,128)(2,1)S(1)}, bf16[4,8,256,128]{3,2,1,0:T(8,128)(2,1)}, u32[]{:S(2)}) copy-start(bf16[4,8,256,128]{3,2,1,0:T(8,128)(2,1)} %refs_11_.1) | copy-start | bytes 6291460
  75.6 15.7 %collective-permute-start.26 = (f32[640,256]{1,0:T(8,128)S(1)}, f32[640,256]{1,0:T(8,128)S(1)}, u32[]{:S(2)}, u32[]{:S(2)}) collective-permute-start(f32[640,256]{1,0:T(8,128)S(1)} %pick.17.refs_2_), channel_id=1, source_target_pairs={{0,4},{16,20},{8,12},{24,28},{5,1},{21,17},{13,9},{29,25},{2,6},{1... | collective-permute-start | bytes 1966088 | tf_op jit(solution)/shard_map/ppermute | solution.py:444
  77.0 15.6 %collective-permute-start.30 = (f32[640,256]{1,0:T(8,128)S(1)}, f32[640,256]{1,0:T(8,128)S(1)}, u32[]{:S(2)}, u32[]{:S(2)}) collective-permute-start(f32[640,256]{1,0:T(8,128)S(1)} %collective-permute-done.29.refs_6_), channel_id=1, source_target_pairs={{0,4},{16,20},{8,12},{24,28},{5,1},{21,17},{13,9},{29,25},{2,6},{1... | collective-permute-start | bytes 1966088 | tf_op jit(solution)/shard_map/ppermute | solution.py:444
  78.3 15.6 %collective-permute-start.25 = (f32[640,256]{1,0:T(8,128)S(1)}, f32[640,256]{1,0:T(8,128)S(1)}, u32[]{:S(2)}, u32[]{:S(2)}) collective-permute-start(f32[640,256]{1,0:T(8,128)S(1)} %pick.19.refs_0_), channel_id=1, source_target_pairs={{0,4},{16,20},{8,12},{24,28},{5,1},{21,17},{13,9},{29,25},{2,6},{1... | collective-permute-start | bytes 1966088 | tf_op jit(solution)/shard_map/ppermute | solution.py:444
  79.6 19.4 %collective-permute-start.28 = (f32[640,256]{1,0:T(8,128)S(1)}, f32[640,256]{1,0:T(8,128)S(1)}, u32[]{:S(2)}, u32[]{:S(2)}) collective-permute-start(f32[640,256]{1,0:T(8,128)S(1)} %collective-permute-done.27.refs_4_), channel_id=1, source_target_pairs={{0,4},{16,20},{8,12},{24,28},{5,1},{21,17},{13,9},{29,25},{2,6},{1... | collective-permute-start | bytes 1966088 | tf_op jit(solution)/shard_map/ppermute | solution.py:444

commit v3 on v2

--- a/solution.py
+++ b/solution.py
@@ -125,7 +125,7 @@
             pltpu.SemaphoreType.DMA,
         ],
         compiler_params=params(8),
-        cost_estimate=cost(2**10, 2**10),
+        cost_estimate=cost(2**33, 2**20),
         name="first_inverse",
     )(place, tiles)
 
@@ -464,13 +464,13 @@
     if factoring:
         inverse0 = first_inverse(place, diag_tiles)
         passed = move(inverse0, [((0, c), (1, c)) for c in every_col])
-    packed, pivot_bases = pack(after(place, inverse0) if factoring else place, ranks, left_fac, right_fac, capacity, grid_rows)
+    packed, pivot_bases = pack(place, ranks, left_fac, right_fac, capacity, grid_rows)
     back = move(packed, [((r, 1), (r, 0)) for r in every_row])
     chain = [packed]
     if factoring:
         received = [move(pivot_bases, [((1, 0), (1, c))]) for c in every_col if c]
         pivot_bases = jnp.where(col_here == 0, pivot_bases, sum(received))
-        chain.append(chain_step(after(packed, passed, pivot_bases), 1))
+        chain.append(chain_step(packed, 1))
         weights = second_inverse(place, ranks, diag_tiles, pivot_bases, passed)
         chain[1], weights = lax.optimization_barrier((chain[1], weights))
     else:

time: 116 us -> 108 us (0.931)
  the two profiles are of different devices: /device:TPU:21 before, /device:TPU:15 now
where the time goes in v3:
time: 108 us; the launch traced here: 107 us
  waiting for transfers between devices  50.4 us (47%)
  starting transfers between devices  29.5 us (27%)
  Pallas kernels  23.1 us (21%)
  other arithmetic  1.78 us (2%)
  local copies, waits for them, and re-layouts  1.25 us (1%)
    ppermute x19, waiting for transfers between devices, move(): return lax.ppermute(array, AXES, flat)  50.4 us
    ppermute x19, starting transfers between devices, move(): return lax.ppermute(array, AXES, flat)  29.5 us
    pallas_call x1, Pallas kernels, schur(): pl.pallas_call(functools.partial(schur_kernel, capacity, grid_rows, grid_...  15.4 us
    pallas_call x1, Pallas kernels, pack(): pl.pallas_call(functools.partial(pack_kernel, capacity, grid_rows), out_s...  2.88 us
    pallas_call x1, Pallas kernels, row_panels(): pl.pallas_call(functools.partial(rows_kernel, capacity, grid_rows, count)...  2.7 us
  transfers between devices with their start and end apart: 19, of which 8 were waited for; matrix products, arithmetic and copies ran while one was open for 2% of the time, Pallas kernels for 4%

profile of v3, /device:TPU:15, one launch (start us, length us, event | category | flops | bytes accessed | tf_op | source)
XLA Modules:
  0.0 107.1 jit_solution(10254868872014574516)
XLA Ops:
  0.0 0.1 pad_add_fusion.1.place
  0.1 2.9 %pack.3 = (f32[640,256]{1,0:T(8,128)S(1)}, f32[256,256]{1,0:T(8,128)S(1)}) custom-call(s32[2]{0:T(128)S(1)} %pad_add_fusion.1.place, s32[32,32]{1,0:T(8,128)} %ranks.7, bf16[4,8,256,128]{3,2,1,0:T(8,128)(2,1)} %refs_11_.1, bf16[4,8,256,128]{3,2,1,0:T(8,128)(2,1)} %refs_12_.1), custom_call_target="tpu_custom_call" | custom-call | flops 1024 | bytes 1024 | tf_op jit(solution)/shard_map/pack/pallas_call | solution.py:205
  3.0 0.7 collective-permute-start.15
  3.6 1.4 %collective-permute-start.14 = (f32[256,256]{1,0:T(8,128)S(1)}, f32[256,256]{1,0:T(8,128)}, u32[]{:S(2)}, u32[]{:S(2)}) collective-permute-start(f32[256,256]{1,0:T(8,128)S(1)} %get-tuple-element.57), channel_id=1, source_target_pairs={{4,6}} | collective-permute-start | bytes 786440 | tf_op jit(solution)/shard_map/ppermute | solution.py:444
  5.0 1.3 %collective-permute-start.13 = (f32[256,256]{1,0:T(8,128)S(1)}, f32[256,256]{1,0:T(8,128)}, u32[]{:S(2)}, u32[]{:S(2)}) collective-permute-start(f32[256,256]{1,0:T(8,128)S(1)} %get-tuple-element.57), channel_id=1, source_target_pairs={{4,5}} | collective-permute-start | bytes 786440 | tf_op jit(solution)/shard_map/ppermute | solution.py:444
  6.4 3.2 %collective-permute-start.12 = (f32[640,256]{1,0:T(8,128)S(1)}, f32[640,256]{1,0:T(8,128)S(1)}, u32[]{:S(2)}, u32[]{:S(2)}) collective-permute-start(f32[640,256]{1,0:T(8,128)S(1)} %get-tuple-element.56.refs_0_.refs_1_.refs_5_), channel_id=1, source_target_pairs={{0,1},{4,5},{8,9},{12,13},{16,17},{20,21},{24,25},{28,29},{1,2},{5... | collective-permute-start | bytes 1966088 | tf_op jit(solution)/shard_map/ppermute | solution.py:444
  9.6 0.0 copy-start
  9.6 1.2 %copy-done = f32[4,256,256]{2,1,0:T(8,128)S(1)} copy-done((f32[4,256,256]{2,1,0:T(8,128)S(1)}, f32[4,256,256]{2,1,0:T(8,128)}, u32[]{:S(2)}) %copy-start) | copy-done | bytes 1048600
  10.8 0.6 first_inverse.1
  11.4 0.7 collective-permute-start.16
  12.0 0.0 collective-permute-done.15
  12.1 0.0 collective-permute-done.14
  12.1 1.1 %add_select_fusion.bases = f32[256,256]{1,0:T(8,128)S(1)} fusion(f32[256,256]{1,0:T(8,128)S(1)} %get-tuple-element.57, f32[256,256]{1,0:T(8,128)S(1)} %collective-permute-done.15, f32[256,256]{1,0:T(8,128)} %collective-permute-done.13, f32[256,256]{1,0:T(8,128)} %collective-permute-done.14, pred[]{:T(512)S(6)} %eq.62), kind=kLoop, calls=%fused_computation.1 | loop fusion | flops 196608 | bytes 1310721 | tf_op jit(solution)/shard_map/jit(_where)/select_n | solution.py:472
  13.2 1.0 second_inverse.1.refs_0_
  14.2 9.6 %collective-permute-done.12.refs_1_.refs_2_.refs_6_ = f32[640,256]{1,0:T(8,128)S(1)} collective-permute-done((f32[640,256]{1,0:T(8,128)S(1)}, f32[640,256]{1,0:T(8,128)S(1)}, u32[]{:S(2)}, u32[]{:S(2)}) %collective-permute-start.12) | collective-permute-done | bytes 655392 | tf_op jit(solution)/shard_map/ppermute | solution.py:444
  23.8 3.2 %collective-permute-start.17 = (f32[640,256]{1,0:T(8,128)S(1)}, f32[640,256]{1,0:T(8,128)S(1)}, u32[]{:S(2)}, u32[]{:S(2)}) collective-permute-start(f32[640,256]{1,0:T(8,128)S(1)} %collective-permute-done.12.refs_1_.refs_2_.refs_6_), channel_id=1, source_target_pairs={{1,2},{5,6},{9,10},{13,14},{17,18},{21,22},{25,26},{29,30},{2,3},{... | collective-permute-start | bytes 1966088 | tf_op jit(solution)/shard_map/ppermute | solution.py:444
  27.1 2.2 %collective-permute-start.20 = (f32[640,256]{1,0:T(8,128)S(1)}, f32[640,256]{1,0:T(8,128)}, u32[]{:S(2)}, u32[]{:S(2)}) collective-permute-start(f32[640,256]{1,0:T(8,128)S(1)} %get-tuple-element.56.refs_0_.refs_1_.refs_5_), channel_id=1, source_target_pairs={{1,0},{5,4},{9,8},{13,12},{17,16},{21,20},{25,24},{29,28}} | collective-permute-start | bytes 1966088 | tf_op jit(solution)/shard_map/ppermute | solution.py:444
  29.2 1.6 %collective-permute-start.21 = (f32[768,256]{1,0:T(8,128)S(1)}, f32[768,256]{1,0:T(8,128)}, u32[]{:S(2)}, u32[]{:S(2)}) collective-permute-start(f32[768,256]{1,0:T(8,128)S(1)} %second_inverse.1.refs_0_), channel_id=1, source_target_pairs={{4,12},{5,13},{6,14},{7,15}} | collective-permute-start | bytes 2359304 | tf_op jit(solution)/shard_map/ppermute | solution.py:444
  30.8 8.7 %collective-permute-done.17.refs_2_.refs_3_.refs_7_ = f32[640,256]{1,0:T(8,128)S(1)} collective-permute-done((f32[640,256]{1,0:T(8,128)S(1)}, f32[640,256]{1,0:T(8,128)S(1)}, u32[]{:S(2)}, u32[]{:S(2)}) %collective-permute-start.17) | collective-permute-done | bytes 655392 | tf_op jit(solution)/shard_map/ppermute | solution.py:444
  39.5 0.7 collective-permute-start.18
  40.2 0.6 collective-permute-done.20.refs_0_.refs_4_
  40.8 1.3 %collective-permute-start.23 = (f32[640,256]{1,0:T(8,128)S(1)}, f32[640,256]{1,0:T(8,128)S(1)}, u32[]{:S(2)}, u32[]{:S(2)}) collective-permute-start(f32[640,256]{1,0:T(8,128)S(1)} %pick.16.refs_0_), channel_id=1, source_target_pairs={{0,8},{16,24},{5,13},{21,29},{10,2},{26,18},{15,7},{31,23}} | collective-permute-start | bytes 1966088 | tf_op jit(solution)/shard_map/ppermute | solution.py:444
  42.2 1.3 %collective-permute-start.22 = (f32[768,256]{1,0:T(8,128)S(1)}, f32[768,256]{1,0:T(8,128)S(1)}, u32[]{:S(2)}, u32[]{:S(2)}) collective-permute-start(f32[768,256]{1,0:T(8,128)S(1)} %pick.15.refs_0_), channel_id=1, source_target_pairs={{4,20},{5,21},{6,22},{7,23},{12,28},{13,29},{14,30},{15,31}} | collective-permute-start | bytes 2359304 | tf_op jit(solution)/shard_map/ppermute | solution.py:444
  43.5 0.0 collective-permute-done.18.refs_3_
  43.5 8.6 %collective-permute-done.23.refs_1_ = f32[640,256]{1,0:T(8,128)S(1)} collective-permute-done((f32[640,256]{1,0:T(8,128)S(1)}, f32[640,256]{1,0:T(8,128)S(1)}, u32[]{:S(2)}, u32[]{:S(2)}) %collective-permute-start.23) | collective-permute-done | bytes 655392 | tf_op jit(solution)/shard_map/ppermute | solution.py:444
  52.2 0.2 pick.17.refs_2_
  52.4 11.3 %collective-permute-done.22.refs_1_ = f32[768,256]{1,0:T(8,128)S(1)} collective-permute-done((f32[768,256]{1,0:T(8,128)S(1)}, f32[768,256]{1,0:T(8,128)S(1)}, u32[]{:S(2)}, u32[]{:S(2)}) %collective-permute-start.22) | collective-permute-done | bytes 786464 | tf_op jit(solution)/shard_map/ppermute | solution.py:444
  63.7 0.1 pick.18.refs_8_
  63.8 1.3 %collective-permute-start.24 = (f32[768,256]{1,0:T(8,128)S(1)}, f32[768,256]{1,0:T(8,128)S(1)}, u32[]{:S(2)}, u32[]{:S(2)}) collective-permute-start(f32[768,256]{1,0:T(8,128)S(1)} %pick.18.refs_8_), channel_id=1, source_target_pairs={{4,0},{5,1},{6,2},{7,3},{12,8},{13,9},{14,10},{15,11},{20,16},{21,... | collective-permute-start | bytes 2359304 | tf_op jit(solution)/shard_map/ppermute | solution.py:444
  65.1 1.3 %collective-permute-start.19 = (f32[640,256]{1,0:T(8,128)S(1)}, f32[640,256]{1,0:T(8,128)S(1)}, u32[]{:S(2)}, u32[]{:S(2)}) collective-permute-start(f32[640,256]{1,0:T(8,128)S(1)} %pick.14.refs_0_), channel_id=1, source_target_pairs={{0,8},{16,24},{5,13},{21,29},{10,2},{26,18},{15,7},{31,23}} | collective-permute-start | bytes 1966088 | tf_op jit(solution)/shard_map/ppermute | solution.py:444
  66.4 1.9 %collective-permute-start.29 = (f32[640,256]{1,0:T(8,128)S(1)}, f32[640,256]{1,0:T(8,128)S(1)}, u32[]{:S(2)}, u32[]{:S(2)}) collective-permute-start(f32[640,256]{1,0:T(8,128)S(1)} %pick.17.refs_2_), channel_id=1, source_target_pairs={{0,16},{16,0},{8,24},{24,8},{5,21},{21,5},{13,29},{29,13},{2,18},{... | collective-permute-start | bytes 1966088 | tf_op jit(solution)/shard_map/ppermute | solution.py:444
  68.4 0.0 collective-permute-done.24.refs_9_
  68.4 2.7 %row_panels.3.refs_10_ = bf16[4,256,1536]{2,1,0:T(8,128)(2,1)S(1)} custom-call(s32[2]{0:T(128)S(1)} %pad_add_fusion.1.place, s32[32,32]{1,0:T(8,128)S(1)} %copy-done.10, f32[640,256]{1,0:T(8,128)S(1)} %get-tuple-element.56.refs_0_.refs_1_.refs_5_, f32[640,256]{1,0:T(8,128)S(1)} %collective-permute-done.12.refs_1_.refs_2_.refs_6_, ...), custom_call_target="tpu_custom_call" | custom-call | flops 1024 | bytes 1024 | tf_op jit(solution)/shard_map/row_panels/pallas_call | solution.py:282
  71.1 0.0 copy-start.2
  71.1 0.0 copy-start.4
  71.1 5.3 %collective-permute-done.19.refs_1_ = f32[640,256]{1,0:T(8,128)S(1)} collective-permute-done((f32[640,256]{1,0:T(8,128)S(1)}, f32[640,256]{1,0:T(8,128)S(1)}, u32[]{:S(2)}, u32[]{:S(2)}) %collective-permute-start.19) | collective-permute-done | bytes 655392 | tf_op jit(solution)/shard_map/ppermute | solution.py:444
  76.5 0.2 pick.19.refs_0_
  76.7 1.9 %collective-permute-start.27 = (f32[640,256]{1,0:T(8,128)S(1)}, f32[640,256]{1,0:T(8,128)S(1)}, u32[]{:S(2)}, u32[]{:S(2)}) collective-permute-start(f32[640,256]{1,0:T(8,128)S(1)} %pick.19.refs_0_), channel_id=1, source_target_pairs={{0,16},{16,0},{8,24},{24,8},{5,21},{21,5},{13,29},{29,13},{2,18},{... | collective-permute-start | bytes 1966088 | tf_op jit(solution)/shard_map/ppermute | solution.py:444
  78.6 0.6 fusion
  79.2 1.3 %collective-permute-start.26 = (f32[640,256]{1,0:T(8,128)S(1)}, f32[640,256]{1,0:T(8,128)S(1)}, u32[]{:S(2)}, u32[]{:S(2)}) collective-permute-start(f32[640,256]{1,0:T(8,128)S(1)} %pick.17.refs_2_), channel_id=1, source_target_pairs={{0,4},{16,20},{8,12},{24,28},{5,1},{21,17},{13,9},{29,25},{2,6},{1... | collective-permute-start | bytes 1966088 | tf_op jit(solution)/shard_map/ppermute | solution.py:444
  80.6 0.0 collective-permute-done.29.refs_6_
  80.6 1.3 %collective-permute-start.30 = (f32[640,256]{1,0:T(8,128)S(1)}, f32[640,256]{1,0:T(8,128)S(1)}, u32[]{:S(2)}, u32[]{:S(2)}) collective-permute-start(f32[640,256]{1,0:T(8,128)S(1)} %collective-permute-done.29.refs_6_), channel_id=1, source_target_pairs={{0,4},{16,20},{8,12},{24,28},{5,1},{21,17},{13,9},{29,25},{2,6},{1... | collective-permute-start | bytes 1966088 | tf_op jit(solution)/shard_map/ppermute | solution.py:444
  81.9 1.3 %collective-permute-start.25 = (f32[640,256]{1,0:T(8,128)S(1)}, f32[640,256]{1,0:T(8,128)S(1)}, u32[]{:S(2)}, u32[]{:S(2)}) collective-permute-start(f32[640,256]{1,0:T(8,128)S(1)} %pick.19.refs_0_), channel_id=1, source_target_pairs={{0,4},{16,20},{8,12},{24,28},{5,1},{21,17},{13,9},{29,25},{2,6},{1... | collective-permute-start | bytes 1966088 | tf_op jit(solution)/shard_map/ppermute | solution.py:444
  83.2 4.8 %collective-permute-done.27.refs_4_ = f32[640,256]{1,0:T(8,128)S(1)} collective-permute-done((f32[640,256]{1,0:T(8,128)S(1)}, f32[640,256]{1,0:T(8,128)S(1)}, u32[]{:S(2)}, u32[]{:S(2)}) %collective-permute-start.27) | collective-permute-done | bytes 655392 | tf_op jit(solution)/shard_map/ppermute | solution.py:444
  88.0 1.5 %collective-permute-start.28 = (f32[640,256]{1,0:T(8,128)S(1)}, f32[640,256]{1,0:T(8,128)S(1)}, u32[]{:S(2)}, u32[]{:S(2)}) collective-permute-start(f32[640,256]{1,0:T(8,128)S(1)} %collective-permute-done.27.refs_4_), channel_id=1, source_target_pairs={{0,4},{16,20},{8,12},{24,28},{5,1},{21,17},{13,9},{29,25},{2,6},{1... | collective-permute-start | bytes 1966088 | tf_op jit(solution)/shard_map/ppermute | solution.py:444
  89.6 1.4 %collective-permute-done.28.refs_5_ = f32[640,256]{1,0:T(8,128)S(1)} collective-permute-done((f32[640,256]{1,0:T(8,128)S(1)}, f32[640,256]{1,0:T(8,128)S(1)}, u32[]{:S(2)}, u32[]{:S(2)}) %collective-permute-start.28) | collective-permute-done | bytes 655392 | tf_op jit(solution)/shard_map/ppermute | solution.py:444
  91.0 15.4 %schur.3 = f32[4,8,256,256]{3,2,1,0:T(8,128)} custom-call(s32[2]{0:T(128)S(1)} %pad_add_fusion.1.place, s32[32,32]{1,0:T(8,128)S(1)} %copy-done.10, f32[640,256]{1,0:T(8,128)S(1)} %pick.19.refs_0_, f32[640,256]{1,0:T(8,128)S(1)} %collective-permute-done.25.refs_1_, f32[640,256]{1,0:T(8,128)S(1)} %pick.17.refs_2_, ...), custom_call_target="tpu_custom_call" | custom-call | flops 8589934592 | bytes 16777216 | tf_op jit(solution)/shard_map/schur/pallas_call | solution.py:402
  106.4 0.6 while.9
  (20 shorter events, 0.1 us)
Async XLA Ops:
  3.0 9.1 %collective-permute-start.15 = (f32[256,256]{1,0:T(8,128)S(1)}, f32[256,256]{1,0:T(8,128)S(1)}, u32[]{:S(2)}, u32[]{:S(2)}) collective-permute-start(f32[256,256]{1,0:T(8,128)S(1)} %get-tuple-element.57), channel_id=1, source_target_pairs={{4,7}} | collective-permute-start | bytes 786440 | tf_op jit(solution)/shard_map/ppermute | solution.py:444
  3.6 8.4 %collective-permute-start.14 = (f32[256,256]{1,0:T(8,128)S(1)}, f32[256,256]{1,0:T(8,128)}, u32[]{:S(2)}, u32[]{:S(2)}) collective-permute-start(f32[256,256]{1,0:T(8,128)S(1)} %get-tuple-element.57), channel_id=1, source_target_pairs={{4,6}} | collective-permute-start | bytes 786440 | tf_op jit(solution)/shard_map/ppermute | solution.py:444
  5.0 7.1 %collective-permute-start.13 = (f32[256,256]{1,0:T(8,128)S(1)}, f32[256,256]{1,0:T(8,128)}, u32[]{:S(2)}, u32[]{:S(2)}) collective-permute-start(f32[256,256]{1,0:T(8,128)S(1)} %get-tuple-element.57), channel_id=1, source_target_pairs={{4,5}} | collective-permute-start | bytes 786440 | tf_op jit(solution)/shard_map/ppermute | solution.py:444
  6.4 17.5 %collective-permute-start.12 = (f32[640,256]{1,0:T(8,128)S(1)}, f32[640,256]{1,0:T(8,128)S(1)}, u32[]{:S(2)}, u32[]{:S(2)}) collective-permute-start(f32[640,256]{1,0:T(8,128)S(1)} %get-tuple-element.56.refs_0_.refs_1_.refs_5_), channel_id=1, source_target_pairs={{0,1},{4,5},{8,9},{12,13},{16,17},{20,21},{24,25},{28,29},{1,2},{5... | collective-permute-start | bytes 1966088 | tf_op jit(solution)/shard_map/ppermute | solution.py:444
  9.6 1.2 %copy-start = (f32[4,256,256]{2,1,0:T(8,128)S(1)}, f32[4,256,256]{2,1,0:T(8,128)}, u32[]{:S(2)}) copy-start(f32[4,256,256]{2,1,0:T(8,128)} %tiles.3) | copy-start | bytes 3145732
  10.8 2.4 %copy-start.1 = (f32[4,256,256]{2,1,0:T(8,128)S(1)}, f32[4,256,256]{2,1,0:T(8,128)}, u32[]{:S(2)}) copy-start(f32[4,256,256]{2,1,0:T(8,128)} %tiles.3) | copy-start | bytes 3145732
  10.8 2.4 %copy-start.10 = (s32[32,32]{1,0:T(8,128)S(1)}, s32[32,32]{1,0:T(8,128)}, u32[]{:S(2)}) copy-start(s32[32,32]{1,0:T(8,128)} %ranks.7) | copy-start | bytes 12292
  11.4 1.8 %collective-permute-start.16 = (f32[256,256]{1,0:T(8,128)S(1)}, f32[256,256]{1,0:T(8,128)S(1)}, u32[]{:S(2)}, u32[]{:S(2)}) collective-permute-start(f32[256,256]{1,0:T(8,128)S(1)} %first_inverse.1), channel_id=1, source_target_pairs={{0,4},{1,5},{2,6},{3,7}} | collective-permute-start | bytes 786440 | tf_op jit(solution)/shard_map/ppermute | solution.py:444
  23.8 15.6 %collective-permute-start.17 = (f32[640,256]{1,0:T(8,128)S(1)}, f32[640,256]{1,0:T(8,128)S(1)}, u32[]{:S(2)}, u32[]{:S(2)}) collective-permute-start(f32[640,256]{1,0:T(8,128)S(1)} %collective-permute-done.12.refs_1_.refs_2_.refs_6_), channel_id=1, source_target_pairs={{1,2},{5,6},{9,10},{13,14},{17,18},{21,22},{25,26},{29,30},{2,3},{... | collective-permute-start | bytes 1966088 | tf_op jit(solution)/shard_map/ppermute | solution.py:444
  27.1 13.8 %collective-permute-start.20 = (f32[640,256]{1,0:T(8,128)S(1)}, f32[640,256]{1,0:T(8,128)}, u32[]{:S(2)}, u32[]{:S(2)}) collective-permute-start(f32[640,256]{1,0:T(8,128)S(1)} %get-tuple-element.56.refs_0_.refs_1_.refs_5_), channel_id=1, source_target_pairs={{1,0},{5,4},{9,8},{13,12},{17,16},{21,20},{25,24},{29,28}} | collective-permute-start | bytes 1966088 | tf_op jit(solution)/shard_map/ppermute | solution.py:444
  29.2 12.9 %collective-permute-start.21 = (f32[768,256]{1,0:T(8,128)S(1)}, f32[768,256]{1,0:T(8,128)}, u32[]{:S(2)}, u32[]{:S(2)}) collective-permute-start(f32[768,256]{1,0:T(8,128)S(1)} %second_inverse.1.refs_0_), channel_id=1, source_target_pairs={{4,12},{5,13},{6,14},{7,15}} | collective-permute-start | bytes 2359304 | tf_op jit(solution)/shard_map/ppermute | solution.py:444
  39.5 4.0 %collective-permute-start.18 = (f32[640,256]{1,0:T(8,128)S(1)}, f32[640,256]{1,0:T(8,128)S(1)}, u32[]{:S(2)}, u32[]{:S(2)}) collective-permute-start(f32[640,256]{1,0:T(8,128)S(1)} %collective-permute-done.17.refs_2_.refs_3_.refs_7_), channel_id=1, source_target_pairs={{2,3},{6,7},{10,11},{14,15},{18,19},{22,23},{26,27},{30,31}} | collective-permute-start | bytes 1966088 | tf_op jit(solution)/shard_map/ppermute | solution.py:444
  40.8 11.3 %collective-permute-start.23 = (f32[640,256]{1,0:T(8,128)S(1)}, f32[640,256]{1,0:T(8,128)S(1)}, u32[]{:S(2)}, u32[]{:S(2)}) collective-permute-start(f32[640,256]{1,0:T(8,128)S(1)} %pick.16.refs_0_), channel_id=1, source_target_pairs={{0,8},{16,24},{5,13},{21,29},{10,2},{26,18},{15,7},{31,23}} | collective-permute-start | bytes 1966088 | tf_op jit(solution)/shard_map/ppermute | solution.py:444
  42.2 21.5 %collective-permute-start.22 = (f32[768,256]{1,0:T(8,128)S(1)}, f32[768,256]{1,0:T(8,128)S(1)}, u32[]{:S(2)}, u32[]{:S(2)}) collective-permute-start(f32[768,256]{1,0:T(8,128)S(1)} %pick.15.refs_0_), channel_id=1, source_target_pairs={{4,20},{5,21},{6,22},{7,23},{12,28},{13,29},{14,30},{15,31}} | collective-permute-start | bytes 2359304 | tf_op jit(solution)/shard_map/ppermute | solution.py:444
  63.8 42.6 %copy-start.6 = (f32[768,256]{1,0:T(8,128)}, f32[768,256]{1,0:T(8,128)S(1)}, u32[]{:S(2)}) copy-start(f32[768,256]{1,0:T(8,128)S(1)} %pick.18.refs_8_) | copy-start | bytes 2359300
  63.8 4.6 %collective-permute-start.24 = (f32[768,256]{1,0:T(8,128)S(1)}, f32[768,256]{1,0:T(8,128)S(1)}, u32[]{:S(2)}, u32[]{:S(2)}) collective-permute-start(f32[768,256]{1,0:T(8,128)S(1)} %pick.18.refs_8_), channel_id=1, source_target_pairs={{4,0},{5,1},{6,2},{7,3},{12,8},{13,9},{14,10},{15,11},{20,16},{21,... | collective-permute-start | bytes 2359304 | tf_op jit(solution)/shard_map/ppermute | solution.py:444
  65.1 11.3 %collective-permute-start.19 = (f32[640,256]{1,0:T(8,128)S(1)}, f32[640,256]{1,0:T(8,128)S(1)}, u32[]{:S(2)}, u32[]{:S(2)}) collective-permute-start(f32[640,256]{1,0:T(8,128)S(1)} %pick.14.refs_0_), channel_id=1, source_target_pairs={{0,8},{16,24},{5,13},{21,29},{10,2},{26,18},{15,7},{31,23}} | collective-permute-start | bytes 1966088 | tf_op jit(solution)/shard_map/ppermute | solution.py:444
  66.4 14.1 %collective-permute-start.29 = (f32[640,256]{1,0:T(8,128)S(1)}, f32[640,256]{1,0:T(8,128)S(1)}, u32[]{:S(2)}, u32[]{:S(2)}) collective-permute-start(f32[640,256]{1,0:T(8,128)S(1)} %pick.17.refs_2_), channel_id=1, source_target_pairs={{0,16},{16,0},{8,24},{24,8},{5,21},{21,5},{13,29},{29,13},{2,18},{... | collective-permute-start | bytes 1966088 | tf_op jit(solution)/shard_map/ppermute | solution.py:444
  68.4 38.0 %copy-start.8 = (f32[768,256]{1,0:T(8,128)}, f32[768,256]{1,0:T(8,128)S(1)}, u32[]{:S(2)}) copy-start(f32[768,256]{1,0:T(8,128)S(1)} %collective-permute-done.24.refs_9_) | copy-start | bytes 2359300
  71.1 19.9 %copy-start.2 = (bf16[4,8,256,128]{3,2,1,0:T(8,128)(2,1)S(1)}, bf16[4,8,256,128]{3,2,1,0:T(8,128)(2,1)}, u32[]{:S(2)}) copy-start(bf16[4,8,256,128]{3,2,1,0:T(8,128)(2,1)} %refs_11_.1) | copy-start | bytes 6291460
  71.1 19.9 %copy-start.4 = (bf16[4,8,256,128]{3,2,1,0:T(8,128)(2,1)S(1)}, bf16[4,8,256,128]{3,2,1,0:T(8,128)(2,1)}, u32[]{:S(2)}) copy-start(bf16[4,8,256,128]{3,2,1,0:T(8,128)(2,1)} %refs_12_.1) | copy-start | bytes 6291460
  76.7 11.3 %collective-permute-start.27 = (f32[640,256]{1,0:T(8,128)S(1)}, f32[640,256]{1,0:T(8,128)S(1)}, u32[]{:S(2)}, u32[]{:S(2)}) collective-permute-start(f32[640,256]{1,0:T(8,128)S(1)} %pick.19.refs_0_), channel_id=1, source_target_pairs={{0,16},{16,0},{8,24},{24,8},{5,21},{21,5},{13,29},{29,13},{2,18},{... | collective-permute-start | bytes 1966088 | tf_op jit(solution)/shard_map/ppermute | solution.py:444
  79.2 10.3 %collective-permute-start.26 = (f32[640,256]{1,0:T(8,128)S(1)}, f32[640,256]{1,0:T(8,128)S(1)}, u32[]{:S(2)}, u32[]{:S(2)}) collective-permute-start(f32[640,256]{1,0:T(8,128)S(1)} %pick.17.refs_2_), channel_id=1, source_target_pairs={{0,4},{16,20},{8,12},{24,28},{5,1},{21,17},{13,9},{29,25},{2,6},{1... | collective-permute-start | bytes 1966088 | tf_op jit(solution)/shard_map/ppermute | solution.py:444
  80.6 9.0 %collective-permute-start.30 = (f32[640,256]{1,0:T(8,128)S(1)}, f32[640,256]{1,0:T(8,128)S(1)}, u32[]{:S(2)}, u32[]{:S(2)}) collective-permute-start(f32[640,256]{1,0:T(8,128)S(1)} %collective-permute-done.29.refs_6_), channel_id=1, source_target_pairs={{0,4},{16,20},{8,12},{24,28},{5,1},{21,17},{13,9},{29,25},{2,6},{1... | collective-permute-start | bytes 1966088 | tf_op jit(solution)/shard_map/ppermute | solution.py:444
  81.9 7.7 %collective-permute-start.25 = (f32[640,256]{1,0:T(8,128)S(1)}, f32[640,256]{1,0:T(8,128)S(1)}, u32[]{:S(2)}, u32[]{:S(2)}) collective-permute-start(f32[640,256]{1,0:T(8,128)S(1)} %pick.19.refs_0_), channel_id=1, source_target_pairs={{0,4},{16,20},{8,12},{24,28},{5,1},{21,17},{13,9},{29,25},{2,6},{1... | collective-permute-start | bytes 1966088 | tf_op jit(solution)/shard_map/ppermute | solution.py:444
  88.0 3.0 %collective-permute-start.28 = (f32[640,256]{1,0:T(8,128)S(1)}, f32[640,256]{1,0:T(8,128)S(1)}, u32[]{:S(2)}, u32[]{:S(2)}) collective-permute-start(f32[640,256]{1,0:T(8,128)S(1)} %collective-permute-done.27.refs_4_), channel_id=1, source_target_pairs={{0,4},{16,20},{8,12},{24,28},{5,1},{21,17},{13,9},{29,25},{2,6},{1... | collective-permute-start | bytes 1966088 | tf_op jit(solution)/shard_map/ppermute | solution.py:444

commit v4 on v3

--- a/solution.py
+++ b/solution.py
@@ -445,6 +445,7 @@
 
     def down_column(array, root, fences):
         held = [root]
+        stages = []
         for bit in range(1, row_bits):
             step = 1 << bit
             got = move(array, [((r, c), (r ^ step, c)) for r in held for c in every_col])
@@ -452,7 +453,8 @@
             mine = row_here % 2 == root
             array = pick(jnp.where(mine & (row_here >> bit == 0), 0, jnp.where(mine & (row_here >> bit == 1), 1, -1)), [array, got])
             held = held + [r ^ step for r in held]
-        return array
+            stages.append(array)
+        return stages
 
     def to_other_parity(array, root):
         return move(array, [((r, c), (r ^ 1, c)) for r in every_row if r % 2 == root for c in every_col])
@@ -518,14 +520,16 @@
         sets = [after(array, *fence) if fence else array for array in sets]
         return [[array, hop(array, 0, held)] for array in sets]
 
+    if factoring:
+        stages = down_column(weights, 1, [chain[min(2, grid_cols - 1)], second_source])
+        weights = stages[-1]
+        inverses = [weights, to_other_parity(weights, 1)]
+        firsts = [firsts[0], *[after(array, stages[0]) for array in firsts[1:]]]
     first_source = source(firsts)
     second_have = low_hops(second_source, first_source)
-    if factoring:
-        weights = down_column(weights, 1, [chain[min(2, grid_cols - 1)], second_have])
-        inverses = [weights, to_other_parity(weights, 1)]
+    first_have = low_hops(first_source)
     rows = row_panels(place, ranks, firsts, seconds, inverses, capacity, row_slots, grid_rows)
-    first_have = low_hops(first_source, rows)
-    second_sets, first_sets = high_hops(second_have, early), high_hops(first_have)
+    second_sets, first_sets = high_hops(second_have, early), high_hops(first_have, rows)
     col_arrays = [sets[g] for g in range(spread) for sets in (first_sets, second_sets)]
     return schur(place, ranks, col_arrays, inverses, rows, left_fac, right_fac, capacity, grid_rows, grid_cols), inverses
 

time: 108 us -> 104 us (0.963)
  the two profiles are of different devices: /device:TPU:15 before, /device:TPU:21 now
where the time goes in v4:
time: 104 us; the launch traced here: 102 us
  waiting for transfers between devices  50.2 us (48%)
  starting transfers between devices  25 us (24%)
  Pallas kernels  22.7 us (22%)
  other arithmetic  1.78 us (2%)
  local copies, waits for them, and re-layouts  1.24 us (1%)
    ppermute x19, waiting for transfers between devices, move(): return lax.ppermute(array, AXES, flat)  50.2 us
    ppermute x19, starting transfers between devices, move(): return lax.ppermute(array, AXES, flat)  25 us
    pallas_call x1, Pallas kernels, schur(): pl.pallas_call(functools.partial(schur_kernel, capacity, grid_rows, grid_...  15.4 us
    pallas_call x1, Pallas kernels, pack(): pl.pallas_call(functools.partial(pack_kernel, capacity, grid_rows), out_s...  2.88 us
    pallas_call x1, Pallas kernels, row_panels(): pl.pallas_call(functools.partial(rows_kernel, capacity, grid_rows, count)...  2.7 us
  transfers between devices with their start and end apart: 19, of which 8 were waited for; matrix products, arithmetic and copies ran while one was open for 2% of the time, Pallas kernels for 4%

profile of v4, /device:TPU:21, one launch (start us, length us, event | category | flops | bytes accessed | tf_op | source)
XLA Modules:
  0.0 102.1 jit_solution(14347616347360881942)
XLA Ops:
  0.0 0.1 pad_add_fusion.1.place
  0.1 2.9 %pack.3 = (f32[640,256]{1,0:T(8,128)S(1)}, f32[256,256]{1,0:T(8,128)S(1)}) custom-call(s32[2]{0:T(128)S(1)} %pad_add_fusion.1.place, s32[32,32]{1,0:T(8,128)} %ranks.7, bf16[4,8,256,128]{3,2,1,0:T(8,128)(2,1)} %refs_11_.1, bf16[4,8,256,128]{3,2,1,0:T(8,128)(2,1)} %refs_12_.1), custom_call_target="tpu_custom_call" | custom-call | flops 1024 | bytes 1024 | tf_op jit(solution)/shard_map/pack/pallas_call | solution.py:205
  3.0 0.7 collective-permute-start.15
  3.6 1.4 %collective-permute-start.14 = (f32[256,256]{1,0:T(8,128)S(1)}, f32[256,256]{1,0:T(8,128)}, u32[]{:S(2)}, u32[]{:S(2)}) collective-permute-start(f32[256,256]{1,0:T(8,128)S(1)} %get-tuple-element.62), channel_id=1, source_target_pairs={{4,6}} | collective-permute-start | bytes 786440 | tf_op jit(solution)/shard_map/ppermute | solution.py:444
  5.0 1.3 %collective-permute-start.13 = (f32[256,256]{1,0:T(8,128)S(1)}, f32[256,256]{1,0:T(8,128)}, u32[]{:S(2)}, u32[]{:S(2)}) collective-permute-start(f32[256,256]{1,0:T(8,128)S(1)} %get-tuple-element.62), channel_id=1, source_target_pairs={{4,5}} | collective-permute-start | bytes 786440 | tf_op jit(solution)/shard_map/ppermute | solution.py:444
  6.4 1.3 %collective-permute-start.12 = (f32[640,256]{1,0:T(8,128)S(1)}, f32[640,256]{1,0:T(8,128)S(1)}, u32[]{:S(2)}, u32[]{:S(2)}) collective-permute-start(f32[640,256]{1,0:T(8,128)S(1)} %get-tuple-element.61.refs_0_.refs_1_.refs_5_), channel_id=1, source_target_pairs={{0,1},{4,5},{8,9},{12,13},{16,17},{20,21},{24,25},{28,29},{1,2},{5... | collective-permute-start | bytes 1966088 | tf_op jit(solution)/shard_map/ppermute | solution.py:444
  7.7 0.0 copy-start
  7.7 1.2 %copy-done = f32[4,256,256]{2,1,0:T(8,128)S(1)} copy-done((f32[4,256,256]{2,1,0:T(8,128)S(1)}, f32[4,256,256]{2,1,0:T(8,128)}, u32[]{:S(2)}) %copy-start) | copy-done | bytes 1048600
  8.9 0.6 first_inverse.1
  9.4 0.7 collective-permute-start.16
  10.1 0.0 collective-permute-done.15
  10.1 0.0 collective-permute-done.14
  10.2 0.0 collective-permute-done.13
  10.2 1.1 %add_select_fusion.bases = f32[256,256]{1,0:T(8,128)S(1)} fusion(f32[256,256]{1,0:T(8,128)S(1)} %get-tuple-element.62, f32[256,256]{1,0:T(8,128)S(1)} %collective-permute-done.15, f32[256,256]{1,0:T(8,128)} %collective-permute-done.13, f32[256,256]{1,0:T(8,128)} %collective-permute-done.14, pred[]{:T(512)S(6)} %eq.62), kind=kLoop, calls=%fused_computation.1 | loop fusion | flops 196608 | bytes 1310721 | tf_op jit(solution)/shard_map/jit(_where)/select_n | solution.py:474
  11.3 0.0 collective-permute-done.16.inverse
  11.3 1.0 second_inverse.1.refs_0_
  12.3 11.5 %collective-permute-done.12.refs_1_.refs_2_.refs_6_ = f32[640,256]{1,0:T(8,128)S(1)} collective-permute-done((f32[640,256]{1,0:T(8,128)S(1)}, f32[640,256]{1,0:T(8,128)S(1)}, u32[]{:S(2)}, u32[]{:S(2)}) %collective-permute-start.12) | collective-permute-done | bytes 655392 | tf_op jit(solution)/shard_map/ppermute | solution.py:444
  23.8 1.9 %collective-permute-start.18 = (f32[640,256]{1,0:T(8,128)S(1)}, f32[640,256]{1,0:T(8,128)S(1)}, u32[]{:S(2)}, u32[]{:S(2)}) collective-permute-start(f32[640,256]{1,0:T(8,128)S(1)} %collective-permute-done.12.refs_1_.refs_2_.refs_6_), channel_id=1, source_target_pairs={{1,2},{5,6},{9,10},{13,14},{17,18},{21,22},{25,26},{29,30},{2,3},{... | collective-permute-start | bytes 1966088 | tf_op jit(solution)/shard_map/ppermute | solution.py:444
  25.8 1.5 %collective-permute-start.21 = (f32[640,256]{1,0:T(8,128)S(1)}, f32[640,256]{1,0:T(8,128)}, u32[]{:S(2)}, u32[]{:S(2)}) collective-permute-start(f32[640,256]{1,0:T(8,128)S(1)} %get-tuple-element.61.refs_0_.refs_1_.refs_5_), channel_id=1, source_target_pairs={{1,0},{5,4},{9,8},{13,12},{17,16},{21,20},{25,24},{29,28}} | collective-permute-start | bytes 1966088 | tf_op jit(solution)/shard_map/ppermute | solution.py:444
  27.3 1.6 %collective-permute-start.17 = (f32[768,256]{1,0:T(8,128)S(1)}, f32[768,256]{1,0:T(8,128)}, u32[]{:S(2)}, u32[]{:S(2)}) collective-permute-start(f32[768,256]{1,0:T(8,128)S(1)} %second_inverse.1.refs_0_), channel_id=1, source_target_pairs={{4,12},{5,13},{6,14},{7,15}} | collective-permute-start | bytes 2359304 | tf_op jit(solution)/shard_map/ppermute | solution.py:444
  28.9 11.6 %collective-permute-done.18.refs_2_.refs_3_.refs_7_ = f32[640,256]{1,0:T(8,128)S(1)} collective-permute-done((f32[640,256]{1,0:T(8,128)S(1)}, f32[640,256]{1,0:T(8,128)S(1)}, u32[]{:S(2)}, u32[]{:S(2)}) %collective-permute-start.18) | collective-permute-done | bytes 655392 | tf_op jit(solution)/shard_map/ppermute | solution.py:444
  40.4 2.2 %collective-permute-start.19 = (f32[640,256]{1,0:T(8,128)S(1)}, f32[640,256]{1,0:T(8,128)S(1)}, u32[]{:S(2)}, u32[]{:S(2)}) collective-permute-start(f32[640,256]{1,0:T(8,128)S(1)} %collective-permute-done.18.refs_2_.refs_3_.refs_7_), channel_id=1, source_target_pairs={{2,3},{6,7},{10,11},{14,15},{18,19},{22,23},{26,27},{30,31}} | collective-permute-start | bytes 1966088 | tf_op jit(solution)/shard_map/ppermute | solution.py:444
  42.6 0.0 collective-permute-done.21.refs_0_.refs_4_
  42.7 0.7 collective-permute-start.25
  43.4 0.0 collective-permute-done.17.refs_1_
  43.4 1.3 %collective-permute-start.22 = (f32[768,256]{1,0:T(8,128)S(1)}, f32[768,256]{1,0:T(8,128)S(1)}, u32[]{:S(2)}, u32[]{:S(2)}) collective-permute-start(f32[768,256]{1,0:T(8,128)S(1)} %pick.14.refs_0_), channel_id=1, source_target_pairs={{4,20},{5,21},{6,22},{7,23},{12,28},{13,29},{14,30},{15,31}} | collective-permute-start | bytes 2359304 | tf_op jit(solution)/shard_map/ppermute | solution.py:444
  44.7 9.7 %collective-permute-done.19.refs_3_ = f32[640,256]{1,0:T(8,128)S(1)} collective-permute-done((f32[640,256]{1,0:T(8,128)S(1)}, f32[640,256]{1,0:T(8,128)S(1)}, u32[]{:S(2)}, u32[]{:S(2)}) %collective-permute-start.19) | collective-permute-done | bytes 655392 | tf_op jit(solution)/shard_map/ppermute | solution.py:444
  54.4 0.7 collective-permute-start.20
  55.2 0.7 collective-permute-start.29
  55.9 5.8 %collective-permute-done.22.refs_1_ = f32[768,256]{1,0:T(8,128)S(1)} collective-permute-done((f32[768,256]{1,0:T(8,128)S(1)}, f32[768,256]{1,0:T(8,128)S(1)}, u32[]{:S(2)}, u32[]{:S(2)}) %collective-permute-start.22) | collective-permute-done | bytes 786464 | tf_op jit(solution)/shard_map/ppermute | solution.py:444
  61.7 0.1 pick.18.refs_8_
  61.8 2.8 %collective-permute-start.23 = (f32[768,256]{1,0:T(8,128)S(1)}, f32[768,256]{1,0:T(8,128)S(1)}, u32[]{:S(2)}, u32[]{:S(2)}) collective-permute-start(f32[768,256]{1,0:T(8,128)S(1)} %pick.18.refs_8_), channel_id=1, source_target_pairs={{4,0},{5,1},{6,2},{7,3},{12,8},{13,9},{14,10},{15,11},{20,16},{21,... | collective-permute-start | bytes 2359304 | tf_op jit(solution)/shard_map/ppermute | solution.py:444
  64.7 0.0 copy-start.2
  64.7 0.0 copy-start.4
  64.7 0.8 collective-permute-start.27
  65.5 0.6 fusion
  66.1 1.3 %collective-permute-start.26 = (f32[640,256]{1,0:T(8,128)S(1)}, f32[640,256]{1,0:T(8,128)S(1)}, u32[]{:S(2)}, u32[]{:S(2)}) collective-permute-start(f32[640,256]{1,0:T(8,128)S(1)} %pick.19.refs_2_), channel_id=1, source_target_pairs={{0,4},{16,20},{8,12},{24,28},{5,1},{21,17},{13,9},{29,25},{2,6},{1... | collective-permute-start | bytes 1966088 | tf_op jit(solution)/shard_map/ppermute | solution.py:444
  67.4 1.3 %collective-permute-start.30 = (f32[640,256]{1,0:T(8,128)S(1)}, f32[640,256]{1,0:T(8,128)S(1)}, u32[]{:S(2)}, u32[]{:S(2)}) collective-permute-start(f32[640,256]{1,0:T(8,128)S(1)} %collective-permute-done.29.refs_6_), channel_id=1, source_target_pairs={{0,4},{16,20},{8,12},{24,28},{5,1},{21,17},{13,9},{29,25},{2,6},{1... | collective-permute-start | bytes 1966088 | tf_op jit(solution)/shard_map/ppermute | solution.py:444
  68.7 0.0 collective-permute-done.23.refs_9_
  68.8 2.7 %row_panels.3.refs_10_ = bf16[4,256,1536]{2,1,0:T(8,128)(2,1)S(1)} custom-call(s32[2]{0:T(128)S(1)} %pad_add_fusion.1.place, s32[32,32]{1,0:T(8,128)S(1)} %copy-done.10, f32[640,256]{1,0:T(8,128)S(1)} %get-tuple-element.61.refs_0_.refs_1_.refs_5_, f32[640,256]{1,0:T(8,128)S(1)} %collective-permute-done.12.refs_1_.refs_2_.refs_6_, ...), custom_call_target="tpu_custom_call" | custom-call | flops 1024 | bytes 1024 | tf_op jit(solution)/shard_map/row_panels/pallas_call | solution.py:282
  71.5 1.3 %collective-permute-start.24 = (f32[640,256]{1,0:T(8,128)S(1)}, f32[640,256]{1,0:T(8,128)S(1)}, u32[]{:S(2)}, u32[]{:S(2)}) collective-permute-start(f32[640,256]{1,0:T(8,128)S(1)} %pick.16.refs_0_), channel_id=1, source_target_pairs={{0,4},{16,20},{8,12},{24,28},{5,1},{21,17},{13,9},{29,25},{2,6},{1... | collective-permute-start | bytes 1966088 | tf_op jit(solution)/shard_map/ppermute | solution.py:444
  72.8 1.5 %collective-permute-start.28 = (f32[640,256]{1,0:T(8,128)S(1)}, f32[640,256]{1,0:T(8,128)S(1)}, u32[]{:S(2)}, u32[]{:S(2)}) collective-permute-start(f32[640,256]{1,0:T(8,128)S(1)} %collective-permute-done.27.refs_4_), channel_id=1, source_target_pairs={{0,4},{16,20},{8,12},{24,28},{5,1},{21,17},{13,9},{29,25},{2,6},{1... | collective-permute-start | bytes 1966088 | tf_op jit(solution)/shard_map/ppermute | solution.py:444
  74.3 3.2 %collective-permute-done.26.refs_3_ = f32[640,256]{1,0:T(8,128)S(1)} collective-permute-done((f32[640,256]{1,0:T(8,128)S(1)}, f32[640,256]{1,0:T(8,128)S(1)}, u32[]{:S(2)}, u32[]{:S(2)}) %collective-permute-start.26) | collective-permute-done | bytes 655392 | tf_op jit(solution)/shard_map/ppermute | solution.py:444
  77.5 1.3 %collective-permute-done.30.refs_7_ = f32[640,256]{1,0:T(8,128)S(1)} collective-permute-done((f32[640,256]{1,0:T(8,128)S(1)}, f32[640,256]{1,0:T(8,128)S(1)}, u32[]{:S(2)}, u32[]{:S(2)}) %collective-permute-start.30) | collective-permute-done | bytes 655392 | tf_op jit(solution)/shard_map/ppermute | solution.py:444
  78.9 4.1 %collective-permute-done.24.refs_1_ = f32[640,256]{1,0:T(8,128)S(1)} collective-permute-done((f32[640,256]{1,0:T(8,128)S(1)}, f32[640,256]{1,0:T(8,128)S(1)}, u32[]{:S(2)}, u32[]{:S(2)}) %collective-permute-start.24) | collective-permute-done | bytes 655392 | tf_op jit(solution)/shard_map/ppermute | solution.py:444
  82.9 3.0 %collective-permute-done.28.refs_5_ = f32[640,256]{1,0:T(8,128)S(1)} collective-permute-done((f32[640,256]{1,0:T(8,128)S(1)}, f32[640,256]{1,0:T(8,128)S(1)}, u32[]{:S(2)}, u32[]{:S(2)}) %collective-permute-start.28) | collective-permute-done | bytes 655392 | tf_op jit(solution)/shard_map/ppermute | solution.py:444
  85.9 15.4 %schur.3 = f32[4,8,256,256]{3,2,1,0:T(8,128)} custom-call(s32[2]{0:T(128)S(1)} %pad_add_fusion.1.place, s32[32,32]{1,0:T(8,128)S(1)} %copy-done.10, f32[640,256]{1,0:T(8,128)S(1)} %pick.16.refs_0_, f32[640,256]{1,0:T(8,128)S(1)} %collective-permute-done.24.refs_1_, f32[640,256]{1,0:T(8,128)S(1)} %pick.19.refs_2_, ...), custom_call_target="tpu_custom_call" | custom-call | flops 8589934592 | bytes 16777216 | tf_op jit(solution)/shard_map/schur/pallas_call | solution.py:402
  101.3 0.6 while.9
  (18 shorter events, 0.2 us)
Async XLA Ops:
  3.0 7.2 %collective-permute-start.15 = (f32[256,256]{1,0:T(8,128)S(1)}, f32[256,256]{1,0:T(8,128)S(1)}, u32[]{:S(2)}, u32[]{:S(2)}) collective-permute-start(f32[256,256]{1,0:T(8,128)S(1)} %get-tuple-element.62), channel_id=1, source_target_pairs={{4,7}} | collective-permute-start | bytes 786440 | tf_op jit(solution)/shard_map/ppermute | solution.py:444
  3.6 6.5 %collective-permute-start.14 = (f32[256,256]{1,0:T(8,128)S(1)}, f32[256,256]{1,0:T(8,128)}, u32[]{:S(2)}, u32[]{:S(2)}) collective-permute-start(f32[256,256]{1,0:T(8,128)S(1)} %get-tuple-element.62), channel_id=1, source_target_pairs={{4,6}} | collective-permute-start | bytes 786440 | tf_op jit(solution)/shard_map/ppermute | solution.py:444
  5.0 5.1 %collective-permute-start.13 = (f32[256,256]{1,0:T(8,128)S(1)}, f32[256,256]{1,0:T(8,128)}, u32[]{:S(2)}, u32[]{:S(2)}) collective-permute-start(f32[256,256]{1,0:T(8,128)S(1)} %get-tuple-element.62), channel_id=1, source_target_pairs={{4,5}} | collective-permute-start | bytes 786440 | tf_op jit(solution)/shard_map/ppermute | solution.py:444
  6.4 17.5 %collective-permute-start.12 = (f32[640,256]{1,0:T(8,128)S(1)}, f32[640,256]{1,0:T(8,128)S(1)}, u32[]{:S(2)}, u32[]{:S(2)}) collective-permute-start(f32[640,256]{1,0:T(8,128)S(1)} %get-tuple-element.61.refs_0_.refs_1_.refs_5_), channel_id=1, source_target_pairs={{0,1},{4,5},{8,9},{12,13},{16,17},{20,21},{24,25},{28,29},{1,2},{5... | collective-permute-start | bytes 1966088 | tf_op jit(solution)/shard_map/ppermute | solution.py:444
  7.7 1.2 %copy-start = (f32[4,256,256]{2,1,0:T(8,128)S(1)}, f32[4,256,256]{2,1,0:T(8,128)}, u32[]{:S(2)}) copy-start(f32[4,256,256]{2,1,0:T(8,128)} %tiles.3) | copy-start | bytes 3145732
  8.9 2.4 %copy-start.1 = (f32[4,256,256]{2,1,0:T(8,128)S(1)}, f32[4,256,256]{2,1,0:T(8,128)}, u32[]{:S(2)}) copy-start(f32[4,256,256]{2,1,0:T(8,128)} %tiles.3) | copy-start | bytes 3145732
  8.9 2.4 %copy-start.10 = (s32[32,32]{1,0:T(8,128)S(1)}, s32[32,32]{1,0:T(8,128)}, u32[]{:S(2)}) copy-start(s32[32,32]{1,0:T(8,128)} %ranks.7) | copy-start | bytes 12292
  9.4 1.8 %collective-permute-start.16 = (f32[256,256]{1,0:T(8,128)S(1)}, f32[256,256]{1,0:T(8,128)S(1)}, u32[]{:S(2)}, u32[]{:S(2)}) collective-permute-start(f32[256,256]{1,0:T(8,128)S(1)} %first_inverse.1), channel_id=1, source_target_pairs={{0,4},{1,5},{2,6},{3,7}} | collective-permute-start | bytes 786440 | tf_op jit(solution)/shard_map/ppermute | solution.py:444
  23.8 16.6 %collective-permute-start.18 = (f32[640,256]{1,0:T(8,128)S(1)}, f32[640,256]{1,0:T(8,128)S(1)}, u32[]{:S(2)}, u32[]{:S(2)}) collective-permute-start(f32[640,256]{1,0:T(8,128)S(1)} %collective-permute-done.12.refs_1_.refs_2_.refs_6_), channel_id=1, source_target_pairs={{1,2},{5,6},{9,10},{13,14},{17,18},{21,22},{25,26},{29,30},{2,3},{... | collective-permute-start | bytes 1966088 | tf_op jit(solution)/shard_map/ppermute | solution.py:444
  25.8 16.9 %collective-permute-start.21 = (f32[640,256]{1,0:T(8,128)S(1)}, f32[640,256]{1,0:T(8,128)}, u32[]{:S(2)}, u32[]{:S(2)}) collective-permute-start(f32[640,256]{1,0:T(8,128)S(1)} %get-tuple-element.61.refs_0_.refs_1_.refs_5_), channel_id=1, source_target_pairs={{1,0},{5,4},{9,8},{13,12},{17,16},{21,20},{25,24},{29,28}} | collective-permute-start | bytes 1966088 | tf_op jit(solution)/shard_map/ppermute | solution.py:444
  27.3 16.1 %collective-permute-start.17 = (f32[768,256]{1,0:T(8,128)S(1)}, f32[768,256]{1,0:T(8,128)}, u32[]{:S(2)}, u32[]{:S(2)}) collective-permute-start(f32[768,256]{1,0:T(8,128)S(1)} %second_inverse.1.refs_0_), channel_id=1, source_target_pairs={{4,12},{5,13},{6,14},{7,15}} | collective-permute-start | bytes 2359304 | tf_op jit(solution)/shard_map/ppermute | solution.py:444
  40.4 14.0 %collective-permute-start.19 = (f32[640,256]{1,0:T(8,128)S(1)}, f32[640,256]{1,0:T(8,128)S(1)}, u32[]{:S(2)}, u32[]{:S(2)}) collective-permute-start(f32[640,256]{1,0:T(8,128)S(1)} %collective-permute-done.18.refs_2_.refs_3_.refs_7_), channel_id=1, source_target_pairs={{2,3},{6,7},{10,11},{14,15},{18,19},{22,23},{26,27},{30,31}} | collective-permute-start | bytes 1966088 | tf_op jit(solution)/shard_map/ppermute | solution.py:444
  42.7 12.5 %collective-permute-start.25 = (f32[640,256]{1,0:T(8,128)S(1)}, f32[640,256]{1,0:T(8,128)S(1)}, u32[]{:S(2)}, u32[]{:S(2)}) collective-permute-start(f32[640,256]{1,0:T(8,128)S(1)} %pick.17.refs_0_), channel_id=1, source_target_pairs={{0,8},{16,24},{5,13},{21,29},{10,2},{26,18},{15,7},{31,23}} | collective-permute-start | bytes 1966088 | tf_op jit(solution)/shard_map/ppermute | solution.py:444
  43.4 18.3 %collective-permute-start.22 = (f32[768,256]{1,0:T(8,128)S(1)}, f32[768,256]{1,0:T(8,128)S(1)}, u32[]{:S(2)}, u32[]{:S(2)}) collective-permute-start(f32[768,256]{1,0:T(8,128)S(1)} %pick.14.refs_0_), channel_id=1, source_target_pairs={{4,20},{5,21},{6,22},{7,23},{12,28},{13,29},{14,30},{15,31}} | collective-permute-start | bytes 2359304 | tf_op jit(solution)/shard_map/ppermute | solution.py:444
  54.4 10.2 %collective-permute-start.20 = (f32[640,256]{1,0:T(8,128)S(1)}, f32[640,256]{1,0:T(8,128)S(1)}, u32[]{:S(2)}, u32[]{:S(2)}) collective-permute-start(f32[640,256]{1,0:T(8,128)S(1)} %pick.15.refs_0_), channel_id=1, source_target_pairs={{0,8},{16,24},{5,13},{21,29},{10,2},{26,18},{15,7},{31,23}} | collective-permute-start | bytes 1966088 | tf_op jit(solution)/shard_map/ppermute | solution.py:444
  55.2 12.2 %collective-permute-start.29 = (f32[640,256]{1,0:T(8,128)S(1)}, f32[640,256]{1,0:T(8,128)S(1)}, u32[]{:S(2)}, u32[]{:S(2)}) collective-permute-start(f32[640,256]{1,0:T(8,128)S(1)} %pick.19.refs_2_), channel_id=1, source_target_pairs={{0,16},{16,0},{8,24},{24,8},{5,21},{21,5},{13,29},{29,13},{2,18},{... | collective-permute-start | bytes 1966088 | tf_op jit(solution)/shard_map/ppermute | solution.py:444
  61.8 39.5 %copy-start.6 = (f32[768,256]{1,0:T(8,128)}, f32[768,256]{1,0:T(8,128)S(1)}, u32[]{:S(2)}) copy-start(f32[768,256]{1,0:T(8,128)S(1)} %pick.18.refs_8_) | copy-start | bytes 2359300
  61.8 6.9 %collective-permute-start.23 = (f32[768,256]{1,0:T(8,128)S(1)}, f32[768,256]{1,0:T(8,128)S(1)}, u32[]{:S(2)}, u32[]{:S(2)}) collective-permute-start(f32[768,256]{1,0:T(8,128)S(1)} %pick.18.refs_8_), channel_id=1, source_target_pairs={{4,0},{5,1},{6,2},{7,3},{12,8},{13,9},{14,10},{15,11},{20,16},{21,... | collective-permute-start | bytes 2359304 | tf_op jit(solution)/shard_map/ppermute | solution.py:444
  64.7 21.2 %copy-start.2 = (bf16[4,8,256,128]{3,2,1,0:T(8,128)(2,1)S(1)}, bf16[4,8,256,128]{3,2,1,0:T(8,128)(2,1)}, u32[]{:S(2)}) copy-start(bf16[4,8,256,128]{3,2,1,0:T(8,128)(2,1)} %refs_11_.1) | copy-start | bytes 6291460
  64.7 21.2 %copy-start.4 = (bf16[4,8,256,128]{3,2,1,0:T(8,128)(2,1)S(1)}, bf16[4,8,256,128]{3,2,1,0:T(8,128)(2,1)}, u32[]{:S(2)}) copy-start(bf16[4,8,256,128]{3,2,1,0:T(8,128)(2,1)} %refs_12_.1) | copy-start | bytes 6291460
  64.7 8.1 %collective-permute-start.27 = (f32[640,256]{1,0:T(8,128)S(1)}, f32[640,256]{1,0:T(8,128)S(1)}, u32[]{:S(2)}, u32[]{:S(2)}) collective-permute-start(f32[640,256]{1,0:T(8,128)S(1)} %pick.16.refs_0_), channel_id=1, source_target_pairs={{0,16},{16,0},{8,24},{24,8},{5,21},{21,5},{13,29},{29,13},{2,18},{... | collective-permute-start | bytes 1966088 | tf_op jit(solution)/shard_map/ppermute | solution.py:444
  66.1 11.4 %collective-permute-start.26 = (f32[640,256]{1,0:T(8,128)S(1)}, f32[640,256]{1,0:T(8,128)S(1)}, u32[]{:S(2)}, u32[]{:S(2)}) collective-permute-start(f32[640,256]{1,0:T(8,128)S(1)} %pick.19.refs_2_), channel_id=1, source_target_pairs={{0,4},{16,20},{8,12},{24,28},{5,1},{21,17},{13,9},{29,25},{2,6},{1... | collective-permute-start | bytes 1966088 | tf_op jit(solution)/shard_map/ppermute | solution.py:444
  67.4 11.4 %collective-permute-start.30 = (f32[640,256]{1,0:T(8,128)S(1)}, f32[640,256]{1,0:T(8,128)S(1)}, u32[]{:S(2)}, u32[]{:S(2)}) collective-permute-start(f32[640,256]{1,0:T(8,128)S(1)} %collective-permute-done.29.refs_6_), channel_id=1, source_target_pairs={{0,4},{16,20},{8,12},{24,28},{5,1},{21,17},{13,9},{29,25},{2,6},{1... | collective-permute-start | bytes 1966088 | tf_op jit(solution)/shard_map/ppermute | solution.py:444
  71.5 11.5 %collective-permute-start.24 = (f32[640,256]{1,0:T(8,128)S(1)}, f32[640,256]{1,0:T(8,128)S(1)}, u32[]{:S(2)}, u32[]{:S(2)}) collective-permute-start(f32[640,256]{1,0:T(8,128)S(1)} %pick.16.refs_0_), channel_id=1, source_target_pairs={{0,4},{16,20},{8,12},{24,28},{5,1},{21,17},{13,9},{29,25},{2,6},{1... | collective-permute-start | bytes 1966088 | tf_op jit(solution)/shard_map/ppermute | solution.py:444
  72.8 13.1 %collective-permute-start.28 = (f32[640,256]{1,0:T(8,128)S(1)}, f32[640,256]{1,0:T(8,128)S(1)}, u32[]{:S(2)}, u32[]{:S(2)}) collective-permute-start(f32[640,256]{1,0:T(8,128)S(1)} %collective-permute-done.27.refs_4_), channel_id=1, source_target_pairs={{0,4},{16,20},{8,12},{24,28},{5,1},{21,17},{13,9},{29,25},{2,6},{1... | collective-permute-start | bytes 1966088 | tf_op jit(solution)/shard_map/ppermute | solution.py:444

commit v5 on v4

--- a/solution.py
+++ b/solution.py
@@ -473,8 +473,8 @@
         received = [move(pivot_bases, [((1, 0), (1, c))]) for c in every_col if c]
         pivot_bases = jnp.where(col_here == 0, pivot_bases, sum(received))
         chain.append(chain_step(packed, 1))
-        weights = second_inverse(place, ranks, diag_tiles, pivot_bases, passed)
-        chain[1], weights = lax.optimization_barrier((chain[1], weights))
+        chain[1] = after(chain[1], passed)
+        weights = second_inverse(place, ranks, diag_tiles, after(pivot_bases, chain[1]), passed)
     else:
         chain.append(chain_step(packed, 1))
 

time: 104 us -> 115 us (1.11)
  the two profiles are of different devices: /device:TPU:21 before, /device:TPU:5 now
where the time goes in v5:
time: 115 us; the launch traced here: 114 us
  waiting for transfers between devices  62.2 us (54%)
  Pallas kernels  24.4 us (21%)
  starting transfers between devices  22.6 us (20%)
  other arithmetic  1.96 us (2%)
  local copies, waits for them, and re-layouts  1.26 us (1%)
    ppermute x19, waiting for transfers between devices, move(): return lax.ppermute(array, AXES, flat)  62.2 us
    ppermute x19, starting transfers between devices, move(): return lax.ppermute(array, AXES, flat)  22.6 us
    pallas_call x1, Pallas kernels, schur(): pl.pallas_call(functools.partial(schur_kernel, capacity, grid_rows, grid_...  15.3 us
    pallas_call x1, Pallas kernels, row_panels(): pl.pallas_call(functools.partial(rows_kernel, capacity, grid_rows, count)...  3.43 us
    pallas_call x1, Pallas kernels, pack(): pl.pallas_call(functools.partial(pack_kernel, capacity, grid_rows), out_s...  2.88 us
  transfers between devices with their start and end apart: 19, of which 5 were waited for; matrix products, arithmetic and copies ran while one was open for 2% of the time, Pallas kernels for 5%

profile of v5, /device:TPU:5, one launch (start us, length us, event | category | flops | bytes accessed | tf_op | source)
XLA Modules:
  0.0 113.8 jit_solution(1765539286227240846)
XLA Ops:
  0.0 0.1 pad_add_fusion.1.place
  0.1 2.9 %pack.3 = (f32[640,256]{1,0:T(8,128)S(1)}, f32[256,256]{1,0:T(8,128)S(1)}) custom-call(s32[2]{0:T(128)S(1)} %pad_add_fusion.1.place, s32[32,32]{1,0:T(8,128)} %ranks.7, bf16[4,8,256,128]{3,2,1,0:T(8,128)(2,1)} %refs_11_.1, bf16[4,8,256,128]{3,2,1,0:T(8,128)(2,1)} %refs_12_.1), custom_call_target="tpu_custom_call" | custom-call | flops 1024 | bytes 1024 | tf_op jit(solution)/shard_map/pack/pallas_call | solution.py:205
  3.0 3.2 %collective-permute-start.12 = (f32[640,256]{1,0:T(8,128)S(1)}, f32[640,256]{1,0:T(8,128)S(1)}, u32[]{:S(2)}, u32[]{:S(2)}) collective-permute-start(f32[640,256]{1,0:T(8,128)S(1)} %get-tuple-element.61.refs_0_.refs_1_.refs_5_), channel_id=1, source_target_pairs={{0,1},{4,5},{8,9},{12,13},{16,17},{20,21},{24,25},{28,29},{1,2},{5... | collective-permute-start | bytes 1966088 | tf_op jit(solution)/shard_map/ppermute | solution.py:444
  6.2 0.0 copy-start
  6.2 1.2 %copy-done = f32[4,256,256]{2,1,0:T(8,128)S(1)} copy-done((f32[4,256,256]{2,1,0:T(8,128)S(1)}, f32[4,256,256]{2,1,0:T(8,128)}, u32[]{:S(2)}) %copy-start) | copy-done | bytes 1048600
  7.4 0.6 first_inverse.1
  8.0 0.7 collective-permute-start.13
  8.7 1.4 %collective-permute-start.16 = (f32[256,256]{1,0:T(8,128)S(1)}, f32[256,256]{1,0:T(8,128)}, u32[]{:S(2)}, u32[]{:S(2)}) collective-permute-start(f32[256,256]{1,0:T(8,128)S(1)} %get-tuple-element.63), channel_id=1, source_target_pairs={{4,7}} | collective-permute-start | bytes 786440 | tf_op jit(solution)/shard_map/ppermute | solution.py:444
  10.1 1.4 %collective-permute-start.15 = (f32[256,256]{1,0:T(8,128)S(1)}, f32[256,256]{1,0:T(8,128)}, u32[]{:S(2)}, u32[]{:S(2)}) collective-permute-start(f32[256,256]{1,0:T(8,128)S(1)} %get-tuple-element.63), channel_id=1, source_target_pairs={{4,6}} | collective-permute-start | bytes 786440 | tf_op jit(solution)/shard_map/ppermute | solution.py:444
  11.4 1.4 %collective-permute-start.14 = (f32[256,256]{1,0:T(8,128)S(1)}, f32[256,256]{1,0:T(8,128)}, u32[]{:S(2)}, u32[]{:S(2)}) collective-permute-start(f32[256,256]{1,0:T(8,128)S(1)} %get-tuple-element.63), channel_id=1, source_target_pairs={{4,5}} | collective-permute-start | bytes 786440 | tf_op jit(solution)/shard_map/ppermute | solution.py:444
  12.8 6.7 %collective-permute-done.12.refs_1_.refs_2_.refs_6_ = f32[640,256]{1,0:T(8,128)S(1)} collective-permute-done((f32[640,256]{1,0:T(8,128)S(1)}, f32[640,256]{1,0:T(8,128)S(1)}, u32[]{:S(2)}, u32[]{:S(2)}) %collective-permute-start.12) | collective-permute-done | bytes 655392 | tf_op jit(solution)/shard_map/ppermute | solution.py:444
  19.6 0.7 collective-permute-start.18
  20.3 1.3 %collective-permute-start.21 = (f32[640,256]{1,0:T(8,128)S(1)}, f32[640,256]{1,0:T(8,128)}, u32[]{:S(2)}, u32[]{:S(2)}) collective-permute-start(f32[640,256]{1,0:T(8,128)S(1)} %get-tuple-element.61.refs_0_.refs_1_.refs_5_), channel_id=1, source_target_pairs={{1,0},{5,4},{9,8},{13,12},{17,16},{21,20},{25,24},{29,28}} | collective-permute-start | bytes 1966088 | tf_op jit(solution)/shard_map/ppermute | solution.py:444
  21.6 0.0 collective-permute-done.16
  21.6 0.0 collective-permute-done.14
  21.6 1.2 %add_select_fusion.bases = f32[256,256]{1,0:T(8,128)S(1)} fusion(f32[256,256]{1,0:T(8,128)S(1)} %get-tuple-element.63, f32[256,256]{1,0:T(8,128)} %collective-permute-done.16, f32[256,256]{1,0:T(8,128)} %collective-permute-done.14, f32[256,256]{1,0:T(8,128)} %collective-permute-done.15, pred[]{:T(512)S(6)} %eq.65), kind=kLoop, calls=%fused_computation.1 | loop fusion | flops 196608 | bytes 1310721 | tf_op jit(solution)/shard_map/jit(_where)/select_n | solution.py:474
  22.8 2.0 %second_inverse.1.refs_0_ = f32[768,256]{1,0:T(8,128)} custom-call(s32[2]{0:T(128)S(1)} %pad_add_fusion.1.place, s32[32,32]{1,0:T(8,128)} %ranks.7, f32[4,256,256]{2,1,0:T(8,128)S(1)} %copy-done.1, f32[256,256]{1,0:T(8,128)S(1)} %add_select_fusion.bases, f32[256,256]{1,0:T(8,128)S(1)} %collective-permute-done.13.inverse), custom_call_target="tpu_custom_call" | custom-call | flops 1024 | bytes 1024 | tf_op jit(solution)/shard_map/second_inverse/pallas_call | solution.py:155
  24.8 0.7 collective-permute-start.17
  25.6 0.0 collective-permute-done.18.refs_2_.refs_3_.refs_7_
  25.6 0.7 collective-permute-start.19
  26.3 13.3 %collective-permute-done.21.refs_0_.refs_4_ = f32[640,256]{1,0:T(8,128)} collective-permute-done((f32[640,256]{1,0:T(8,128)S(1)}, f32[640,256]{1,0:T(8,128)}, u32[]{:S(2)}, u32[]{:S(2)}) %collective-permute-start.21) | collective-permute-done | bytes 655392 | tf_op jit(solution)/shard_map/ppermute | solution.py:444
  39.6 0.7 collective-permute-start.25
  40.3 0.0 collective-permute-done.17.refs_1_
  40.4 1.3 %collective-permute-start.22 = (f32[768,256]{1,0:T(8,128)S(1)}, f32[768,256]{1,0:T(8,128)S(1)}, u32[]{:S(2)}, u32[]{:S(2)}) collective-permute-start(f32[768,256]{1,0:T(8,128)S(1)} %pick.14.refs_0_), channel_id=1, source_target_pairs={{4,20},{5,21},{6,22},{7,23},{12,28},{13,29},{14,30},{15,31}} | collective-permute-start | bytes 2359304 | tf_op jit(solution)/shard_map/ppermute | solution.py:444
  41.7 0.0 collective-permute-done.19.refs_3_
  41.7 0.7 collective-permute-start.20
  42.4 0.0 collective-permute-done.25.refs_1_
  42.5 0.7 collective-permute-start.29
  43.2 39.6 %collective-permute-done.22.refs_1_ = f32[768,256]{1,0:T(8,128)S(1)} collective-permute-done((f32[768,256]{1,0:T(8,128)S(1)}, f32[768,256]{1,0:T(8,128)S(1)}, u32[]{:S(2)}, u32[]{:S(2)}) %collective-permute-start.22) | collective-permute-done | bytes 786464 | tf_op jit(solution)/shard_map/ppermute | solution.py:444
  82.8 0.1 pick.18.refs_8_
  82.9 0.0 copy-start.11
  82.9 1.5 %collective-permute-start.23 = (f32[768,256]{1,0:T(8,128)S(1)}, f32[768,256]{1,0:T(8,128)S(1)}, u32[]{:S(2)}, u32[]{:S(2)}) collective-permute-start(f32[768,256]{1,0:T(8,128)S(1)} %pick.18.refs_8_), channel_id=1, source_target_pairs={{4,0},{5,1},{6,2},{7,3},{12,8},{13,9},{14,10},{15,11},{20,16},{21,... | collective-permute-start | bytes 2359304 | tf_op jit(solution)/shard_map/ppermute | solution.py:444
  84.4 0.0 collective-permute-done.20.refs_1_
  84.4 0.0 copy-start.2
  84.4 0.0 copy-start.5
  84.4 0.8 collective-permute-start.27
  85.3 0.7 fusion
  86.0 1.3 %collective-permute-start.26 = (f32[640,256]{1,0:T(8,128)S(1)}, f32[640,256]{1,0:T(8,128)S(1)}, u32[]{:S(2)}, u32[]{:S(2)}) collective-permute-start(f32[640,256]{1,0:T(8,128)S(1)} %pick.19.refs_2_), channel_id=1, source_target_pairs={{0,4},{16,20},{8,12},{24,28},{5,1},{21,17},{13,9},{29,25},{2,6},{1... | collective-permute-start | bytes 1966088 | tf_op jit(solution)/shard_map/ppermute | solution.py:444
  87.3 0.0 collective-permute-done.29.refs_6_
  87.3 1.3 %collective-permute-start.30 = (f32[640,256]{1,0:T(8,128)S(1)}, f32[640,256]{1,0:T(8,128)S(1)}, u32[]{:S(2)}, u32[]{:S(2)}) collective-permute-start(f32[640,256]{1,0:T(8,128)S(1)} %collective-permute-done.29.refs_6_), channel_id=1, source_target_pairs={{0,4},{16,20},{8,12},{24,28},{5,1},{21,17},{13,9},{29,25},{2,6},{1... | collective-permute-start | bytes 1966088 | tf_op jit(solution)/shard_map/ppermute | solution.py:444
  88.6 3.4 %row_panels.3.refs_10_ = bf16[4,256,1536]{2,1,0:T(8,128)(2,1)S(1)} custom-call(s32[2]{0:T(128)S(1)} %pad_add_fusion.1.place, s32[32,32]{1,0:T(8,128)S(1)} %copy-done.11, f32[640,256]{1,0:T(8,128)S(1)} %get-tuple-element.61.refs_0_.refs_1_.refs_5_, f32[640,256]{1,0:T(8,128)S(1)} %collective-permute-done.12.refs_1_.refs_2_.refs_6_, ...), custom_call_target="tpu_custom_call" | custom-call | flops 1024 | bytes 1024 | tf_op jit(solution)/shard_map/row_panels/pallas_call | solution.py:282
  92.0 0.0 copy-start.3
  92.1 1.4 %collective-permute-start.24 = (f32[640,256]{1,0:T(8,128)S(1)}, f32[640,256]{1,0:T(8,128)S(1)}, u32[]{:S(2)}, u32[]{:S(2)}) collective-permute-start(f32[640,256]{1,0:T(8,128)S(1)} %pick.16.refs_0_), channel_id=1, source_target_pairs={{0,4},{16,20},{8,12},{24,28},{5,1},{21,17},{13,9},{29,25},{2,6},{1... | collective-permute-start | bytes 1966088 | tf_op jit(solution)/shard_map/ppermute | solution.py:444
  93.5 1.5 %collective-permute-start.28 = (f32[640,256]{1,0:T(8,128)S(1)}, f32[640,256]{1,0:T(8,128)S(1)}, u32[]{:S(2)}, u32[]{:S(2)}) collective-permute-start(f32[640,256]{1,0:T(8,128)S(1)} %collective-permute-done.27.refs_4_), channel_id=1, source_target_pairs={{0,4},{16,20},{8,12},{24,28},{5,1},{21,17},{13,9},{29,25},{2,6},{1... | collective-permute-start | bytes 1966088 | tf_op jit(solution)/shard_map/ppermute | solution.py:444
  95.0 1.2 %collective-permute-done.24.refs_1_ = f32[640,256]{1,0:T(8,128)S(1)} collective-permute-done((f32[640,256]{1,0:T(8,128)S(1)}, f32[640,256]{1,0:T(8,128)S(1)}, u32[]{:S(2)}, u32[]{:S(2)}) %collective-permute-start.24) | collective-permute-done | bytes 655392 | tf_op jit(solution)/shard_map/ppermute | solution.py:444
  96.3 1.3 %collective-permute-done.28.refs_5_ = f32[640,256]{1,0:T(8,128)S(1)} collective-permute-done((f32[640,256]{1,0:T(8,128)S(1)}, f32[640,256]{1,0:T(8,128)S(1)}, u32[]{:S(2)}, u32[]{:S(2)}) %collective-permute-start.28) | collective-permute-done | bytes 655392 | tf_op jit(solution)/shard_map/ppermute | solution.py:444
  97.6 15.3 %schur.3 = f32[4,8,256,256]{3,2,1,0:T(8,128)} custom-call(s32[2]{0:T(128)S(1)} %pad_add_fusion.1.place, s32[32,32]{1,0:T(8,128)S(1)} %copy-done.11, f32[640,256]{1,0:T(8,128)S(1)} %pick.16.refs_0_, f32[640,256]{1,0:T(8,128)S(1)} %collective-permute-done.24.refs_1_, f32[640,256]{1,0:T(8,128)S(1)} %pick.19.refs_2_, ...), custom_call_target="tpu_custom_call" | custom-call | flops 8589934592 | bytes 16777216 | tf_op jit(solution)/shard_map/schur/pallas_call | solution.py:402
  113.0 0.7 while.9
  (22 shorter events, 0.2 us)
Async XLA Ops:
  3.0 16.6 %collective-permute-start.12 = (f32[640,256]{1,0:T(8,128)S(1)}, f32[640,256]{1,0:T(8,128)S(1)}, u32[]{:S(2)}, u32[]{:S(2)}) collective-permute-start(f32[640,256]{1,0:T(8,128)S(1)} %get-tuple-element.61.refs_0_.refs_1_.refs_5_), channel_id=1, source_target_pairs={{0,1},{4,5},{8,9},{12,13},{16,17},{20,21},{24,25},{28,29},{1,2},{5... | collective-permute-start | bytes 1966088 | tf_op jit(solution)/shard_map/ppermute | solution.py:444
  6.2 1.2 %copy-start = (f32[4,256,256]{2,1,0:T(8,128)S(1)}, f32[4,256,256]{2,1,0:T(8,128)}, u32[]{:S(2)}) copy-start(f32[4,256,256]{2,1,0:T(8,128)} %tiles.3) | copy-start | bytes 3145732
  7.4 15.3 %copy-start.1 = (f32[4,256,256]{2,1,0:T(8,128)S(1)}, f32[4,256,256]{2,1,0:T(8,128)}, u32[]{:S(2)}) copy-start(f32[4,256,256]{2,1,0:T(8,128)} %tiles.3) | copy-start | bytes 3145732
  8.0 4.8 %collective-permute-start.13 = (f32[256,256]{1,0:T(8,128)S(1)}, f32[256,256]{1,0:T(8,128)S(1)}, u32[]{:S(2)}, u32[]{:S(2)}) collective-permute-start(f32[256,256]{1,0:T(8,128)S(1)} %first_inverse.1), channel_id=1, source_target_pairs={{0,4},{1,5},{2,6},{3,7}} | collective-permute-start | bytes 786440 | tf_op jit(solution)/shard_map/ppermute | solution.py:444
  8.7 12.9 %collective-permute-start.16 = (f32[256,256]{1,0:T(8,128)S(1)}, f32[256,256]{1,0:T(8,128)}, u32[]{:S(2)}, u32[]{:S(2)}) collective-permute-start(f32[256,256]{1,0:T(8,128)S(1)} %get-tuple-element.63), channel_id=1, source_target_pairs={{4,7}} | collective-permute-start | bytes 786440 | tf_op jit(solution)/shard_map/ppermute | solution.py:444
  10.1 11.5 %collective-permute-start.15 = (f32[256,256]{1,0:T(8,128)S(1)}, f32[256,256]{1,0:T(8,128)}, u32[]{:S(2)}, u32[]{:S(2)}) collective-permute-start(f32[256,256]{1,0:T(8,128)S(1)} %get-tuple-element.63), channel_id=1, source_target_pairs={{4,6}} | collective-permute-start | bytes 786440 | tf_op jit(solution)/shard_map/ppermute | solution.py:444
  11.4 10.1 %collective-permute-start.14 = (f32[256,256]{1,0:T(8,128)S(1)}, f32[256,256]{1,0:T(8,128)}, u32[]{:S(2)}, u32[]{:S(2)}) collective-permute-start(f32[256,256]{1,0:T(8,128)S(1)} %get-tuple-element.63), channel_id=1, source_target_pairs={{4,5}} | collective-permute-start | bytes 786440 | tf_op jit(solution)/shard_map/ppermute | solution.py:444
  19.6 6.0 %collective-permute-start.18 = (f32[640,256]{1,0:T(8,128)S(1)}, f32[640,256]{1,0:T(8,128)S(1)}, u32[]{:S(2)}, u32[]{:S(2)}) collective-permute-start(f32[640,256]{1,0:T(8,128)S(1)} %collective-permute-done.12.refs_1_.refs_2_.refs_6_), channel_id=1, source_target_pairs={{1,2},{5,6},{9,10},{13,14},{17,18},{21,22},{25,26},{29,30},{2,3},{... | collective-permute-start | bytes 1966088 | tf_op jit(solution)/shard_map/ppermute | solution.py:444
  20.3 19.3 %collective-permute-start.21 = (f32[640,256]{1,0:T(8,128)S(1)}, f32[640,256]{1,0:T(8,128)}, u32[]{:S(2)}, u32[]{:S(2)}) collective-permute-start(f32[640,256]{1,0:T(8,128)S(1)} %get-tuple-element.61.refs_0_.refs_1_.refs_5_), channel_id=1, source_target_pairs={{1,0},{5,4},{9,8},{13,12},{17,16},{21,20},{25,24},{29,28}} | collective-permute-start | bytes 1966088 | tf_op jit(solution)/shard_map/ppermute | solution.py:444
  24.8 15.5 %collective-permute-start.17 = (f32[768,256]{1,0:T(8,128)}, f32[768,256]{1,0:T(8,128)S(1)}, u32[]{:S(2)}, u32[]{:S(2)}) collective-permute-start(f32[768,256]{1,0:T(8,128)} %second_inverse.1.refs_0_), channel_id=1, source_target_pairs={{4,12},{5,13},{6,14},{7,15}} | collective-permute-start | bytes 2359304 | tf_op jit(solution)/shard_map/ppermute | solution.py:444
  25.6 16.1 %collective-permute-start.19 = (f32[640,256]{1,0:T(8,128)S(1)}, f32[640,256]{1,0:T(8,128)S(1)}, u32[]{:S(2)}, u32[]{:S(2)}) collective-permute-start(f32[640,256]{1,0:T(8,128)S(1)} %collective-permute-done.18.refs_2_.refs_3_.refs_7_), channel_id=1, source_target_pairs={{2,3},{6,7},{10,11},{14,15},{18,19},{22,23},{26,27},{30,31}} | collective-permute-start | bytes 1966088 | tf_op jit(solution)/shard_map/ppermute | solution.py:444
  39.6 2.8 %collective-permute-start.25 = (f32[640,256]{1,0:T(8,128)S(1)}, f32[640,256]{1,0:T(8,128)S(1)}, u32[]{:S(2)}, u32[]{:S(2)}) collective-permute-start(f32[640,256]{1,0:T(8,128)S(1)} %pick.17.refs_0_), channel_id=1, source_target_pairs={{0,8},{16,24},{5,13},{21,29},{10,2},{26,18},{15,7},{31,23}} | collective-permute-start | bytes 1966088 | tf_op jit(solution)/shard_map/ppermute | solution.py:444
  40.4 42.4 %collective-permute-start.22 = (f32[768,256]{1,0:T(8,128)S(1)}, f32[768,256]{1,0:T(8,128)S(1)}, u32[]{:S(2)}, u32[]{:S(2)}) collective-permute-start(f32[768,256]{1,0:T(8,128)S(1)} %pick.14.refs_0_), channel_id=1, source_target_pairs={{4,20},{5,21},{6,22},{7,23},{12,28},{13,29},{14,30},{15,31}} | collective-permute-start | bytes 2359304 | tf_op jit(solution)/shard_map/ppermute | solution.py:444
  41.7 42.6 %collective-permute-start.20 = (f32[640,256]{1,0:T(8,128)S(1)}, f32[640,256]{1,0:T(8,128)S(1)}, u32[]{:S(2)}, u32[]{:S(2)}) collective-permute-start(f32[640,256]{1,0:T(8,128)S(1)} %pick.15.refs_0_), channel_id=1, source_target_pairs={{0,8},{16,24},{5,13},{21,29},{10,2},{26,18},{15,7},{31,23}} | collective-permute-start | bytes 1966088 | tf_op jit(solution)/shard_map/ppermute | solution.py:444
  42.5 44.8 %collective-permute-start.29 = (f32[640,256]{1,0:T(8,128)S(1)}, f32[640,256]{1,0:T(8,128)S(1)}, u32[]{:S(2)}, u32[]{:S(2)}) collective-permute-start(f32[640,256]{1,0:T(8,128)S(1)} %pick.19.refs_2_), channel_id=1, source_target_pairs={{0,16},{16,0},{8,24},{24,8},{5,21},{21,5},{13,29},{29,13},{2,18},{... | collective-permute-start | bytes 1966088 | tf_op jit(solution)/shard_map/ppermute | solution.py:444
  82.9 14.8 %copy-start.7 = (f32[768,256]{1,0:T(8,128)}, f32[768,256]{1,0:T(8,128)S(1)}, u32[]{:S(2)}) copy-start(f32[768,256]{1,0:T(8,128)S(1)} %pick.18.refs_8_) | copy-start | bytes 2359300
  82.9 2.4 %copy-start.11 = (s32[32,32]{1,0:T(8,128)S(1)}, s32[32,32]{1,0:T(8,128)}, u32[]{:S(2)}) copy-start(s32[32,32]{1,0:T(8,128)} %ranks.7) | copy-start | bytes 12292
  82.9 5.7 %collective-permute-start.23 = (f32[768,256]{1,0:T(8,128)S(1)}, f32[768,256]{1,0:T(8,128)S(1)}, u32[]{:S(2)}, u32[]{:S(2)}) collective-permute-start(f32[768,256]{1,0:T(8,128)S(1)} %pick.18.refs_8_), channel_id=1, source_target_pairs={{4,0},{5,1},{6,2},{7,3},{12,8},{13,9},{14,10},{15,11},{20,16},{21,... | collective-permute-start | bytes 2359304 | tf_op jit(solution)/shard_map/ppermute | solution.py:444
  84.4 13.2 %copy-start.2 = (bf16[4,8,256,128]{3,2,1,0:T(8,128)(2,1)S(1)}, bf16[4,8,256,128]{3,2,1,0:T(8,128)(2,1)}, u32[]{:S(2)}) copy-start(bf16[4,8,256,128]{3,2,1,0:T(8,128)(2,1)} %refs_11_.1) | copy-start | bytes 6291460
  84.4 13.2 %copy-start.5 = (bf16[4,8,256,128]{3,2,1,0:T(8,128)(2,1)S(1)}, bf16[4,8,256,128]{3,2,1,0:T(8,128)(2,1)}, u32[]{:S(2)}) copy-start(bf16[4,8,256,128]{3,2,1,0:T(8,128)(2,1)} %refs_12_.1) | copy-start | bytes 6291460
  84.4 9.1 %collective-permute-start.27 = (f32[640,256]{1,0:T(8,128)S(1)}, f32[640,256]{1,0:T(8,128)S(1)}, u32[]{:S(2)}, u32[]{:S(2)}) collective-permute-start(f32[640,256]{1,0:T(8,128)S(1)} %pick.16.refs_0_), channel_id=1, source_target_pairs={{0,16},{16,0},{8,24},{24,8},{5,21},{21,5},{13,29},{29,13},{2,18},{... | collective-permute-start | bytes 1966088 | tf_op jit(solution)/shard_map/ppermute | solution.py:444
  86.0 9.0 %collective-permute-start.26 = (f32[640,256]{1,0:T(8,128)S(1)}, f32[640,256]{1,0:T(8,128)S(1)}, u32[]{:S(2)}, u32[]{:S(2)}) collective-permute-start(f32[640,256]{1,0:T(8,128)S(1)} %pick.19.refs_2_), channel_id=1, source_target_pairs={{0,4},{16,20},{8,12},{24,28},{5,1},{21,17},{13,9},{29,25},{2,6},{1... | collective-permute-start | bytes 1966088 | tf_op jit(solution)/shard_map/ppermute | solution.py:444
  87.3 7.7 %collective-permute-start.30 = (f32[640,256]{1,0:T(8,128)S(1)}, f32[640,256]{1,0:T(8,128)S(1)}, u32[]{:S(2)}, u32[]{:S(2)}) collective-permute-start(f32[640,256]{1,0:T(8,128)S(1)} %collective-permute-done.29.refs_6_), channel_id=1, source_target_pairs={{0,4},{16,20},{8,12},{24,28},{5,1},{21,17},{13,9},{29,25},{2,6},{1... | collective-permute-start | bytes 1966088 | tf_op jit(solution)/shard_map/ppermute | solution.py:444
  88.6 24.4 %copy-start.9 = (f32[768,256]{1,0:T(8,128)}, f32[768,256]{1,0:T(8,128)S(1)}, u32[]{:S(2)}) copy-start(f32[768,256]{1,0:T(8,128)S(1)} %collective-permute-done.23.refs_9_) | copy-start | bytes 2359300
  92.0 20.9 %copy-start.3 = (bf16[4,8,256,128]{3,2,1,0:T(8,128)(2,1)S(1)}, bf16[4,8,256,128]{3,2,1,0:T(8,128)(2,1)}, u32[]{:S(2)}) copy-start(bf16[4,8,256,128]{3,2,1,0:T(8,128)(2,1)} %refs_11_.1) | copy-start | bytes 6291460
  92.1 4.2 %collective-permute-start.24 = (f32[640,256]{1,0:T(8,128)S(1)}, f32[640,256]{1,0:T(8,128)S(1)}, u32[]{:S(2)}, u32[]{:S(2)}) collective-permute-start(f32[640,256]{1,0:T(8,128)S(1)} %pick.16.refs_0_), channel_id=1, source_target_pairs={{0,4},{16,20},{8,12},{24,28},{5,1},{21,17},{13,9},{29,25},{2,6},{1... | collective-permute-start | bytes 1966088 | tf_op jit(solution)/shard_map/ppermute | solution.py:444
  93.5 4.1 %collective-permute-start.28 = (f32[640,256]{1,0:T(8,128)S(1)}, f32[640,256]{1,0:T(8,128)S(1)}, u32[]{:S(2)}, u32[]{:S(2)}) collective-permute-start(f32[640,256]{1,0:T(8,128)S(1)} %collective-permute-done.27.refs_4_), channel_id=1, source_target_pairs={{0,4},{16,20},{8,12},{24,28},{5,1},{21,17},{13,9},{29,25},{2,6},{1... | collective-permute-start | bytes 1966088 | tf_op jit(solution)/shard_map/ppermute | solution.py:444

commit v6 on v5

--- a/solution.py
+++ b/solution.py
@@ -473,7 +473,7 @@
         received = [move(pivot_bases, [((1, 0), (1, c))]) for c in every_col if c]
         pivot_bases = jnp.where(col_here == 0, pivot_bases, sum(received))
         chain.append(chain_step(packed, 1))
-        chain[1] = after(chain[1], passed)
+        chain[1] = after(chain[1], passed, pivot_bases)
         weights = second_inverse(place, ranks, diag_tiles, after(pivot_bases, chain[1]), passed)
     else:
         chain.append(chain_step(packed, 1))

time: 115 us -> 108 us (0.939)
  the two profiles are of different devices: /device:TPU:5 before, /device:TPU:21 now
where the time goes in v6:
time: 108 us
  waiting for transfers between devices  55.3 us (51%)
  starting transfers between devices  24.3 us (22%)
  Pallas kernels  23.6 us (22%)
  other arithmetic  1.96 us (2%)
  local copies, waits for them, and re-layouts  1.25 us (1%)
    ppermute x19, waiting for transfers between devices, move(): return lax.ppermute(array, AXES, flat)  55.3 us
    ppermute x19, starting transfers between devices, move(): return lax.ppermute(array, AXES, flat)  24.3 us
    pallas_call x1, Pallas kernels, schur(): pl.pallas_call(functools.partial(schur_kernel, capacity, grid_rows, grid_...  15.4 us
    pallas_call x1, Pallas kernels, pack(): pl.pallas_call(functools.partial(pack_kernel, capacity, grid_rows), out_s...  2.88 us
    pallas_call x1, Pallas kernels, row_panels(): pl.pallas_call(functools.partial(rows_kernel, capacity, grid_rows, count)...  2.7 us
  transfers between devices with their start and end apart: 19, of which 8 were waited for; matrix products, arithmetic and copies ran while one was open for 2% of the time, Pallas kernels for 5%

profile of v6, /device:TPU:21, one launch (start us, length us, event | category | flops | bytes accessed | tf_op | source)
XLA Modules:
  0.0 107.7 jit_solution(17399551124257650903)
XLA Ops:
  0.0 0.1 pad_add_fusion.1.place
  0.1 2.9 %pack.3 = (f32[640,256]{1,0:T(8,128)S(1)}, f32[256,256]{1,0:T(8,128)S(1)}) custom-call(s32[2]{0:T(128)S(1)} %pad_add_fusion.1.place, s32[32,32]{1,0:T(8,128)} %ranks.7, bf16[4,8,256,128]{3,2,1,0:T(8,128)(2,1)} %refs_11_.1, bf16[4,8,256,128]{3,2,1,0:T(8,128)(2,1)} %refs_12_.1), custom_call_target="tpu_custom_call" | custom-call | flops 1024 | bytes 1024 | tf_op jit(solution)/shard_map/pack/pallas_call | solution.py:205
  3.0 1.4 %collective-permute-start.16 = (f32[256,256]{1,0:T(8,128)S(1)}, f32[256,256]{1,0:T(8,128)}, u32[]{:S(2)}, u32[]{:S(2)}) collective-permute-start(f32[256,256]{1,0:T(8,128)S(1)} %get-tuple-element.62), channel_id=1, source_target_pairs={{4,7}} | collective-permute-start | bytes 786440 | tf_op jit(solution)/shard_map/ppermute | solution.py:444
  4.3 1.4 %collective-permute-start.15 = (f32[256,256]{1,0:T(8,128)S(1)}, f32[256,256]{1,0:T(8,128)}, u32[]{:S(2)}, u32[]{:S(2)}) collective-permute-start(f32[256,256]{1,0:T(8,128)S(1)} %get-tuple-element.62), channel_id=1, source_target_pairs={{4,6}} | collective-permute-start | bytes 786440 | tf_op jit(solution)/shard_map/ppermute | solution.py:444
  5.7 1.4 %collective-permute-start.14 = (f32[256,256]{1,0:T(8,128)S(1)}, f32[256,256]{1,0:T(8,128)}, u32[]{:S(2)}, u32[]{:S(2)}) collective-permute-start(f32[256,256]{1,0:T(8,128)S(1)} %get-tuple-element.62), channel_id=1, source_target_pairs={{4,5}} | collective-permute-start | bytes 786440 | tf_op jit(solution)/shard_map/ppermute | solution.py:444
  7.1 1.3 %collective-permute-start.12 = (f32[640,256]{1,0:T(8,128)S(1)}, f32[640,256]{1,0:T(8,128)S(1)}, u32[]{:S(2)}, u32[]{:S(2)}) collective-permute-start(f32[640,256]{1,0:T(8,128)S(1)} %get-tuple-element.61.refs_0_.refs_1_.refs_5_), channel_id=1, source_target_pairs={{0,1},{4,5},{8,9},{12,13},{16,17},{20,21},{24,25},{28,29},{1,2},{5... | collective-permute-start | bytes 1966088 | tf_op jit(solution)/shard_map/ppermute | solution.py:444
  8.3 0.0 copy-start
  8.4 1.2 %copy-done = f32[4,256,256]{2,1,0:T(8,128)S(1)} copy-done((f32[4,256,256]{2,1,0:T(8,128)S(1)}, f32[4,256,256]{2,1,0:T(8,128)}, u32[]{:S(2)}) %copy-start) | copy-done | bytes 1048600
  9.6 0.6 first_inverse.1
  10.1 0.7 collective-permute-start.13
  10.8 0.0 collective-permute-done.15
  10.9 1.2 %add_select_fusion.bases = f32[256,256]{1,0:T(8,128)S(1)} fusion(f32[256,256]{1,0:T(8,128)S(1)} %get-tuple-element.62, f32[256,256]{1,0:T(8,128)} %collective-permute-done.16, f32[256,256]{1,0:T(8,128)} %collective-permute-done.14, f32[256,256]{1,0:T(8,128)} %collective-permute-done.15, pred[]{:T(512)S(6)} %eq.62), kind=kLoop, calls=%fused_computation.1 | loop fusion | flops 196608 | bytes 1310721 | tf_op jit(solution)/shard_map/jit(_where)/select_n | solution.py:474
  12.0 0.0 collective-permute-done.13.inverse
  12.1 12.5 %collective-permute-done.12.refs_1_.refs_2_.refs_6_ = f32[640,256]{1,0:T(8,128)S(1)} collective-permute-done((f32[640,256]{1,0:T(8,128)S(1)}, f32[640,256]{1,0:T(8,128)S(1)}, u32[]{:S(2)}, u32[]{:S(2)}) %collective-permute-start.12) | collective-permute-done | bytes 655392 | tf_op jit(solution)/shard_map/ppermute | solution.py:444
  24.5 1.9 %collective-permute-start.18 = (f32[640,256]{1,0:T(8,128)S(1)}, f32[640,256]{1,0:T(8,128)S(1)}, u32[]{:S(2)}, u32[]{:S(2)}) collective-permute-start(f32[640,256]{1,0:T(8,128)S(1)} %collective-permute-done.12.refs_1_.refs_2_.refs_6_), channel_id=1, source_target_pairs={{1,2},{5,6},{9,10},{13,14},{17,18},{21,22},{25,26},{29,30},{2,3},{... | collective-permute-start | bytes 1966088 | tf_op jit(solution)/shard_map/ppermute | solution.py:444
  26.5 1.5 %collective-permute-start.21 = (f32[640,256]{1,0:T(8,128)S(1)}, f32[640,256]{1,0:T(8,128)}, u32[]{:S(2)}, u32[]{:S(2)}) collective-permute-start(f32[640,256]{1,0:T(8,128)S(1)} %get-tuple-element.61.refs_0_.refs_1_.refs_5_), channel_id=1, source_target_pairs={{1,0},{5,4},{9,8},{13,12},{17,16},{21,20},{25,24},{29,28}} | collective-permute-start | bytes 1966088 | tf_op jit(solution)/shard_map/ppermute | solution.py:444
  28.0 1.9 %second_inverse.1.refs_0_ = f32[768,256]{1,0:T(8,128)} custom-call(s32[2]{0:T(128)S(1)} %pad_add_fusion.1.place, s32[32,32]{1,0:T(8,128)S(1)} %copy-done.11, f32[4,256,256]{2,1,0:T(8,128)S(1)} %copy-done.1, f32[256,256]{1,0:T(8,128)S(1)} %add_select_fusion.bases, f32[256,256]{1,0:T(8,128)S(1)} %collective-permute-done.13.inverse), custom_call_target="tpu_custom_call" | custom-call | flops 1024 | bytes 1024 | tf_op jit(solution)/shard_map/second_inverse/pallas_call | solution.py:155
  29.9 0.7 collective-permute-start.17
  30.6 10.5 %collective-permute-done.18.refs_2_.refs_3_.refs_7_ = f32[640,256]{1,0:T(8,128)S(1)} collective-permute-done((f32[640,256]{1,0:T(8,128)S(1)}, f32[640,256]{1,0:T(8,128)S(1)}, u32[]{:S(2)}, u32[]{:S(2)}) %collective-permute-start.18) | collective-permute-done | bytes 655392 | tf_op jit(solution)/shard_map/ppermute | solution.py:444
  41.1 2.2 %collective-permute-start.19 = (f32[640,256]{1,0:T(8,128)S(1)}, f32[640,256]{1,0:T(8,128)S(1)}, u32[]{:S(2)}, u32[]{:S(2)}) collective-permute-start(f32[640,256]{1,0:T(8,128)S(1)} %collective-permute-done.18.refs_2_.refs_3_.refs_7_), channel_id=1, source_target_pairs={{2,3},{6,7},{10,11},{14,15},{18,19},{22,23},{26,27},{30,31}} | collective-permute-start | bytes 1966088 | tf_op jit(solution)/shard_map/ppermute | solution.py:444
  43.3 0.0 collective-permute-done.21.refs_0_.refs_4_
  43.4 0.7 collective-permute-start.25
  44.1 0.0 collective-permute-done.17.refs_1_
  44.1 1.3 %collective-permute-start.22 = (f32[768,256]{1,0:T(8,128)S(1)}, f32[768,256]{1,0:T(8,128)S(1)}, u32[]{:S(2)}, u32[]{:S(2)}) collective-permute-start(f32[768,256]{1,0:T(8,128)S(1)} %pick.14.refs_0_), channel_id=1, source_target_pairs={{4,20},{5,21},{6,22},{7,23},{12,28},{13,29},{14,30},{15,31}} | collective-permute-start | bytes 2359304 | tf_op jit(solution)/shard_map/ppermute | solution.py:444
  45.4 9.7 %collective-permute-done.19.refs_3_ = f32[640,256]{1,0:T(8,128)S(1)} collective-permute-done((f32[640,256]{1,0:T(8,128)S(1)}, f32[640,256]{1,0:T(8,128)S(1)}, u32[]{:S(2)}, u32[]{:S(2)}) %collective-permute-start.19) | collective-permute-done | bytes 655392 | tf_op jit(solution)/shard_map/ppermute | solution.py:444
  55.1 0.7 collective-permute-start.20
  55.9 0.7 collective-permute-start.29
  56.6 11.8 %collective-permute-done.22.refs_1_ = f32[768,256]{1,0:T(8,128)S(1)} collective-permute-done((f32[768,256]{1,0:T(8,128)S(1)}, f32[768,256]{1,0:T(8,128)S(1)}, u32[]{:S(2)}, u32[]{:S(2)}) %collective-permute-start.22) | collective-permute-done | bytes 786464 | tf_op jit(solution)/shard_map/ppermute | solution.py:444
  68.4 0.1 pick.18.refs_8_
  68.5 2.1 %collective-permute-start.23 = (f32[768,256]{1,0:T(8,128)S(1)}, f32[768,256]{1,0:T(8,128)S(1)}, u32[]{:S(2)}, u32[]{:S(2)}) collective-permute-start(f32[768,256]{1,0:T(8,128)S(1)} %pick.18.refs_8_), channel_id=1, source_target_pairs={{4,0},{5,1},{6,2},{7,3},{12,8},{13,9},{14,10},{15,11},{20,16},{21,... | collective-permute-start | bytes 2359304 | tf_op jit(solution)/shard_map/ppermute | solution.py:444
  70.6 0.0 collective-permute-done.20.refs_1_
  70.6 0.0 copy-start.2
  70.6 0.0 copy-start.5
  70.6 0.8 collective-permute-start.27
  71.5 0.7 fusion
  72.2 1.3 %collective-permute-start.26 = (f32[640,256]{1,0:T(8,128)S(1)}, f32[640,256]{1,0:T(8,128)S(1)}, u32[]{:S(2)}, u32[]{:S(2)}) collective-permute-start(f32[640,256]{1,0:T(8,128)S(1)} %pick.19.refs_2_), channel_id=1, source_target_pairs={{0,4},{16,20},{8,12},{24,28},{5,1},{21,17},{13,9},{29,25},{2,6},{1... | collective-permute-start | bytes 1966088 | tf_op jit(solution)/shard_map/ppermute | solution.py:444
  73.5 0.0 collective-permute-done.29.refs_6_
  73.5 1.3 %collective-permute-start.30 = (f32[640,256]{1,0:T(8,128)S(1)}, f32[640,256]{1,0:T(8,128)S(1)}, u32[]{:S(2)}, u32[]{:S(2)}) collective-permute-start(f32[640,256]{1,0:T(8,128)S(1)} %collective-permute-done.29.refs_6_), channel_id=1, source_target_pairs={{0,4},{16,20},{8,12},{24,28},{5,1},{21,17},{13,9},{29,25},{2,6},{1... | collective-permute-start | bytes 1966088 | tf_op jit(solution)/shard_map/ppermute | solution.py:444
  74.8 2.7 %row_panels.3.refs_10_ = bf16[4,256,1536]{2,1,0:T(8,128)(2,1)S(1)} custom-call(s32[2]{0:T(128)S(1)} %pad_add_fusion.1.place, s32[32,32]{1,0:T(8,128)S(1)} %copy-done.11, f32[640,256]{1,0:T(8,128)S(1)} %get-tuple-element.61.refs_0_.refs_1_.refs_5_, f32[640,256]{1,0:T(8,128)S(1)} %collective-permute-done.12.refs_1_.refs_2_.refs_6_, ...), custom_call_target="tpu_custom_call" | custom-call | flops 1024 | bytes 1024 | tf_op jit(solution)/shard_map/row_panels/pallas_call | solution.py:282
  77.5 0.0 copy-start.3
  77.5 1.4 %collective-permute-start.24 = (f32[640,256]{1,0:T(8,128)S(1)}, f32[640,256]{1,0:T(8,128)S(1)}, u32[]{:S(2)}, u32[]{:S(2)}) collective-permute-start(f32[640,256]{1,0:T(8,128)S(1)} %pick.16.refs_0_), channel_id=1, source_target_pairs={{0,4},{16,20},{8,12},{24,28},{5,1},{21,17},{13,9},{29,25},{2,6},{1... | collective-permute-start | bytes 1966088 | tf_op jit(solution)/shard_map/ppermute | solution.py:444
  79.0 1.5 %collective-permute-start.28 = (f32[640,256]{1,0:T(8,128)S(1)}, f32[640,256]{1,0:T(8,128)S(1)}, u32[]{:S(2)}, u32[]{:S(2)}) collective-permute-start(f32[640,256]{1,0:T(8,128)S(1)} %collective-permute-done.27.refs_4_), channel_id=1, source_target_pairs={{0,4},{16,20},{8,12},{24,28},{5,1},{21,17},{13,9},{29,25},{2,6},{1... | collective-permute-start | bytes 1966088 | tf_op jit(solution)/shard_map/ppermute | solution.py:444
  80.5 3.1 %collective-permute-done.26.refs_3_ = f32[640,256]{1,0:T(8,128)S(1)} collective-permute-done((f32[640,256]{1,0:T(8,128)S(1)}, f32[640,256]{1,0:T(8,128)S(1)}, u32[]{:S(2)}, u32[]{:S(2)}) %collective-permute-start.26) | collective-permute-done | bytes 655392 | tf_op jit(solution)/shard_map/ppermute | solution.py:444
  83.6 1.3 %collective-permute-done.30.refs_7_ = f32[640,256]{1,0:T(8,128)S(1)} collective-permute-done((f32[640,256]{1,0:T(8,128)S(1)}, f32[640,256]{1,0:T(8,128)S(1)}, u32[]{:S(2)}, u32[]{:S(2)}) %collective-permute-start.30) | collective-permute-done | bytes 655392 | tf_op jit(solution)/shard_map/ppermute | solution.py:444
  84.9 4.2 %collective-permute-done.24.refs_1_ = f32[640,256]{1,0:T(8,128)S(1)} collective-permute-done((f32[640,256]{1,0:T(8,128)S(1)}, f32[640,256]{1,0:T(8,128)S(1)}, u32[]{:S(2)}, u32[]{:S(2)}) %collective-permute-start.24) | collective-permute-done | bytes 655392 | tf_op jit(solution)/shard_map/ppermute | solution.py:444
  89.1 2.3 %collective-permute-done.28.refs_5_ = f32[640,256]{1,0:T(8,128)S(1)} collective-permute-done((f32[640,256]{1,0:T(8,128)S(1)}, f32[640,256]{1,0:T(8,128)S(1)}, u32[]{:S(2)}, u32[]{:S(2)}) %collective-permute-start.28) | collective-permute-done | bytes 655392 | tf_op jit(solution)/shard_map/ppermute | solution.py:444
  91.4 15.4 %schur.3 = f32[4,8,256,256]{3,2,1,0:T(8,128)} custom-call(s32[2]{0:T(128)S(1)} %pad_add_fusion.1.place, s32[32,32]{1,0:T(8,128)S(1)} %copy-done.11, f32[640,256]{1,0:T(8,128)S(1)} %pick.16.refs_0_, f32[640,256]{1,0:T(8,128)S(1)} %collective-permute-done.24.refs_1_, f32[640,256]{1,0:T(8,128)S(1)} %pick.19.refs_2_, ...), custom_call_target="tpu_custom_call" | custom-call | flops 8589934592 | bytes 16777216 | tf_op jit(solution)/shard_map/schur/pallas_call | solution.py:402
  106.9 0.7 while.9
  (22 shorter events, 0.2 us)
Async XLA Ops:
  3.0 7.9 %collective-permute-start.16 = (f32[256,256]{1,0:T(8,128)S(1)}, f32[256,256]{1,0:T(8,128)}, u32[]{:S(2)}, u32[]{:S(2)}) collective-permute-start(f32[256,256]{1,0:T(8,128)S(1)} %get-tuple-element.62), channel_id=1, source_target_pairs={{4,7}} | collective-permute-start | bytes 786440 | tf_op jit(solution)/shard_map/ppermute | solution.py:444
  4.3 6.5 %collective-permute-start.15 = (f32[256,256]{1,0:T(8,128)S(1)}, f32[256,256]{1,0:T(8,128)}, u32[]{:S(2)}, u32[]{:S(2)}) collective-permute-start(f32[256,256]{1,0:T(8,128)S(1)} %get-tuple-element.62), channel_id=1, source_target_pairs={{4,6}} | collective-permute-start | bytes 786440 | tf_op jit(solution)/shard_map/ppermute | solution.py:444
  5.7 5.2 %collective-permute-start.14 = (f32[256,256]{1,0:T(8,128)S(1)}, f32[256,256]{1,0:T(8,128)}, u32[]{:S(2)}, u32[]{:S(2)}) collective-permute-start(f32[256,256]{1,0:T(8,128)S(1)} %get-tuple-element.62), channel_id=1, source_target_pairs={{4,5}} | collective-permute-start | bytes 786440 | tf_op jit(solution)/shard_map/ppermute | solution.py:444
  7.1 17.5 %collective-permute-start.12 = (f32[640,256]{1,0:T(8,128)S(1)}, f32[640,256]{1,0:T(8,128)S(1)}, u32[]{:S(2)}, u32[]{:S(2)}) collective-permute-start(f32[640,256]{1,0:T(8,128)S(1)} %get-tuple-element.61.refs_0_.refs_1_.refs_5_), channel_id=1, source_target_pairs={{0,1},{4,5},{8,9},{12,13},{16,17},{20,21},{24,25},{28,29},{1,2},{5... | collective-permute-start | bytes 1966088 | tf_op jit(solution)/shard_map/ppermute | solution.py:444
  8.3 1.2 %copy-start = (f32[4,256,256]{2,1,0:T(8,128)S(1)}, f32[4,256,256]{2,1,0:T(8,128)}, u32[]{:S(2)}) copy-start(f32[4,256,256]{2,1,0:T(8,128)} %tiles.3) | copy-start | bytes 3145732
  9.6 18.4 %copy-start.1 = (f32[4,256,256]{2,1,0:T(8,128)S(1)}, f32[4,256,256]{2,1,0:T(8,128)}, u32[]{:S(2)}) copy-start(f32[4,256,256]{2,1,0:T(8,128)} %tiles.3) | copy-start | bytes 3145732
  9.6 18.4 %copy-start.11 = (s32[32,32]{1,0:T(8,128)S(1)}, s32[32,32]{1,0:T(8,128)}, u32[]{:S(2)}) copy-start(s32[32,32]{1,0:T(8,128)} %ranks.7) | copy-start | bytes 12292
  10.1 1.9 %collective-permute-start.13 = (f32[256,256]{1,0:T(8,128)S(1)}, f32[256,256]{1,0:T(8,128)S(1)}, u32[]{:S(2)}, u32[]{:S(2)}) collective-permute-start(f32[256,256]{1,0:T(8,128)S(1)} %first_inverse.1), channel_id=1, source_target_pairs={{0,4},{1,5},{2,6},{3,7}} | collective-permute-start | bytes 786440 | tf_op jit(solution)/shard_map/ppermute | solution.py:444
  24.5 16.6 %collective-permute-start.18 = (f32[640,256]{1,0:T(8,128)S(1)}, f32[640,256]{1,0:T(8,128)S(1)}, u32[]{:S(2)}, u32[]{:S(2)}) collective-permute-start(f32[640,256]{1,0:T(8,128)S(1)} %collective-permute-done.12.refs_1_.refs_2_.refs_6_), channel_id=1, source_target_pairs={{1,2},{5,6},{9,10},{13,14},{17,18},{21,22},{25,26},{29,30},{2,3},{... | collective-permute-start | bytes 1966088 | tf_op jit(solution)/shard_map/ppermute | solution.py:444
  26.5 16.9 %collective-permute-start.21 = (f32[640,256]{1,0:T(8,128)S(1)}, f32[640,256]{1,0:T(8,128)}, u32[]{:S(2)}, u32[]{:S(2)}) collective-permute-start(f32[640,256]{1,0:T(8,128)S(1)} %get-tuple-element.61.refs_0_.refs_1_.refs_5_), channel_id=1, source_target_pairs={{1,0},{5,4},{9,8},{13,12},{17,16},{21,20},{25,24},{29,28}} | collective-permute-start | bytes 1966088 | tf_op jit(solution)/shard_map/ppermute | solution.py:444
  29.9 14.2 %collective-permute-start.17 = (f32[768,256]{1,0:T(8,128)}, f32[768,256]{1,0:T(8,128)S(1)}, u32[]{:S(2)}, u32[]{:S(2)}) collective-permute-start(f32[768,256]{1,0:T(8,128)} %second_inverse.1.refs_0_), channel_id=1, source_target_pairs={{4,12},{5,13},{6,14},{7,15}} | collective-permute-start | bytes 2359304 | tf_op jit(solution)/shard_map/ppermute | solution.py:444
  41.1 14.0 %collective-permute-start.19 = (f32[640,256]{1,0:T(8,128)S(1)}, f32[640,256]{1,0:T(8,128)S(1)}, u32[]{:S(2)}, u32[]{:S(2)}) collective-permute-start(f32[640,256]{1,0:T(8,128)S(1)} %collective-permute-done.18.refs_2_.refs_3_.refs_7_), channel_id=1, source_target_pairs={{2,3},{6,7},{10,11},{14,15},{18,19},{22,23},{26,27},{30,31}} | collective-permute-start | bytes 1966088 | tf_op jit(solution)/shard_map/ppermute | solution.py:444
  43.4 12.5 %collective-permute-start.25 = (f32[640,256]{1,0:T(8,128)S(1)}, f32[640,256]{1,0:T(8,128)S(1)}, u32[]{:S(2)}, u32[]{:S(2)}) collective-permute-start(f32[640,256]{1,0:T(8,128)S(1)} %pick.17.refs_0_), channel_id=1, source_target_pairs={{0,8},{16,24},{5,13},{21,29},{10,2},{26,18},{15,7},{31,23}} | collective-permute-start | bytes 1966088 | tf_op jit(solution)/shard_map/ppermute | solution.py:444
  44.1 24.2 %collective-permute-start.22 = (f32[768,256]{1,0:T(8,128)S(1)}, f32[768,256]{1,0:T(8,128)S(1)}, u32[]{:S(2)}, u32[]{:S(2)}) collective-permute-start(f32[768,256]{1,0:T(8,128)S(1)} %pick.14.refs_0_), channel_id=1, source_target_pairs={{4,20},{5,21},{6,22},{7,23},{12,28},{13,29},{14,30},{15,31}} | collective-permute-start | bytes 2359304 | tf_op jit(solution)/shard_map/ppermute | solution.py:444
  55.1 15.4 %collective-permute-start.20 = (f32[640,256]{1,0:T(8,128)S(1)}, f32[640,256]{1,0:T(8,128)S(1)}, u32[]{:S(2)}, u32[]{:S(2)}) collective-permute-start(f32[640,256]{1,0:T(8,128)S(1)} %pick.15.refs_0_), channel_id=1, source_target_pairs={{0,8},{16,24},{5,13},{21,29},{10,2},{26,18},{15,7},{31,23}} | collective-permute-start | bytes 1966088 | tf_op jit(solution)/shard_map/ppermute | solution.py:444
  55.9 17.6 %collective-permute-start.29 = (f32[640,256]{1,0:T(8,128)S(1)}, f32[640,256]{1,0:T(8,128)S(1)}, u32[]{:S(2)}, u32[]{:S(2)}) collective-permute-start(f32[640,256]{1,0:T(8,128)S(1)} %pick.19.refs_2_), channel_id=1, source_target_pairs={{0,16},{16,0},{8,24},{24,8},{5,21},{21,5},{13,29},{29,13},{2,18},{... | collective-permute-start | bytes 1966088 | tf_op jit(solution)/shard_map/ppermute | solution.py:444
  68.4 23.0 %copy-start.7 = (f32[768,256]{1,0:T(8,128)}, f32[768,256]{1,0:T(8,128)S(1)}, u32[]{:S(2)}) copy-start(f32[768,256]{1,0:T(8,128)S(1)} %pick.18.refs_8_) | copy-start | bytes 2359300
  68.5 6.3 %collective-permute-start.23 = (f32[768,256]{1,0:T(8,128)S(1)}, f32[768,256]{1,0:T(8,128)S(1)}, u32[]{:S(2)}, u32[]{:S(2)}) collective-permute-start(f32[768,256]{1,0:T(8,128)S(1)} %pick.18.refs_8_), channel_id=1, source_target_pairs={{4,0},{5,1},{6,2},{7,3},{12,8},{13,9},{14,10},{15,11},{20,16},{21,... | collective-permute-start | bytes 2359304 | tf_op jit(solution)/shard_map/ppermute | solution.py:444
  70.6 20.8 %copy-start.2 = (bf16[4,8,256,128]{3,2,1,0:T(8,128)(2,1)S(1)}, bf16[4,8,256,128]{3,2,1,0:T(8,128)(2,1)}, u32[]{:S(2)}) copy-start(bf16[4,8,256,128]{3,2,1,0:T(8,128)(2,1)} %refs_11_.1) | copy-start | bytes 6291460
  70.6 20.8 %copy-start.5 = (bf16[4,8,256,128]{3,2,1,0:T(8,128)(2,1)S(1)}, bf16[4,8,256,128]{3,2,1,0:T(8,128)(2,1)}, u32[]{:S(2)}) copy-start(bf16[4,8,256,128]{3,2,1,0:T(8,128)(2,1)} %refs_12_.1) | copy-start | bytes 6291460
  70.6 8.3 %collective-permute-start.27 = (f32[640,256]{1,0:T(8,128)S(1)}, f32[640,256]{1,0:T(8,128)S(1)}, u32[]{:S(2)}, u32[]{:S(2)}) collective-permute-start(f32[640,256]{1,0:T(8,128)S(1)} %pick.16.refs_0_), channel_id=1, source_target_pairs={{0,16},{16,0},{8,24},{24,8},{5,21},{21,5},{13,29},{29,13},{2,18},{... | collective-permute-start | bytes 1966088 | tf_op jit(solution)/shard_map/ppermute | solution.py:444
  72.2 11.4 %collective-permute-start.26 = (f32[640,256]{1,0:T(8,128)S(1)}, f32[640,256]{1,0:T(8,128)S(1)}, u32[]{:S(2)}, u32[]{:S(2)}) collective-permute-start(f32[640,256]{1,0:T(8,128)S(1)} %pick.19.refs_2_), channel_id=1, source_target_pairs={{0,4},{16,20},{8,12},{24,28},{5,1},{21,17},{13,9},{29,25},{2,6},{1... | collective-permute-start | bytes 1966088 | tf_op jit(solution)/shard_map/ppermute | solution.py:444
  73.5 11.4 %collective-permute-start.30 = (f32[640,256]{1,0:T(8,128)S(1)}, f32[640,256]{1,0:T(8,128)S(1)}, u32[]{:S(2)}, u32[]{:S(2)}) collective-permute-start(f32[640,256]{1,0:T(8,128)S(1)} %collective-permute-done.29.refs_6_), channel_id=1, source_target_pairs={{0,4},{16,20},{8,12},{24,28},{5,1},{21,17},{13,9},{29,25},{2,6},{1... | collective-permute-start | bytes 1966088 | tf_op jit(solution)/shard_map/ppermute | solution.py:444
  74.8 32.0 %copy-start.9 = (f32[768,256]{1,0:T(8,128)}, f32[768,256]{1,0:T(8,128)S(1)}, u32[]{:S(2)}) copy-start(f32[768,256]{1,0:T(8,128)S(1)} %collective-permute-done.23.refs_9_) | copy-start | bytes 2359300
  77.5 29.3 %copy-start.3 = (bf16[4,8,256,128]{3,2,1,0:T(8,128)(2,1)S(1)}, bf16[4,8,256,128]{3,2,1,0:T(8,128)(2,1)}, u32[]{:S(2)}) copy-start(bf16[4,8,256,128]{3,2,1,0:T(8,128)(2,1)} %refs_11_.1) | copy-start | bytes 6291460
  77.5 11.6 %collective-permute-start.24 = (f32[640,256]{1,0:T(8,128)S(1)}, f32[640,256]{1,0:T(8,128)S(1)}, u32[]{:S(2)}, u32[]{:S(2)}) collective-permute-start(f32[640,256]{1,0:T(8,128)S(1)} %pick.16.refs_0_), channel_id=1, source_target_pairs={{0,4},{16,20},{8,12},{24,28},{5,1},{21,17},{13,9},{29,25},{2,6},{1... | collective-permute-start | bytes 1966088 | tf_op jit(solution)/shard_map/ppermute | solution.py:444
  79.0 12.4 %collective-permute-start.28 = (f32[640,256]{1,0:T(8,128)S(1)}, f32[640,256]{1,0:T(8,128)S(1)}, u32[]{:S(2)}, u32[]{:S(2)}) collective-permute-start(f32[640,256]{1,0:T(8,128)S(1)} %collective-permute-done.27.refs_4_), channel_id=1, source_target_pairs={{0,4},{16,20},{8,12},{24,28},{5,1},{21,17},{13,9},{29,25},{2,6},{1... | collective-permute-start | bytes 1966088 | tf_op jit(solution)/shard_map/ppermute | solution.py:444
